TPU v7x, 256 devices: a whole 4x4x8 slice. The times are simulated.
256 devices in a mesh: dp: 4 (over y), group: 16 (over z, core), tensor: 4 (over x).
Axes of the slice: x: 4, y: 4, z: 8, core: 2. Of those that a mesh axis runs over, the one named last changes fastest.
Arguments:
- queries: bfloat16 [4, 16, 512, 2560], P('dp', 'group', None, 'tensor'), may hold values from -60 to 60
- comp_kv: bfloat16 [4, 16, 512, 2, 512], P('dp', 'group', None, None, 'tensor'), may hold values from -6 to 6
- prompt_kv: bfloat16 [4, 4096, 2, 512], P('dp', 'group', None, 'tensor'), may hold values from -6 to 6
- residual: bfloat16 [4, 16, 512, 5120], P('dp', 'group', 'tensor'), may hold values from -1.796875 to 1.796875
- out_weight: bfloat16 [2560, 5120], P('tensor', ('dp', 'group')), may hold values from -0.125 to 0.125
- gain: float32 [5120], replicated, may hold values from 0.1 to 1.9
- lengths: int32 [4, 16], P('dp', 'group'), may hold values from 128 to 512, as said below
Outputs:
- attended: bfloat16 [4, 16, 512, 5120], P('dp', 'group', 'tensor')
- normed: bfloat16 [4, 16, 512, 5120], P('dp', 'group', 'tensor')
Inputs may be any that keep to these rules, and one draw needn't show every extreme that they name: `lengths`: each completion has between a quarter of 512 and 512 live tokens, and some completion has 512.
All inputs are finite; a program needn't handle non-finite values.
Results may differ from a plain program's by a relative error of at most 0.015.
Values may be sent and summed in bfloat16 or wider, within the bound.
No kernel may reach another device: no remote copies, remote signals or barrier semaphores. Data moves between devices by JAX's collectives and lax.ppermute only.
A program may use at most 128 MiB of HBM per device.

v0:
```python
import jax
import jax.numpy as jnp
from jax import lax
from jax.sharding import PartitionSpec as P

QH = 20
KVH = 4
HD = 128


def block_stats(query_part, keys_part, values_part, visible):
    scores = jnp.einsum(
        "cgjh,lgh->gjcl", query_part, keys_part, preferred_element_type=jnp.float32
    ) * HD ** (-0.5)
    scores = jnp.where(visible, scores, jnp.float32(-1e30))
    top = jnp.max(scores, axis=-1, keepdims=True)
    weights = jnp.exp(scores - top)
    total = jnp.sum(weights, axis=-1, keepdims=True)
    mixed = jnp.einsum(
        "gjcl,lgh->gjch",
        weights.astype(jnp.bfloat16),
        values_part,
        preferred_element_type=jnp.float32,
    )
    return (top, total, mixed)


def shards(queries, comp_kv, prompt_kv, residual, out_weight, gain, lengths):
    clen = queries.shape[2]
    kv_local = comp_kv.shape[4] // HD
    groups = QH // KVH
    query_heads = queries[0, 0].reshape(clen, kv_local, groups, HD)
    own_keys = comp_kv[0, 0, :, 0].reshape(clen, kv_local, HD)
    own_values = comp_kv[0, 0, :, 1].reshape(clen, kv_local, HD)
    rows_here = jnp.arange(clen)
    whole_prompt = lax.all_gather(prompt_kv, "group", axis=1, tiled=True)
    plen = whole_prompt.shape[1]
    keys_all = jnp.concatenate(
        [whole_prompt[0, :, 0].reshape(plen, kv_local, HD), own_keys], axis=0
    )
    values_all = jnp.concatenate(
        [whole_prompt[0, :, 1].reshape(plen, kv_local, HD), own_values], axis=0
    )
    positions = jnp.arange(plen + clen)
    visible = (positions[None, :] < plen) | (positions[None, :] - plen <= rows_here[:, None])

    def one_head(head_queries):
        return block_stats(head_queries, keys_all, values_all, visible)

    per_head = lax.map(one_head, jnp.moveaxis(query_heads, 2, 0)[:, :, :, None, :])
    top, total, mixed = jax.tree.map(lambda stacked: jnp.swapaxes(stacked[:, :, 0], 0, 1), per_head)
    context = (
        (mixed / total)
        .transpose(2, 0, 1, 3)
        .reshape(clen, kv_local * groups * HD)
        .astype(jnp.bfloat16)
    )
    live = rows_here[:, None] < lengths[0, 0]
    context = jnp.where(live, context, jnp.zeros_like(context))
    terms = jnp.dot(
        context,
        lax.all_gather(out_weight, ("dp", "group"), axis=1, tiled=True),
        preferred_element_type=jnp.float32,
    )
    rows_dev = residual.shape[2]
    summed = lax.psum(terms.astype(jnp.bfloat16), "tensor").astype(jnp.float32)
    mine = lax.dynamic_slice_in_dim(summed, lax.axis_index("tensor") * rows_dev, rows_dev, 0)
    attended = mine.astype(jnp.bfloat16)
    stream = residual[0, 0].astype(jnp.float32) + attended.astype(jnp.float32)
    normed = stream * lax.rsqrt(jnp.mean(stream * stream, axis=-1, keepdims=True) + 1e-06) * gain
    return (attended[None, None], normed.astype(jnp.bfloat16)[None, None])


def solution(mesh):
    in_specs = (
        P("dp", "group", None, "tensor"),
        P("dp", "group", None, None, "tensor"),
        P("dp", "group", None, "tensor"),
        P("dp", "group", "tensor", None),
        P("tensor", ("dp", "group")),
        P(),
        P("dp", "group"),
    )
    out_specs = (P("dp", "group", "tensor", None), P("dp", "group", "tensor", None))
    return jax.shard_map(shards, mesh=mesh, in_specs=in_specs, out_specs=out_specs, check_vma=False)
```

profile of v0, /device:TPU:1, one launch (start us, length us, event | category | flops | bytes accessed | tf_op | source)
XLA Modules:
  0.0 270.8 jit_solution(9936922095612190733)
XLA Ops:
  7.2 1.6 copy.15
  8.9 0.7 all-gather.5.cloned.1.call-update
  9.6 1.3 copy.13
  11.7 1.5 fusion.29
  13.2 41.2 %all-gather.3.cloned.1.call-done = bf16[1,4096,2,128]{3,1,2,0:T(8,128)(2,1)} async-done(((bf16[1,256,2,128]{3,1,2,0:T(8,128)(2,1)}), bf16[1,4096,2,128]{3,1,2,0:T(8,128)(2,1)}) %all-gather.3.cloned.1.call-update) | async-done | bytes 2097168 | tf_op jit(solution)/shard_map/all_gather | solution.py:36
  54.4 1.7 slice_bitcast_fusion
  56.1 1.1 pad_maximum_fusion
  57.2 0.1 pad_maximum_fusion.1
  57.3 39.2 %while.13 = (s32[]{:T(128)}, f32[5,1,1,512,1]{3,0,2,1,4:T(8,128)S(1)}, f32[5,1,1,512,128]{3,4,0,2,1:T(8,128)S(1)}, bf16[5,512,1,1,128]{1,4,0,3,2:T(8,128)(2,1)S(...) while((s32[]{:T(128)}, ...), condition=%wide.region_3.4_spmd.clone, body=%wide.region_0.3_spmd.clone.sunk | while | flops 1229192192 | bytes 31102064 | solution.py:50
  57.3 4.1 %fusion.39 = (f32[512]{0:T(512)S(1)}, f32[1,1,512,4608]{3,2,1,0:T(8,128)S(1)}) fusion(bf16[4608,1,128]{2,0,1:T(8,128)(2,1)} %get-tuple-element.179, bf16[5,512,1,1,128]{1,4,0,3,2:T(8,128)(2,1)S(1)} %get-tuple-element.178, s32[]{:T(128)} %get-tuple-element.165, s32[4608]{0:T(1024)S(1)} %get-tuple-element.181, pred[4608]{0:T(1024)(128)(4,1)S(1)} %get-tuple-element.182), kind=kOutput, calls=%fused_computation.38.clone.1 | convolution fusion | flops 615775744 | bytes 10775556 | tf_op jit(solution)/shard_map/while/body/eval_jaxpr/cgjh,lgh->gjcl/dot_general | solution.py:12
  61.4 2.2 fusion.41
  63.7 1.4 fusion.40
  65.2 4.1 %fusion.39 = (f32[512]{0:T(512)S(1)}, f32[1,1,512,4608]{3,2,1,0:T(8,128)S(1)}) fusion(bf16[4608,1,128]{2,0,1:T(8,128)(2,1)} %get-tuple-element.179, bf16[5,512,1,1,128]{1,4,0,3,2:T(8,128)(2,1)S(1)} %get-tuple-element.178, s32[]{:T(128)} %get-tuple-element.165, s32[4608]{0:T(1024)S(1)} %get-tuple-element.181, pred[4608]{0:T(1024)(128)(4,1)S(1)} %get-tuple-element.182), kind=kOutput, calls=%fused_computation.38.clone.1 | convolution fusion | flops 615775744 | bytes 10775556 | tf_op jit(solution)/shard_map/while/body/eval_jaxpr/cgjh,lgh->gjcl/dot_general | solution.py:12
  69.3 2.2 fusion.41
  71.5 1.4 fusion.40
  73.0 4.1 %fusion.39 = (f32[512]{0:T(512)S(1)}, f32[1,1,512,4608]{3,2,1,0:T(8,128)S(1)}) fusion(bf16[4608,1,128]{2,0,1:T(8,128)(2,1)} %get-tuple-element.179, bf16[5,512,1,1,128]{1,4,0,3,2:T(8,128)(2,1)S(1)} %get-tuple-element.178, s32[]{:T(128)} %get-tuple-element.165, s32[4608]{0:T(1024)S(1)} %get-tuple-element.181, pred[4608]{0:T(1024)(128)(4,1)S(1)} %get-tuple-element.182), kind=kOutput, calls=%fused_computation.38.clone.1 | convolution fusion | flops 615775744 | bytes 10775556 | tf_op jit(solution)/shard_map/while/body/eval_jaxpr/cgjh,lgh->gjcl/dot_general | solution.py:12
  77.1 2.2 fusion.41
  79.4 1.4 fusion.40
  80.8 4.1 %fusion.39 = (f32[512]{0:T(512)S(1)}, f32[1,1,512,4608]{3,2,1,0:T(8,128)S(1)}) fusion(bf16[4608,1,128]{2,0,1:T(8,128)(2,1)} %get-tuple-element.179, bf16[5,512,1,1,128]{1,4,0,3,2:T(8,128)(2,1)S(1)} %get-tuple-element.178, s32[]{:T(128)} %get-tuple-element.165, s32[4608]{0:T(1024)S(1)} %get-tuple-element.181, pred[4608]{0:T(1024)(128)(4,1)S(1)} %get-tuple-element.182), kind=kOutput, calls=%fused_computation.38.clone.1 | convolution fusion | flops 615775744 | bytes 10775556 | tf_op jit(solution)/shard_map/while/body/eval_jaxpr/cgjh,lgh->gjcl/dot_general | solution.py:12
  85.0 2.2 fusion.41
  87.2 1.4 fusion.40
  88.7 4.1 %fusion.39 = (f32[512]{0:T(512)S(1)}, f32[1,1,512,4608]{3,2,1,0:T(8,128)S(1)}) fusion(bf16[4608,1,128]{2,0,1:T(8,128)(2,1)} %get-tuple-element.179, bf16[5,512,1,1,128]{1,4,0,3,2:T(8,128)(2,1)S(1)} %get-tuple-element.178, s32[]{:T(128)} %get-tuple-element.165, s32[4608]{0:T(1024)S(1)} %get-tuple-element.181, pred[4608]{0:T(1024)(128)(4,1)S(1)} %get-tuple-element.182), kind=kOutput, calls=%fused_computation.38.clone.1 | convolution fusion | flops 615775744 | bytes 10775556 | tf_op jit(solution)/shard_map/while/body/eval_jaxpr/cgjh,lgh->gjcl/dot_general | solution.py:12
  92.8 2.2 fusion.41
  95.0 1.4 fusion.40
  96.5 0.2 fusion.27
  96.7 0.1 bitcast_select_fusion.1
  96.8 40.2 %all-gather.5.cloned.1.call-done = bf16[640,5120]{0,1:T(8,128)(2,1)} async-done(((bf16[640,80]{0,1:T(8,128)(2,1)}), bf16[640,5120]{0,1:T(8,128)(2,1)}) %all-gather.5.cloned.1.call-update) | async-done | bytes 6553616 | tf_op jit(solution)/shard_map/all_gather | solution.py:62
  137.0 8.9 %convolution_convert_fusion = bf16[512,5120]{1,0:T(8,128)(2,1)} fusion(bf16[512,640]{0,1:T(8,128)(2,1)S(1)} %bitcast_select_fusion.1, bf16[640,5120]{0,1:T(8,128)(2,1)} %all-gather.5.cloned.1.call-done), kind=kOutput, calls=%fused_computation.18 | convolution fusion | flops 3358064640 | bytes 12451840 | tf_op jit(solution)/shard_map/dot_general | solution.py:60
  146.0 111.1 %all-reduce.2.cloned.1.call-done = bf16[512,5120]{1,0:T(8,128)(2,1)} async-done(((bf16[512,5120]{1,0:T(8,128)(2,1)}), bf16[512,5120]{1,0:T(8,128)(2,1)}) %all-reduce.2.cloned.1.call-update) | async-done | bytes 5242896 | tf_op jit(solution)/shard_map/psum | solution.py:66
  257.1 1.8 multiply_reduce_fusion
  258.9 2.5 fusion.25
  261.4 2.9 %fusion.26 = bf16[1,1,128,5120]{3,2,1,0:T(8,128)(2,1)} fusion(bf16[1,1,128,5120]{3,2,1,0:T(8,128)(2,1)S(1)} %copy-done, f32[5120]{0:T(1024)S(1)} %copy-done.1, f32[128]{0:T(128)S(1)} %add_rsqrt_fusion, bf16[512,5120]{1,0:T(8,128)(2,1)} %all-reduce.2.cloned.1.call-done, s32[]{:T(128)S(6)} %select_n.12), kind=kLoop, calls=%fused_computation.24 | loop fusion | flops 5242880 | bytes 3953156 | tf_op jit(solution)/shard_map/broadcast_in_dim | solution.py:71
  (21 shorter events, 0.5 us)
Async XLA Ops:
  7.2 47.3 %all-gather.3.cloned.1.call-start = ((), (), s32[]{:S(2)}) async-start(), calls=%async_computation | async-start | bytes 2228224 | tf_op jit(solution)/shard_map/all_gather | solution.py:36
  8.8 128.2 %all-gather.5.cloned.1.call-start = ((), (), s32[]{:S(2)}) async-start(), calls=%async_computation.1 | async-start | bytes 6656000 | tf_op jit(solution)/shard_map/all_gather | solution.py:62
  9.6 247.5 %all-reduce.2.cloned.1.call-start = ((), (), s32[]{:S(2)}) async-start(), calls=%async_computation.2 | async-start | bytes 10485760 | tf_op jit(solution)/shard_map/psum | solution.py:66
  145.9 111.2 %copy-start = (bf16[1,1,128,5120]{3,2,1,0:T(8,128)(2,1)S(1)}, bf16[1,1,128,5120]{3,2,1,0:T(8,128)(2,1)}, u32[]{:S(2)}) copy-start(bf16[1,1,128,5120]{3,2,1,0:T(8,128)(2,1)} %param.12) | copy-start | bytes 3932164
  145.9 115.5 %copy-start.1 = (f32[5120]{0:T(1024)S(1)}, f32[5120]{0:T(1024)}, u32[]{:S(2)}) copy-start(f32[5120]{0:T(1024)} %param.14) | copy-start | bytes 61444
Sparse Core Ops, SparseCore 0:
  10.4 43.9 all-gather.2
  57.1 79.8 all-gather.4
  146.1 110.9 all-reduce.1
where the time goes:
time: 271 us
  waiting for transfers between devices  193 us (71%)
  matrix products  40.7 us (15%)
  other arithmetic  15.6 us (6%)
  between operations  14.5 us (5%)
  local copies, waits for them, and re-layouts  6.4 us (2%)
    psum x1, waiting for transfers between devices, shards(): summed = lax.psum(terms.astype(jnp.bfloat16), 'tensor').astype(jnp.float32)  111 us
    all_gather x1, waiting for transfers between devices, shards(): whole_prompt = lax.all_gather(prompt_kv, 'group', axis=1, tiled=True)  41.2 us
    all_gather x1, waiting for transfers between devices, shards(): lax.all_gather(out_weight, ('dp', 'group'), axis=1, tiled=True)  40.2 us
    dot_general x5, matrix products, block_stats(): jnp.einsum('cgjh,lgh->gjcl', query_part, keys_part, preferred_element_typ...  20.7 us
    dot_general x5, matrix products, block_stats(): jnp.einsum('gjcl,lgh->gjch', weights.astype(jnp.bfloat16), values_part, p...  11.1 us
    dot_general x1, matrix products, shards(): jnp.dot(context, lax.all_gather(out_weight, ('dp', 'group'), axis=1, tile...  8.94 us
    reduce_sum x5, other arithmetic, block_stats(): total = jnp.sum(weights, axis=-1, keepdims=True)  7.02 us
  transfers between devices with their start and end apart: 3, of which 3 were waited for; matrix products, arithmetic and copies ran while one was open for 17% of the time, Pallas kernels for 0%

commit v1 on v0

v1 whole, which is shorter than its diff:
```python
import functools

import jax
import jax.numpy as jnp
import numpy as np
from jax import lax
from jax.experimental import pallas as pl
from jax.experimental.pallas import tpu as pltpu
from jax.sharding import PartitionSpec as P

HD = 128
GROUPS = 5
CLEN = 512
PIECE = 256
SCALE = float(HD**-0.5 * np.log2(np.e))
F32 = jnp.float32
BF16 = jnp.bfloat16
NT = (((1,), (1,)), ((), ()))
ANY = pl.BlockSpec(memory_space=pl.ANY)
SMEM = pl.BlockSpec(memory_space=pltpu.SMEM)
VMEM = pl.BlockSpec(memory_space=pltpu.VMEM)
TILE = 128
PARAMS = pltpu.CompilerParams(vmem_limit_bytes=40 << 20)


def absorb(rows, keys, values, top, mixed, mask=None):
    scores = lax.dot_general(rows, keys, NT, preferred_element_type=F32)
    if mask is not None:
        scores = jnp.where(mask, scores, jnp.float32(-1e30))
    best = jnp.max(scores, axis=-1, keepdims=True) * SCALE
    if top is not None:
        best = jnp.maximum(top, best)
    weights = jnp.exp2(scores * SCALE - best).astype(BF16)
    part = jnp.dot(weights, values, preferred_element_type=F32)
    if top is None:
        return best, part
    return best, mixed * jnp.exp2(top - best) + part


def stage(blocks, keys, values, start):
    for block in blocks:
        for j in range(block.shape[0]):
            keys[start : start + PIECE] = block[j, 0]
            values[start : start + PIECE, :HD] = block[j, 1]
            start += PIECE
    return start


def attend_first(query, own, top_out, mixed_out, values):
    @pl.when(pl.program_id(0) == 0)
    def _():
        values[:, :HD] = own[1]
        values[:, HD:] = jnp.ones((CLEN, HD), BF16)

    for r in range(CLEN // TILE):
        extent = (r + 1) * TILE
        column = lax.broadcasted_iota(jnp.int32, (TILE, extent), 1)
        row = lax.broadcasted_iota(jnp.int32, (TILE, extent), 0)
        best, mixed = absorb(
            query[r], own[0, :extent], values[:extent], None, None, column - row <= r * TILE
        )
        top_out[0, r] = jnp.broadcast_to(best, (TILE, HD))
        mixed_out[0, r] = mixed


def attend_more(count, width, query, *refs):
    blocks, (top_in, mixed_in, top_out, mixed_out, keys, values) = refs[:count], refs[count:]

    @pl.when(pl.program_id(0) == 0)
    def _():
        stage(blocks, keys, values, 0)
        values[:, HD:] = jnp.ones((values.shape[0], HD), BF16)

    for r in range(CLEN // TILE):
        best, mixed = top_in[0, r][:, :1], mixed_in[0, r]
        for start in range(0, keys.shape[0], width):
            best, mixed = absorb(
                query[r], keys[start : start + width], values[start : start + width], best, mixed
            )
        top_out[0, r] = jnp.broadcast_to(best, (TILE, HD))
        mixed_out[0, r] = mixed


def attend_last(count, width, half, place, query, *refs):
    blocks, (top_in, mixed_in), outs, (keys, values) = (
        refs[:count],
        refs[count : count + 2],
        refs[count + 2 : -2],
        refs[-2:],
    )
    rows = outs[0].shape[0]
    x, live = place[0], place[3]

    @pl.when(pl.program_id(0) == 0)
    def _():
        stage(blocks, keys, values, 0)
        values[:, HD:] = jnp.ones((values.shape[0], HD), BF16)

    per = TILE // rows
    for d in range(0, 4, per):
        strips = [lax.rem(x + d + i, 4) for i in range(per)]
        best = jnp.concatenate([top_in[0, r] for r in strips], axis=0)[:, :1]
        mixed = jnp.concatenate([mixed_in[0, r] for r in strips], axis=0)
        lines = jnp.concatenate([query[r] for r in strips], axis=0)
        for start in range(0, keys.shape[0], width):
            best, mixed = absorb(
                lines, keys[start : start + width], values[start : start + width], best, mixed
            )
        context = mixed[:, :HD] / mixed[:, HD:]
        line = lax.broadcasted_iota(jnp.int32, (rows, HD), 0)
        for i, r in enumerate(strips):
            kept = jnp.where(
                line + (r * 128 + half * rows) < live, context[i * rows : (i + 1) * rows], 0.0
            )
            outs[d + i][...] = kept.astype(BF16)


def whole(a):
    return pl.BlockSpec(a.shape, lambda h: (0,) * a.ndim)


def cost(rows, keys):
    return pl.CostEstimate(
        flops=24 * rows * keys * HD, bytes_accessed=12 << 20, transcendentals=0
    )


def state_specs(rows, half):
    return [
        pl.BlockSpec((1, 4, rows, HD), lambda h: (h, 0, half, 0)),
        pl.BlockSpec((1, 4, rows, 2 * HD), lambda h: (h, 0, half, 0)),
    ]


STATE = [
    jax.ShapeDtypeStruct((GROUPS, 4, 128, HD), F32),
    jax.ShapeDtypeStruct((GROUPS, 4, 128, 2 * HD), F32),
]


def first_part(query, own):
    return pl.pallas_call(
        attend_first,
        grid=(GROUPS,),
        in_specs=[pl.BlockSpec((4, 128, HD), lambda h: (0, 0, h)), whole(own)],
        out_specs=state_specs(128, 0),
        out_shape=STATE,
        scratch_shapes=[pltpu.VMEM((CLEN, 2 * HD), BF16)],
        compiler_params=PARAMS,
        cost_estimate=cost(GROUPS * CLEN, CLEN),
    )(query, own)


def more_part(query, blocks, state, width):
    extent = sum(b.shape[0] for b in blocks) * PIECE
    return pl.pallas_call(
        functools.partial(attend_more, len(blocks), width),
        grid=(GROUPS,),
        in_specs=[pl.BlockSpec((4, 128, HD), lambda h: (0, 0, h))]
        + [whole(b) for b in blocks]
        + state_specs(128, 0),
        out_specs=state_specs(128, 0),
        out_shape=STATE,
        scratch_shapes=[pltpu.VMEM((extent, HD), BF16), pltpu.VMEM((extent, 2 * HD), BF16)],
        compiler_params=PARAMS,
        cost_estimate=cost(GROUPS * CLEN, extent),
    )(query, *blocks, *state)


def last_part(place, query, blocks, state, width, half, halves):
    extent = sum(b.shape[0] for b in blocks) * PIECE
    rows = 128 // halves
    return pl.pallas_call(
        functools.partial(attend_last, len(blocks), width, half),
        grid=(GROUPS,),
        in_specs=[SMEM, pl.BlockSpec((4, rows, HD), lambda h: (0, half, h))]
        + [whole(b) for b in blocks]
        + state_specs(rows, half),
        out_specs=[pl.BlockSpec((rows, HD), lambda h: (0, h))] * 4,
        out_shape=[jax.ShapeDtypeStruct((rows, GROUPS * HD), BF16)] * 4,
        scratch_shapes=[pltpu.VMEM((extent, HD), BF16), pltpu.VMEM((extent, 2 * HD), BF16)],
        compiler_params=PARAMS,
        cost_estimate=cost(GROUPS * CLEN // halves, extent),
    )(place, query, *blocks, *state)


def project(place, c0, c1, c2, c3, mine, other, o0, o1, o2, o3, held, sems):
    core = place[2]
    copies = []
    for z in range(8):
        for source, parity in ((mine, core), (other, 1 - core)):
            at = pl.multiple_of(z * 160 + parity * 80, 16)
            copies.append(
                pltpu.make_async_copy(
                    source.at[z], held.at[:, pl.ds(at, 80)], sems.at[len(copies)]
                )
            )
    for copy in copies:
        copy.start()
    contexts, outs = (c0, c1, c2, c3), (o0, o1, o2, o3)
    lines = [jnp.concatenate([c[j] for c in contexts], axis=0) for j in range(4)]
    rows = c0.shape[1]
    waited = 0
    for n in range(0, 1280, 256):
        while waited < len(copies) and waited // 2 * 160 < n + 256:
            copies[waited].wait()
            waited += 1
        total = None
        for j in range(4):
            part = lax.dot_general(lines[j], held[j, n : n + 256], NT, preferred_element_type=F32)
            total = part if total is None else total + part
        total = total.astype(BF16)
        for d, out in enumerate(outs):
            out[:, n : n + 256] = total[d * rows : (d + 1) * rows]


def projected(place, contexts, mine, other):
    rows = contexts[0].shape[1]
    block = jax.ShapeDtypeStruct((rows, 1280), BF16)
    return pl.pallas_call(
        project,
        in_specs=[SMEM] + [VMEM] * 4 + [ANY] * 2,
        out_specs=[VMEM] * 4,
        out_shape=[block] * 4,
        scratch_shapes=[pltpu.VMEM((4, 1280, 640), BF16), pltpu.SemaphoreType.DMA((16,))],
        compiler_params=PARAMS,
        cost_estimate=pl.CostEstimate(
            flops=rows * 2560 * 1280 // 4, bytes_accessed=1 << 20, transcendentals=0
        ),
    )(place, *contexts, mine, other)


def finish(place, *refs):
    count = (len(refs) - 4) // 4
    residual, gain, attended, normed = refs[-4:]
    y = place[1]
    for h in range(count):
        rows = refs[4 * h].shape[0]
        for d in range(4):
            at = pl.multiple_of(lax.rem(y + d, 4) * 1280, 1280)
            attended[h * rows : (h + 1) * rows, pl.ds(at, 1280)] = refs[4 * h + d][...]
    for r in range(0, 128, 16):
        stream = residual[r : r + 16].astype(F32) + attended[r : r + 16].astype(F32)
        power = jnp.mean(stream * stream, axis=-1, keepdims=True)
        normed[r : r + 16] = (stream * lax.rsqrt(power + 1e-06) * gain[...]).astype(BF16)


def finished(place, parts, residual, gain):
    block = jax.ShapeDtypeStruct((128, 5120), BF16)
    return pl.pallas_call(
        finish,
        in_specs=[SMEM] + [VMEM] * (len(parts) + 2),
        out_specs=[VMEM] * 2,
        out_shape=[block] * 2,
        compiler_params=PARAMS,
    )(place, *parts, residual, gain)


UP = [(i, (i + 1) % 4) for i in range(4)]
DOWN = [(i, (i - 1) % 4) for i in range(4)]
ACROSS = [(i, (i + 2) % 4) for i in range(4)]
SWAP = [(i, i ^ 1) for i in range(16)]
EACH_CORE = [list(range(0, 16, 2)), list(range(1, 16, 2))]


def along(distance):
    return [
        (g, (g // 2 + (distance if g % 2 == 0 else -distance)) % 8 * 2 + g % 2) for g in range(16)
    ]


def around(axis, down, across, up):
    return [
        lax.ppermute(down, axis, DOWN),
        lax.ppermute(across, axis, ACROSS),
        lax.ppermute(up, axis, UP),
    ]


def after(value, *others):
    return lax.optimization_barrier((value, *others))[0]


def shards(queries, comp_kv, prompt_kv, residual, out_weight, gain, lengths):
    x, y, group = lax.axis_index("tensor"), lax.axis_index("dp"), lax.axis_index("group")
    place = jnp.stack([x, y, group % 2, lengths[0, 0]]).astype(jnp.int32)
    query = queries[0, 0].reshape(4, 128, GROUPS * HD)
    swap = functools.partial(lax.ppermute, axis_name="group", perm=SWAP)

    with jax.named_scope("prompt"):
        piece = prompt_kv[0].transpose(1, 0, 2)[None]
        pair = jnp.concatenate([piece, swap(piece)], axis=0)

    weight = out_weight.T
    with jax.named_scope("weights"):
        weight = after(weight, pair)
        pieces = jnp.stack([weight] + around("tensor", weight, weight, weight))
        mine = lax.all_gather(pieces, "group", axis=0, axis_index_groups=EACH_CORE)

    with jax.named_scope("attention"):
        own = comp_kv[0, 0].transpose(1, 0, 2)
        state = first_part(query, own)
        come, late = pair, pair
        for step in range(3):
            come = after(lax.ppermute(come, "group", along(1)), *state)
            state = more_part(query, [late, come], state, 1024)
            late = swap(come)
        come = after(lax.ppermute(come[:1], "group", along(1)), *state)
        c0, c1, c2, c3 = last_part(place, query, [late, come, swap(come)], state, 1024, 0, 1)

    with jax.named_scope("exchange"):
        blocks = [c0] + around("tensor", c3, c2, c1)
        halves = 2
        rows = 128 // halves
        contexts = []
        for half in range(halves):
            mixed = jnp.stack([a[half * rows : (half + 1) * rows] for a in blocks])
            contexts.append([mixed] + around("dp", mixed, mixed, mixed))

    with jax.named_scope("weights"):
        mine = after(mine, contexts[0][0])
        other = swap(mine)
    parts = []
    for half in range(halves):
        with jax.named_scope("project"):
            o0, o1, o2, o3 = projected(place, contexts[half], mine, other)
            parts += [o0] + around("dp", o3, o2, o1)
    with jax.named_scope("finish"):
        attended, normed = finished(place, parts, residual[0, 0], gain[None])
    return (attended[None, None], normed[None, None])


def solution(mesh):
    in_specs = (
        P("dp", "group", None, "tensor"),
        P("dp", "group", None, None, "tensor"),
        P("dp", "group", None, "tensor"),
        P("dp", "group", "tensor", None),
        P("tensor", ("dp", "group")),
        P(),
        P("dp", "group"),
    )
    out_specs = (P("dp", "group", "tensor", None), P("dp", "group", "tensor", None))
    return jax.shard_map(shards, mesh=mesh, in_specs=in_specs, out_specs=out_specs, check_vma=False)
```

time: 271 us -> 155 us (0.57)
  waiting for transfers between devices: 193 us -> 53.4 us
  Pallas kernels: 0 us -> 45.9 us
  matrix products: 40.7 us -> 0 us
  starting transfers between devices: 0.12 us -> 32.1 us
  other arithmetic: 15.6 us -> 1.92 us
    psum x1 -> x0, waiting for transfers between devices: 111 us -> none  [shards(): summed = lax.psum(terms.astype(jnp.bfloat16), 'tensor').astype(jnp.float32)]
    all_gather x2 -> x1, waiting for transfers between devices: 81.4 us -> 0.02 us  [shards(): mine = lax.all_gather(pieces, 'group', axis=0, axis_index_groups=EACH_CORE)]
    ppermute x0 -> x28, waiting for transfers between devices: none -> 53.3 us  [the longest x6 21.1 us: around(): lax.ppermute(down, axis, DOWN)]
    pallas_call x0 -> x8, Pallas kernels: none -> 45.9 us  [the longest x3 17.7 us: more_part(): pl.pallas_call(functools.partial(attend_more, len(blocks), width), grid=(...]
    dot_general x11 -> x0, matrix products: 40.7 us -> none  [the longest x5 20.7 us: block_stats(): jnp.einsum('cgjh,lgh->gjcl', query_part, keys_part, preferred_element_typ...]
    ppermute x0 -> x28, starting transfers between devices: none -> 32.1 us  [the longest x6 8.21 us: around(): lax.ppermute(up, axis, UP)]
    reduce_sum x6 -> x0, other arithmetic: 8.84 us -> none  [the longest x5 7.02 us: block_stats(): total = jnp.sum(weights, axis=-1, keepdims=True)]
    broadcast_in_dim x4 -> x0, other arithmetic: 5.34 us -> none  [the longest x2 5.33 us: shards(): return (attended[None, None], normed.astype(jnp.bfloat16)[None, None])]
  transfers between devices with their start and end apart: 3 -> 29, of which waited for: 3 -> 15; matrix products, arithmetic and copies ran while one was open for 17% -> 0% of each run, Pallas kernels for 0% -> 28%
where the time goes in v1:
time: 155 us
  waiting for transfers between devices  53.4 us (34%)
  Pallas kernels  45.9 us (30%)
  starting transfers between devices  32.1 us (21%)
  between operations  14.9 us (10%)
  local copies, waits for them, and re-layouts  6.31 us (4%)
  other arithmetic  1.92 us (1%)
    ppermute x6, waiting for transfers between devices, around(): lax.ppermute(down, axis, DOWN)  21.1 us
    pallas_call x3, Pallas kernels, more_part(): pl.pallas_call(functools.partial(attend_more, len(blocks), width), grid=(...  17.7 us
    ppermute x6, waiting for transfers between devices, around(): lax.ppermute(up, axis, UP)  17.7 us
    pallas_call x2, Pallas kernels, projected(): pl.pallas_call(project, in_specs=[SMEM] + [VMEM] * 4 + [ANY] * 2, out_spe...  12.8 us
    ppermute x3, waiting for transfers between devices, shards(): come = after(lax.ppermute(come, 'group', along(1)), *state)  8.72 us
    ppermute x6, starting transfers between devices, around(): lax.ppermute(up, axis, UP)  8.21 us
    ppermute x3, starting transfers between devices, shards(): come = after(lax.ppermute(come, 'group', along(1)), *state)  7.34 us
    pallas_call x1, Pallas kernels, last_part(): pl.pallas_call(functools.partial(attend_last, len(blocks), width, half),...  6.65 us
  transfers between devices with their start and end apart: 29, of which 15 were waited for; matrix products, arithmetic and copies ran while one was open for 0% of the time, Pallas kernels for 28%

profile of v1, /device:TPU:1, one launch (start us, length us, event | category | flops | bytes accessed | tf_op | source)
XLA Modules:
  0.0 154.5 jit_solution(5103128519796946245)
XLA Ops:
  8.2 3.3 %collective-permute-start = (bf16[1,2,256,128]{3,2,1,0:T(8,128)(2,1)S(1)}, bf16[1,2,256,128]{3,2,1,0:T(8,128)(2,1)S(1)}, u32[]{:S(2)}, u32[]{:S(2)}) collective-permute-start(bf16[1,2,256,128]{3,2,1,0:T(8,128)(2,1)S(1)} %bitcast.55), channel_id=1, source_target_pairs={{0,4},{4,0},{8,12},{12,8},{16,20},{20,16},{24,28},{28,24},{32,36},... | collective-permute-start | bytes 393224 | tf_op jit(solution)/shard_map/prompt/ppermute | solution.py:292
  14.5 2.4 %collective-permute-done.15 = bf16[80,640]{1,0:T(8,128)(2,1)S(1)} collective-permute-done((bf16[80,640]{1,0:T(8,128)(2,1)}, bf16[80,640]{1,0:T(8,128)(2,1)S(1)}, u32[]{:S(2)}, u32[]{:S(2)}) %collective-permute-start.15) | collective-permute-done | bytes 102432 | tf_op jit(solution)/shard_map/weights/ppermute | solution.py:274
  17.0 1.7 %collective-permute-done.16 = bf16[80,640]{1,0:T(8,128)(2,1)S(1)} collective-permute-done((bf16[80,640]{1,0:T(8,128)(2,1)}, bf16[80,640]{1,0:T(8,128)(2,1)S(1)}, u32[]{:S(2)}, u32[]{:S(2)}) %collective-permute-start.16) | collective-permute-done | bytes 102432 | tf_op jit(solution)/shard_map/weights/ppermute | solution.py:275
  18.7 3.3 %collective-permute-done.17 = bf16[80,640]{1,0:T(8,128)(2,1)S(1)} collective-permute-done((bf16[80,640]{1,0:T(8,128)(2,1)}, bf16[80,640]{1,0:T(8,128)(2,1)S(1)}, u32[]{:S(2)}, u32[]{:S(2)}) %collective-permute-start.17) | collective-permute-done | bytes 102432 | tf_op jit(solution)/shard_map/weights/ppermute | solution.py:276
  22.1 1.7 %pad_maximum_fusion = bf16[4,80,640]{2,1,0:T(8,128)(2,1)} fusion(bf16[1,80,640]{2,1,0:T(8,128)(2,1)S(1)} %bitcast.63, bf16[1,80,640]{2,1,0:T(8,128)(2,1)S(1)} %bitcast.62, bf16[1,80,640]{2,1,0:T(8,128)(2,1)S(1)} %bitcast.61, bf16[1,80,640]{2,1,0:T(8,128)(2,1)} %bitcast.60), kind=kLoop, calls=%fused_computation | loop fusion | flops 614400 | bytes 819200 | tf_op jit(solution)/shard_map/weights/stack | solution.py:297
  23.8 5.5 %collective-permute-start.1 = (bf16[2,2,256,128]{3,2,1,0:T(8,128)(2,1)S(1)}, bf16[2,2,256,128]{3,2,1,0:T(8,128)(2,1)S(1)}, u32[]{:S(2)}, u32[]{:S(2)}) collective-permute-start(bf16[2,2,256,128]{3,2,1,0:T(8,128)(2,1)S(1)} %pad_maximum_fusion.3.refs_0_), channel_id=1, source_target_pairs={{0,8},{4,60},{8,16},{12,4},{16,24},{20,12},{24,32},{28,20},{32,40}... | collective-permute-start | bytes 786440 | tf_op jit(solution)/shard_map/attention/ppermute | solution.py:305
  29.4 6.1 %attention.5 = (f32[5,4,128,128]{3,2,1,0:T(8,128)S(1)}, f32[5,4,128,256]{3,2,1,0:T(8,128)S(1)}) custom-call(bf16[4,128,640]{2,1,0:T(8,128)(2,1)S(1)} %bitcast.50, bf16[2,512,128]{2,1,0:T(8,128)(2,1)S(1)} %bitcast.48), custom_call_target="tpu_custom_call" | custom-call | flops 4026531840 | bytes 12582912 | tf_op jit(solution)/shard_map/attention/pallas_call | solution.py:142
  36.3 5.9 %attention.6 = (f32[5,4,128,128]{3,2,1,0:T(8,128)S(1)}, f32[5,4,128,256]{3,2,1,0:T(8,128)S(1)}) custom-call(bf16[4,128,640]{2,1,0:T(8,128)(2,1)S(1)} %bitcast.51, bf16[2,2,256,128]{3,2,1,0:T(8,128)(2,1)S(1)} %pad_maximum_fusion.3.refs_0_, bf16[2,2,256,128]{3,2,1,0:T(8,128)(2,1)S(1)} %collective-permute-done.1.refs_1_, ...), custom_call_target="tpu_custom_call" | custom-call | flops 8053063680 | bytes 12582912 | tf_op jit(solution)/shard_map/attention/pallas_call | solution.py:156
  42.2 4.4 %collective-permute-done.2.refs_1_ = bf16[2,2,256,128]{3,2,1,0:T(8,128)(2,1)S(1)} collective-permute-done((bf16[2,2,256,128]{3,2,1,0:T(8,128)(2,1)S(1)}, bf16[2,2,256,128]{3,2,1,0:T(8,128)(2,1)S(1)}, u32[]{:S(2)}, u32[]{:S(2)}) %collective-permute-start.2) | collective-permute-done | bytes 262176 | tf_op jit(solution)/shard_map/attention/ppermute | solution.py:305
  47.6 5.9 %attention.7 = (f32[5,4,128,128]{3,2,1,0:T(8,128)S(1)}, f32[5,4,128,256]{3,2,1,0:T(8,128)S(1)}) custom-call(bf16[4,128,640]{2,1,0:T(8,128)(2,1)S(1)} %bitcast.52, bf16[2,2,256,128]{3,2,1,0:T(8,128)(2,1)S(1)} %collective-permute-done.4.refs_0_, bf16[2,2,256,128]{3,2,1,0:T(8,128)(2,1)S(1)} %collective-permute-done.2.refs_1_, ...), custom_call_target="tpu_custom_call" | custom-call | flops 8053063680 | bytes 12582912 | tf_op jit(solution)/shard_map/attention/pallas_call | solution.py:156
  53.5 4.3 %collective-permute-done.3.refs_1_ = bf16[2,2,256,128]{3,2,1,0:T(8,128)(2,1)S(1)} collective-permute-done((bf16[2,2,256,128]{3,2,1,0:T(8,128)(2,1)S(1)}, bf16[2,2,256,128]{3,2,1,0:T(8,128)(2,1)S(1)}, u32[]{:S(2)}, u32[]{:S(2)}) %collective-permute-start.3) | collective-permute-done | bytes 262176 | tf_op jit(solution)/shard_map/attention/ppermute | solution.py:305
  57.9 2.0 %collective-permute-start.5 = (bf16[2,2,256,128]{3,2,1,0:T(8,128)(2,1)S(1)}, bf16[2,2,256,128]{3,2,1,0:T(8,128)(2,1)S(1)}, u32[]{:S(2)}, u32[]{:S(2)}) collective-permute-start(bf16[2,2,256,128]{3,2,1,0:T(8,128)(2,1)S(1)} %collective-permute-done.3.refs_1_), channel_id=1, source_target_pairs={{0,4},{4,0},{8,12},{12,8},{16,20},{20,16},{24,28},{28,24},{32,36},... | collective-permute-start | bytes 786440 | tf_op jit(solution)/shard_map/attention/ppermute | solution.py:307
  60.1 5.9 %attention.8 = (f32[5,4,128,128]{3,2,1,0:T(8,128)S(1)}, f32[5,4,128,256]{3,2,1,0:T(8,128)S(1)}) custom-call(bf16[4,128,640]{2,1,0:T(8,128)(2,1)S(1)} %bitcast.53, bf16[2,2,256,128]{3,2,1,0:T(8,128)(2,1)S(1)} %collective-permute-done.7.refs_0_, bf16[2,2,256,128]{3,2,1,0:T(8,128)(2,1)S(1)} %collective-permute-done.3.refs_1_, ...), custom_call_target="tpu_custom_call" | custom-call | flops 8053063680 | bytes 12582912 | tf_op jit(solution)/shard_map/attention/pallas_call | solution.py:156
  66.0 1.5 copy-done.5
  69.9 1.8 %copy-done.6 = f32[5,4,128,256]{3,2,1,0:T(8,128)S(1)} copy-done((f32[5,4,128,256]{3,2,1,0:T(8,128)S(1)}, f32[5,4,128,256]{3,2,1,0:T(8,128)}, u32[]{:S(2)}) %copy-start.6) | copy-done | bytes 2621464
  71.6 6.6 %attention.9 = (bf16[128,640]{1,0:T(8,128)(2,1)S(1)}, bf16[128,640]{1,0:T(8,128)(2,1)S(1)}, bf16[128,640]{1,0:T(8,128)(2,1)S(1)}, bf16[128,640]{1,0:T(8,128)(2,1)S(1)}) custom-call(s32[4]{0:T(128)S(1)} %pad_add_fusion.place, bf16[4,128,640]{2,1,0:T(8,128)(2,1)S(1)} %bitcast.54, bf16[2,2,256,128]{3,2,1,0:T(8,128)(2,1)S(1)} %collective-permute-done.5.refs_0_, ...), custom_call_target="tpu_custom_call" | custom-call | flops 8053063680 | bytes 12582912 | tf_op jit(solution)/shard_map/attention/pallas_call | solution.py:173
  78.5 1.4 collective-permute-start.11
  79.8 3.9 %collective-permute-done.9 = bf16[128,640]{1,0:T(8,128)(2,1)S(1)} collective-permute-done((bf16[128,640]{1,0:T(8,128)(2,1)S(1)}, bf16[128,640]{1,0:T(8,128)(2,1)S(1)}, u32[]{:S(2)}, u32[]{:S(2)}) %collective-permute-start.9) | collective-permute-done | bytes 163872 | tf_op jit(solution)/shard_map/exchange/ppermute | solution.py:274
  83.8 1.6 %collective-permute-done.10 = bf16[128,640]{1,0:T(8,128)(2,1)S(1)} collective-permute-done((bf16[128,640]{1,0:T(8,128)(2,1)S(1)}, bf16[128,640]{1,0:T(8,128)(2,1)S(1)}, u32[]{:S(2)}, u32[]{:S(2)}) %collective-permute-start.10) | collective-permute-done | bytes 163872 | tf_op jit(solution)/shard_map/exchange/ppermute | solution.py:275
  85.4 4.2 %collective-permute-done.11 = bf16[128,640]{1,0:T(8,128)(2,1)S(1)} collective-permute-done((bf16[128,640]{1,0:T(8,128)(2,1)S(1)}, bf16[128,640]{1,0:T(8,128)(2,1)S(1)}, u32[]{:S(2)}, u32[]{:S(2)}) %collective-permute-start.11) | collective-permute-done | bytes 163872 | tf_op jit(solution)/shard_map/exchange/ppermute | solution.py:276
  90.3 3.5 %collective-permute-start.22 = (bf16[4,64,640]{2,1,0:T(8,128)(2,1)S(1)}, bf16[4,64,640]{2,1,0:T(8,128)(2,1)S(1)}, u32[]{:S(2)}, u32[]{:S(2)}) collective-permute-start(bf16[4,64,640]{2,1,0:T(8,128)(2,1)S(1)} %pad_maximum_fusion.2.c0), channel_id=1, source_target_pairs={{0,192},{64,0},{128,64},{192,128},{1,193},{65,1},{129,65},{193,129... | collective-permute-start | bytes 983048 | tf_op jit(solution)/shard_map/exchange/ppermute | solution.py:274
  94.7 1.9 %collective-permute-start.12 = (bf16[4,64,640]{2,1,0:T(8,128)(2,1)S(1)}, bf16[4,64,640]{2,1,0:T(8,128)(2,1)S(1)}, u32[]{:S(2)}, u32[]{:S(2)}) collective-permute-start(bf16[4,64,640]{2,1,0:T(8,128)(2,1)S(1)} %pad_maximum_fusion.1.c0), channel_id=1, source_target_pairs={{0,192},{64,0},{128,64},{192,128},{1,193},{65,1},{129,65},{193,129... | collective-permute-start | bytes 983048 | tf_op jit(solution)/shard_map/exchange/ppermute | solution.py:274
  96.6 11.2 %collective-permute-done.22.c1 = bf16[4,64,640]{2,1,0:T(8,128)(2,1)S(1)} collective-permute-done((bf16[4,64,640]{2,1,0:T(8,128)(2,1)S(1)}, bf16[4,64,640]{2,1,0:T(8,128)(2,1)S(1)}, u32[]{:S(2)}, u32[]{:S(2)}) %collective-permute-start.22) | collective-permute-done | bytes 327712 | tf_op jit(solution)/shard_map/exchange/ppermute | solution.py:274
  107.8 4.1 %collective-permute-start.14 = (bf16[4,64,640]{2,1,0:T(8,128)(2,1)S(1)}, bf16[4,64,640]{2,1,0:T(8,128)(2,1)S(1)}, u32[]{:S(2)}, u32[]{:S(2)}) collective-permute-start(bf16[4,64,640]{2,1,0:T(8,128)(2,1)S(1)} %pad_maximum_fusion.1.c0), channel_id=1, source_target_pairs={{0,64},{64,128},{128,192},{192,0},{1,65},{65,129},{129,193},{193,1... | collective-permute-start | bytes 983048 | tf_op jit(solution)/shard_map/exchange/ppermute | solution.py:276
  112.0 1.9 %copy-done = bf16[32,80,640]{2,1,0:T(8,128)(2,1)S(1)} copy-done((bf16[32,80,640]{2,1,0:T(8,128)(2,1)S(1)}, bf16[32,80,640]{2,1,0:T(8,128)(2,1)}, u32[]{:S(2)}) %copy-start) | copy-done | bytes 3276824
  113.9 6.4 %project.3 = (bf16[64,1280]{1,0:T(8,128)(2,1)S(1)}, bf16[64,1280]{1,0:T(8,128)(2,1)S(1)}, bf16[64,1280]{1,0:T(8,128)(2,1)S(1)}, bf16[64,1280]{1,0:T(8,128)(2,1)S(1)}) custom-call(s32[4]{0:T(128)S(1)} %pad_add_fusion.place, bf16[4,64,640]{2,1,0:T(8,128)(2,1)S(1)} %pad_maximum_fusion.2.c0, bf16[4,64,640]{2,1,0:T(8,128)(2,1)S(1)} %collective-permute-done.22.c1, ...), custom_call_target="tpu_custom_call" | custom-call | flops 52428800 | bytes 1048576 | tf_op jit(solution)/shard_map/project/pallas_call | solution.py:220
  120.4 1.8 %collective-permute-start.26 = (bf16[64,1280]{1,0:T(8,128)(2,1)S(1)}, bf16[64,1280]{1,0:T(8,128)(2,1)S(1)}, u32[]{:S(2)}, u32[]{:S(2)}) collective-permute-start(bf16[64,1280]{1,0:T(8,128)(2,1)S(1)} %get-tuple-element.54), channel_id=1, source_target_pairs={{0,128},{64,192},{128,0},{192,64},{1,129},{65,193},{129,1},{193,65... | collective-permute-start | bytes 491528 | tf_op jit(solution)/shard_map/project/ppermute | solution.py:275
  122.2 5.1 %collective-permute-done.14.c3 = bf16[4,64,640]{2,1,0:T(8,128)(2,1)S(1)} collective-permute-done((bf16[4,64,640]{2,1,0:T(8,128)(2,1)S(1)}, bf16[4,64,640]{2,1,0:T(8,128)(2,1)S(1)}, u32[]{:S(2)}, u32[]{:S(2)}) %collective-permute-start.14) | collective-permute-done | bytes 327712 | tf_op jit(solution)/shard_map/exchange/ppermute | solution.py:276
  127.4 6.4 %project.2 = (bf16[64,1280]{1,0:T(8,128)(2,1)S(1)}, bf16[64,1280]{1,0:T(8,128)(2,1)S(1)}, bf16[64,1280]{1,0:T(8,128)(2,1)S(1)}, bf16[64,1280]{1,0:T(8,128)(2,1)S(1)}) custom-call(s32[4]{0:T(128)S(1)} %pad_add_fusion.place, bf16[4,64,640]{2,1,0:T(8,128)(2,1)S(1)} %pad_maximum_fusion.1.c0, bf16[4,64,640]{2,1,0:T(8,128)(2,1)S(1)} %collective-permute-done.12.c1, ...), custom_call_target="tpu_custom_call" | custom-call | flops 52428800 | bytes 1048576 | tf_op jit(solution)/shard_map/project/pallas_call | solution.py:220
  135.4 3.5 %collective-permute-done.19.refs_1_ = bf16[64,1280]{1,0:T(8,128)(2,1)S(1)} collective-permute-done((bf16[64,1280]{1,0:T(8,128)(2,1)S(1)}, bf16[64,1280]{1,0:T(8,128)(2,1)S(1)}, u32[]{:S(2)}, u32[]{:S(2)}) %collective-permute-start.19) | collective-permute-done | bytes 163872 | tf_op jit(solution)/shard_map/project/ppermute | solution.py:274
  140.0 5.0 %collective-permute-done.21.refs_3_ = bf16[64,1280]{1,0:T(8,128)(2,1)S(1)} collective-permute-done((bf16[64,1280]{1,0:T(8,128)(2,1)S(1)}, bf16[64,1280]{1,0:T(8,128)(2,1)S(1)}, u32[]{:S(2)}, u32[]{:S(2)}) %collective-permute-start.21) | collective-permute-done | bytes 163872 | tf_op jit(solution)/shard_map/project/ppermute | solution.py:276
  145.1 2.6 %finish.1 = (bf16[128,5120]{1,0:T(8,128)(2,1)}, bf16[128,5120]{1,0:T(8,128)(2,1)}) custom-call(s32[4]{0:T(128)S(1)} %pad_add_fusion.place, bf16[64,1280]{1,0:T(8,128)(2,1)S(1)} %get-tuple-element.48.refs_0_, bf16[64,1280]{1,0:T(8,128)(2,1)S(1)} %collective-permute-done.19.refs_1_, bf16[64,1280]{1,0:T(8,128)(2,1)S(1)} %collective-permute-done.20.refs_2_, ...), custom_call_target="tpu_custom_call" | custom-call | tf_op jit(solution)/shard_map/finish/pallas_call | solution.py:250
  (63 shorter events, 12.4 us)
Async XLA Ops:
  7.2 22.2 %copy-start.4 = (bf16[1,1,512,640]{3,2,1,0:T(8,128)(2,1)S(1)}, bf16[1,1,512,640]{3,2,1,0:T(8,128)(2,1)}, u32[]{:S(2)}) copy-start(bf16[1,1,512,640]{3,2,1,0:T(8,128)(2,1)} %param.7) | copy-start | bytes 1966084
  7.2 82.5 %all-gather.3.cloned.1.call-start = ((), (), s32[]{:S(2)}) async-start(), calls=%async_computation | async-start | bytes 3686400 | tf_op jit(solution)/shard_map/weights/all_gather | solution.py:298
  8.2 4.3 %collective-permute-start = (bf16[1,2,256,128]{3,2,1,0:T(8,128)(2,1)S(1)}, bf16[1,2,256,128]{3,2,1,0:T(8,128)(2,1)S(1)}, u32[]{:S(2)}, u32[]{:S(2)}) collective-permute-start(bf16[1,2,256,128]{3,2,1,0:T(8,128)(2,1)S(1)} %bitcast.55), channel_id=1, source_target_pairs={{0,4},{4,0},{8,12},{12,8},{16,20},{20,16},{24,28},{28,24},{32,36},... | collective-permute-start | bytes 393224 | tf_op jit(solution)/shard_map/prompt/ppermute | solution.py:292
  12.6 4.4 %collective-permute-start.15 = (bf16[80,640]{1,0:T(8,128)(2,1)}, bf16[80,640]{1,0:T(8,128)(2,1)S(1)}, u32[]{:S(2)}, u32[]{:S(2)}) collective-permute-start(bf16[80,640]{1,0:T(8,128)(2,1)} %bitcast.57), channel_id=1, source_target_pairs={{0,3},{1,0},{2,1},{3,2},{4,7},{5,4},{6,5},{7,6},{8,11},{9,8},{10,9... | collective-permute-start | bytes 307208 | tf_op jit(solution)/shard_map/weights/ppermute | solution.py:274
  13.4 5.3 %collective-permute-start.16 = (bf16[80,640]{1,0:T(8,128)(2,1)}, bf16[80,640]{1,0:T(8,128)(2,1)S(1)}, u32[]{:S(2)}, u32[]{:S(2)}) collective-permute-start(bf16[80,640]{1,0:T(8,128)(2,1)} %bitcast.58), channel_id=1, source_target_pairs={{0,2},{1,3},{2,0},{3,1},{4,6},{5,7},{6,4},{7,5},{8,10},{9,11},{10,... | collective-permute-start | bytes 307208 | tf_op jit(solution)/shard_map/weights/ppermute | solution.py:275
  13.9 8.1 %collective-permute-start.17 = (bf16[80,640]{1,0:T(8,128)(2,1)}, bf16[80,640]{1,0:T(8,128)(2,1)S(1)}, u32[]{:S(2)}, u32[]{:S(2)}) collective-permute-start(bf16[80,640]{1,0:T(8,128)(2,1)} %bitcast.59), channel_id=1, source_target_pairs={{0,1},{1,2},{2,3},{3,0},{4,5},{5,6},{6,7},{7,4},{8,9},{9,10},{10,1... | collective-permute-start | bytes 307208 | tf_op jit(solution)/shard_map/weights/ppermute | solution.py:276
  23.8 11.7 %collective-permute-start.1 = (bf16[2,2,256,128]{3,2,1,0:T(8,128)(2,1)S(1)}, bf16[2,2,256,128]{3,2,1,0:T(8,128)(2,1)S(1)}, u32[]{:S(2)}, u32[]{:S(2)}) collective-permute-start(bf16[2,2,256,128]{3,2,1,0:T(8,128)(2,1)S(1)} %pad_maximum_fusion.3.refs_0_), channel_id=1, source_target_pairs={{0,8},{4,60},{8,16},{12,4},{16,24},{20,12},{24,32},{28,20},{32,40}... | collective-permute-start | bytes 786440 | tf_op jit(solution)/shard_map/attention/ppermute | solution.py:305
  35.5 11.1 %collective-permute-start.2 = (bf16[2,2,256,128]{3,2,1,0:T(8,128)(2,1)S(1)}, bf16[2,2,256,128]{3,2,1,0:T(8,128)(2,1)S(1)}, u32[]{:S(2)}, u32[]{:S(2)}) collective-permute-start(bf16[2,2,256,128]{3,2,1,0:T(8,128)(2,1)S(1)} %collective-permute-done.1.refs_1_), channel_id=1, source_target_pairs={{0,8},{4,60},{8,16},{12,4},{16,24},{20,12},{24,32},{28,20},{32,40}... | collective-permute-start | bytes 786440 | tf_op jit(solution)/shard_map/attention/ppermute | solution.py:305
  36.3 11.3 %collective-permute-start.4 = (bf16[2,2,256,128]{3,2,1,0:T(8,128)(2,1)S(1)}, bf16[2,2,256,128]{3,2,1,0:T(8,128)(2,1)S(1)}, u32[]{:S(2)}, u32[]{:S(2)}) collective-permute-start(bf16[2,2,256,128]{3,2,1,0:T(8,128)(2,1)S(1)} %collective-permute-done.1.refs_1_), channel_id=1, source_target_pairs={{0,4},{4,0},{8,12},{12,8},{16,20},{20,16},{24,28},{28,24},{32,36},... | collective-permute-start | bytes 786440 | tf_op jit(solution)/shard_map/attention/ppermute | solution.py:307
  46.6 11.2 %collective-permute-start.3 = (bf16[2,2,256,128]{3,2,1,0:T(8,128)(2,1)S(1)}, bf16[2,2,256,128]{3,2,1,0:T(8,128)(2,1)S(1)}, u32[]{:S(2)}, u32[]{:S(2)}) collective-permute-start(bf16[2,2,256,128]{3,2,1,0:T(8,128)(2,1)S(1)} %collective-permute-done.2.refs_1_), channel_id=1, source_target_pairs={{0,8},{4,60},{8,16},{12,4},{16,24},{20,12},{24,32},{28,20},{32,40}... | collective-permute-start | bytes 786440 | tf_op jit(solution)/shard_map/attention/ppermute | solution.py:305
  47.6 12.4 %collective-permute-start.7 = (bf16[2,2,256,128]{3,2,1,0:T(8,128)(2,1)S(1)}, bf16[2,2,256,128]{3,2,1,0:T(8,128)(2,1)S(1)}, u32[]{:S(2)}, u32[]{:S(2)}) collective-permute-start(bf16[2,2,256,128]{3,2,1,0:T(8,128)(2,1)S(1)} %collective-permute-done.2.refs_1_), channel_id=1, source_target_pairs={{0,4},{4,0},{8,12},{12,8},{16,20},{20,16},{24,28},{28,24},{32,36},... | collective-permute-start | bytes 786440 | tf_op jit(solution)/shard_map/attention/ppermute | solution.py:307
  57.9 12.0 %collective-permute-start.5 = (bf16[2,2,256,128]{3,2,1,0:T(8,128)(2,1)S(1)}, bf16[2,2,256,128]{3,2,1,0:T(8,128)(2,1)S(1)}, u32[]{:S(2)}, u32[]{:S(2)}) collective-permute-start(bf16[2,2,256,128]{3,2,1,0:T(8,128)(2,1)S(1)} %collective-permute-done.3.refs_1_), channel_id=1, source_target_pairs={{0,4},{4,0},{8,12},{12,8},{16,20},{20,16},{24,28},{28,24},{32,36},... | collective-permute-start | bytes 786440 | tf_op jit(solution)/shard_map/attention/ppermute | solution.py:307
  59.8 7.7 %collective-permute-start.6 = (bf16[1,2,256,128]{3,2,1,0:T(8,128)(2,1)S(1)}, bf16[1,2,256,128]{3,2,1,0:T(8,128)(2,1)S(1)}, u32[]{:S(2)}, u32[]{:S(2)}) collective-permute-start(bf16[1,2,256,128]{3,2,1,0:T(8,128)(2,1)S(1)} %slice.27), channel_id=1, source_target_pairs={{0,8},{4,60},{8,16},{12,4},{16,24},{20,12},{24,32},{28,20},{32,40}... | collective-permute-start | bytes 393224 | tf_op jit(solution)/shard_map/attention/ppermute | solution.py:308
  67.5 2.3 %collective-permute-start.8 = (bf16[1,2,256,128]{3,2,1,0:T(8,128)(2,1)S(1)}, bf16[1,2,256,128]{3,2,1,0:T(8,128)(2,1)S(1)}, u32[]{:S(2)}, u32[]{:S(2)}) collective-permute-start(bf16[1,2,256,128]{3,2,1,0:T(8,128)(2,1)S(1)} %collective-permute-done.6.refs_1_), channel_id=1, source_target_pairs={{0,4},{4,0},{8,12},{12,8},{16,20},{20,16},{24,28},{28,24},{32,36},... | collective-permute-start | bytes 393224 | tf_op jit(solution)/shard_map/attention/ppermute | solution.py:309
  78.3 5.5 %collective-permute-start.9 = (bf16[128,640]{1,0:T(8,128)(2,1)S(1)}, bf16[128,640]{1,0:T(8,128)(2,1)S(1)}, u32[]{:S(2)}, u32[]{:S(2)}) collective-permute-start(bf16[128,640]{1,0:T(8,128)(2,1)S(1)} %get-tuple-element.43), channel_id=1, source_target_pairs={{0,3},{1,0},{2,1},{3,2},{4,7},{5,4},{6,5},{7,6},{8,11},{9,8},{10,9... | collective-permute-start | bytes 491528 | tf_op jit(solution)/shard_map/exchange/ppermute | solution.py:274
  78.4 7.0 %collective-permute-start.10 = (bf16[128,640]{1,0:T(8,128)(2,1)S(1)}, bf16[128,640]{1,0:T(8,128)(2,1)S(1)}, u32[]{:S(2)}, u32[]{:S(2)}) collective-permute-start(bf16[128,640]{1,0:T(8,128)(2,1)S(1)} %get-tuple-element.44), channel_id=1, source_target_pairs={{0,2},{1,3},{2,0},{3,1},{4,6},{5,7},{6,4},{7,5},{8,10},{9,11},{10,... | collective-permute-start | bytes 491528 | tf_op jit(solution)/shard_map/exchange/ppermute | solution.py:275
  78.5 11.1 %collective-permute-start.11 = (bf16[128,640]{1,0:T(8,128)(2,1)S(1)}, bf16[128,640]{1,0:T(8,128)(2,1)S(1)}, u32[]{:S(2)}, u32[]{:S(2)}) collective-permute-start(bf16[128,640]{1,0:T(8,128)(2,1)S(1)} %get-tuple-element.45), channel_id=1, source_target_pairs={{0,1},{1,2},{2,3},{3,0},{4,5},{5,6},{6,7},{7,4},{8,9},{9,10},{10,1... | collective-permute-start | bytes 491528 | tf_op jit(solution)/shard_map/exchange/ppermute | solution.py:276
  89.7 22.3 %collective-permute-start.18 = (bf16[8,4,80,640]{3,2,1,0:T(8,128)(2,1)}, bf16[8,4,80,640]{3,2,1,0:T(8,128)(2,1)S(1)}, u32[]{:S(2)}, u32[]{:S(2)}) collective-permute-start(bf16[8,4,80,640]{3,2,1,0:T(8,128)(2,1)} %bitcast.44), channel_id=1, source_target_pairs={{0,4},{4,0},{8,12},{12,8},{16,20},{20,16},{24,28},{28,24},{32,36},... | collective-permute-start | bytes 9830408 | tf_op jit(solution)/shard_map/weights/ppermute | solution.py:322
  90.3 17.5 %collective-permute-start.22 = (bf16[4,64,640]{2,1,0:T(8,128)(2,1)S(1)}, bf16[4,64,640]{2,1,0:T(8,128)(2,1)S(1)}, u32[]{:S(2)}, u32[]{:S(2)}) collective-permute-start(bf16[4,64,640]{2,1,0:T(8,128)(2,1)S(1)} %pad_maximum_fusion.2.c0), channel_id=1, source_target_pairs={{0,192},{64,0},{128,64},{192,128},{1,193},{65,1},{129,65},{193,129... | collective-permute-start | bytes 983048 | tf_op jit(solution)/shard_map/exchange/ppermute | solution.py:274
  93.8 14.0 %collective-permute-start.23 = (bf16[4,64,640]{2,1,0:T(8,128)(2,1)S(1)}, bf16[4,64,640]{2,1,0:T(8,128)(2,1)S(1)}, u32[]{:S(2)}, u32[]{:S(2)}) collective-permute-start(bf16[4,64,640]{2,1,0:T(8,128)(2,1)S(1)} %pad_maximum_fusion.2.c0), channel_id=1, source_target_pairs={{0,128},{64,192},{128,0},{192,64},{1,129},{65,193},{129,1},{193,65... | collective-permute-start | bytes 983048 | tf_op jit(solution)/shard_map/exchange/ppermute | solution.py:275
  93.9 18.1 %collective-permute-start.24 = (bf16[4,64,640]{2,1,0:T(8,128)(2,1)S(1)}, bf16[4,64,640]{2,1,0:T(8,128)(2,1)S(1)}, u32[]{:S(2)}, u32[]{:S(2)}) collective-permute-start(bf16[4,64,640]{2,1,0:T(8,128)(2,1)S(1)} %pad_maximum_fusion.2.c0), channel_id=1, source_target_pairs={{0,64},{64,128},{128,192},{192,0},{1,65},{65,129},{129,193},{193,1... | collective-permute-start | bytes 983048 | tf_op jit(solution)/shard_map/exchange/ppermute | solution.py:276
  94.7 27.5 %collective-permute-start.12 = (bf16[4,64,640]{2,1,0:T(8,128)(2,1)S(1)}, bf16[4,64,640]{2,1,0:T(8,128)(2,1)S(1)}, u32[]{:S(2)}, u32[]{:S(2)}) collective-permute-start(bf16[4,64,640]{2,1,0:T(8,128)(2,1)S(1)} %pad_maximum_fusion.1.c0), channel_id=1, source_target_pairs={{0,192},{64,0},{128,64},{192,128},{1,193},{65,1},{129,65},{193,129... | collective-permute-start | bytes 983048 | tf_op jit(solution)/shard_map/exchange/ppermute | solution.py:274
  107.8 14.4 %collective-permute-start.13 = (bf16[4,64,640]{2,1,0:T(8,128)(2,1)S(1)}, bf16[4,64,640]{2,1,0:T(8,128)(2,1)S(1)}, u32[]{:S(2)}, u32[]{:S(2)}) collective-permute-start(bf16[4,64,640]{2,1,0:T(8,128)(2,1)S(1)} %pad_maximum_fusion.1.c0), channel_id=1, source_target_pairs={{0,128},{64,192},{128,0},{192,64},{1,129},{65,193},{129,1},{193,65... | collective-permute-start | bytes 983048 | tf_op jit(solution)/shard_map/exchange/ppermute | solution.py:275
  107.8 19.5 %collective-permute-start.14 = (bf16[4,64,640]{2,1,0:T(8,128)(2,1)S(1)}, bf16[4,64,640]{2,1,0:T(8,128)(2,1)S(1)}, u32[]{:S(2)}, u32[]{:S(2)}) collective-permute-start(bf16[4,64,640]{2,1,0:T(8,128)(2,1)S(1)} %pad_maximum_fusion.1.c0), channel_id=1, source_target_pairs={{0,64},{64,128},{128,192},{192,0},{1,65},{65,129},{129,193},{193,1... | collective-permute-start | bytes 983048 | tf_op jit(solution)/shard_map/exchange/ppermute | solution.py:276
  120.3 13.7 %collective-permute-start.25 = (bf16[64,1280]{1,0:T(8,128)(2,1)S(1)}, bf16[64,1280]{1,0:T(8,128)(2,1)S(1)}, u32[]{:S(2)}, u32[]{:S(2)}) collective-permute-start(bf16[64,1280]{1,0:T(8,128)(2,1)S(1)} %get-tuple-element.53), channel_id=1, source_target_pairs={{0,192},{64,0},{128,64},{192,128},{1,193},{65,1},{129,65},{193,129... | collective-permute-start | bytes 491528 | tf_op jit(solution)/shard_map/project/ppermute | solution.py:274
  120.4 14.9 %collective-permute-start.26 = (bf16[64,1280]{1,0:T(8,128)(2,1)S(1)}, bf16[64,1280]{1,0:T(8,128)(2,1)S(1)}, u32[]{:S(2)}, u32[]{:S(2)}) collective-permute-start(bf16[64,1280]{1,0:T(8,128)(2,1)S(1)} %get-tuple-element.54), channel_id=1, source_target_pairs={{0,128},{64,192},{128,0},{192,64},{1,129},{65,193},{129,1},{193,65... | collective-permute-start | bytes 491528 | tf_op jit(solution)/shard_map/project/ppermute | solution.py:275
  122.2 22.9 %copy-start.2 = (bf16[1,1,128,5120]{3,2,1,0:T(8,128)(2,1)S(1)}, bf16[1,1,128,5120]{3,2,1,0:T(8,128)(2,1)}, u32[]{:S(2)}) copy-start(bf16[1,1,128,5120]{3,2,1,0:T(8,128)(2,1)} %param.10) | copy-start | bytes 3932164
  122.2 22.9 %copy-start.3 = (f32[5120]{0:T(1024)S(1)}, f32[5120]{0:T(1024)}, u32[]{:S(2)}) copy-start(f32[5120]{0:T(1024)} %param.12) | copy-start | bytes 61444
  122.2 13.1 %collective-permute-start.27 = (bf16[64,1280]{1,0:T(8,128)(2,1)S(1)}, bf16[64,1280]{1,0:T(8,128)(2,1)S(1)}, u32[]{:S(2)}, u32[]{:S(2)}) collective-permute-start(bf16[64,1280]{1,0:T(8,128)(2,1)S(1)} %get-tuple-element.55), channel_id=1, source_target_pairs={{0,64},{64,128},{128,192},{192,0},{1,65},{65,129},{129,193},{193,1... | collective-permute-start | bytes 491528 | tf_op jit(solution)/shard_map/project/ppermute | solution.py:276
  133.8 5.1 %collective-permute-start.19 = (bf16[64,1280]{1,0:T(8,128)(2,1)S(1)}, bf16[64,1280]{1,0:T(8,128)(2,1)S(1)}, u32[]{:S(2)}, u32[]{:S(2)}) collective-permute-start(bf16[64,1280]{1,0:T(8,128)(2,1)S(1)} %get-tuple-element.49), channel_id=1, source_target_pairs={{0,192},{64,0},{128,64},{192,128},{1,193},{65,1},{129,65},{193,129... | collective-permute-start | bytes 491528 | tf_op jit(solution)/shard_map/project/ppermute | solution.py:274
  133.9 6.1 %collective-permute-start.20 = (bf16[64,1280]{1,0:T(8,128)(2,1)S(1)}, bf16[64,1280]{1,0:T(8,128)(2,1)S(1)}, u32[]{:S(2)}, u32[]{:S(2)}) collective-permute-start(bf16[64,1280]{1,0:T(8,128)(2,1)S(1)} %get-tuple-element.50), channel_id=1, source_target_pairs={{0,128},{64,192},{128,0},{192,64},{1,129},{65,193},{129,1},{193,65... | collective-permute-start | bytes 491528 | tf_op jit(solution)/shard_map/project/ppermute | solution.py:275
  134.0 11.1 %collective-permute-start.21 = (bf16[64,1280]{1,0:T(8,128)(2,1)S(1)}, bf16[64,1280]{1,0:T(8,128)(2,1)S(1)}, u32[]{:S(2)}, u32[]{:S(2)}) collective-permute-start(bf16[64,1280]{1,0:T(8,128)(2,1)S(1)} %get-tuple-element.51), channel_id=1, source_target_pairs={{0,64},{64,128},{128,192},{192,0},{1,65},{65,129},{129,193},{193,1... | collective-permute-start | bytes 491528 | tf_op jit(solution)/shard_map/project/ppermute | solution.py:276
  (5 other events, 35.3 us)
Sparse Core Ops, SparseCore 0:
  23.9 53.3 all-gather.2

commit v2 on v0

v2 whole, which is shorter than its diff:
```python
import functools

import jax
import jax.numpy as jnp
import numpy as np
from jax import lax
from jax.experimental import pallas as pl
from jax.experimental.pallas import tpu as pltpu
from jax.sharding import PartitionSpec as P

HD = 128
GROUPS = 5
CLEN = 512
PIECE = 256
SCALE = float(HD**-0.5 * np.log2(np.e))
F32 = jnp.float32
BF16 = jnp.bfloat16
NT = (((1,), (1,)), ((), ()))
ANY = pl.BlockSpec(memory_space=pl.ANY)
SMEM = pl.BlockSpec(memory_space=pltpu.SMEM)
VMEM = pl.BlockSpec(memory_space=pltpu.VMEM)
TILE = 256
PARAMS = pltpu.CompilerParams(vmem_limit_bytes=20 << 20)


def absorb(rows, keys, values, top, mixed, mask=None):
    scores = lax.dot_general(rows, keys, NT, preferred_element_type=F32)
    if mask is not None:
        scores = jnp.where(mask, scores, jnp.float32(-1e30))
    best = jnp.max(scores, axis=-1, keepdims=True) * SCALE
    if top is not None:
        best = jnp.maximum(top, best)
    weights = jnp.exp2(scores * SCALE - best).astype(BF16)
    part = jnp.dot(weights, values, preferred_element_type=F32)
    if top is None:
        return best, part
    return best, mixed * jnp.exp2(top - best) + part


def load_state(top, mixed):
    total = jnp.broadcast_to(top[:, HD // 2 : HD // 2 + 1], mixed.shape)
    return top[:, :1], jnp.concatenate([mixed, total], axis=1)


def store_state(best, mixed):
    low = lax.broadcasted_iota(jnp.int32, mixed[:, :HD].shape, 1) < HD // 2
    return jnp.where(low, best, mixed[:, HD:]), mixed[:, :HD]


def stage(blocks, keys, values, start):
    for block in blocks:
        for j in range(block.shape[0]):
            keys[start : start + PIECE] = block[j, 0]
            values[start : start + PIECE, :HD] = block[j, 1]
            start += PIECE
    return start


def head(query, r, h):
    return query[r : r + TILE, h * HD : (h + 1) * HD]


def attend_first(count, query, own, *refs):
    blocks, (top_out, mixed_out, token, keys, values) = refs[:count], refs[count:]
    token[...] = jnp.zeros_like(token)
    prompt = stage(blocks, keys, values, 0)
    keys[prompt:] = own[0]
    values[prompt:, :HD] = own[1]
    values[:, HD:] = jnp.ones((values.shape[0], HD), BF16)

    for h in range(GROUPS):
        for r in range(0, CLEN, TILE):
            lines = head(query, r, h)
            best, mixed = absorb(lines, keys[:1024], values[:1024], None, None)
            extent = prompt + r + TILE - 1024
            column = lax.broadcasted_iota(jnp.int32, (TILE, extent), 1)
            row = lax.broadcasted_iota(jnp.int32, (TILE, extent), 0)
            best, mixed = absorb(
                lines,
                keys[1024 : 1024 + extent],
                values[1024 : 1024 + extent],
                best,
                mixed,
                column - row <= extent - TILE,
            )
            top_out[h, r : r + TILE], mixed_out[h, r : r + TILE] = store_state(best, mixed)


def attend_more(count, query, *refs):
    blocks, (top_in, mixed_in, top_out, mixed_out, token, keys, values) = (
        refs[:count],
        refs[count:],
    )
    token[...] = jnp.zeros_like(token)
    stage(blocks, keys, values, 0)
    values[:, HD:] = jnp.ones((values.shape[0], HD), BF16)

    for h in range(GROUPS):
        for r in range(0, CLEN, TILE):
            best, mixed = load_state(top_in[h, r : r + TILE], mixed_in[h, r : r + TILE])
            best, mixed = absorb(head(query, r, h), keys[...], values[...], best, mixed)
            top_out[h, r : r + TILE], mixed_out[h, r : r + TILE] = store_state(best, mixed)


def attend_last(count, place, query, *refs):
    blocks, (top_in, mixed_in, o0, o1, o2, o3, context, keys, values) = (
        refs[:count],
        refs[count:],
    )
    x, live = place[0], place[3]
    stage(blocks, keys, values, 0)
    values[:, HD:] = jnp.ones((values.shape[0], HD), BF16)

    for h in range(GROUPS):
        best, mixed = load_state(top_in[h], mixed_in[h])
        lines = query[:, h * HD : (h + 1) * HD]
        best, mixed = absorb(lines, keys[...], values[...], best, mixed)
        line = lax.broadcasted_iota(jnp.int32, (CLEN, HD), 0)
        context[:, h * HD : (h + 1) * HD] = jnp.where(
            line < live, mixed[:, :HD] / mixed[:, HD:], 0.0
        ).astype(BF16)
    for d, out in enumerate((o0, o1, o2, o3)):
        out[...] = context[pl.ds(pl.multiple_of(lax.rem(x + d, 4) * 128, 128), 128)]


def cost(rows, keys):
    return pl.CostEstimate(
        flops=24 * rows * keys * HD, bytes_accessed=12 << 20, transcendentals=0
    )


STATE = [jax.ShapeDtypeStruct((GROUPS, CLEN, HD), F32)] * 2
TOKEN = jax.ShapeDtypeStruct((8, HD), F32)


def room(blocks, more=0):
    extent = sum(b.shape[0] for b in blocks) * PIECE + more
    return [pltpu.VMEM((extent, HD), BF16), pltpu.VMEM((extent, 2 * HD), BF16)]


def first_part(query, own, blocks):
    return pl.pallas_call(
        functools.partial(attend_first, len(blocks)),
        in_specs=[VMEM] * (2 + len(blocks)),
        out_specs=[VMEM] * 3,
        out_shape=[pltpu.HBM(s.shape, s.dtype) for s in STATE] + [TOKEN],
        scratch_shapes=room(blocks, CLEN),
        compiler_params=PARAMS,
        cost_estimate=cost(GROUPS * CLEN, 2048),
    )(query, own, *blocks)


def more_part(query, blocks, state):
    return pl.pallas_call(
        functools.partial(attend_more, len(blocks)),
        in_specs=[VMEM] * (3 + len(blocks)),
        out_specs=[VMEM] * 3,
        out_shape=STATE + [TOKEN],
        scratch_shapes=room(blocks),
        compiler_params=PARAMS,
        cost_estimate=cost(GROUPS * CLEN, 1024),
    )(query, *blocks, *state)


def last_part(place, query, blocks, state):
    return pl.pallas_call(
        functools.partial(attend_last, len(blocks)),
        in_specs=[SMEM] + [VMEM] * (3 + len(blocks)),
        out_specs=[VMEM] * 4,
        out_shape=[jax.ShapeDtypeStruct((128, GROUPS * HD), BF16)] * 4,
        scratch_shapes=[pltpu.VMEM((CLEN, GROUPS * HD), BF16)] + room(blocks),
        compiler_params=PARAMS,
        cost_estimate=cost(GROUPS * CLEN, 1024),
    )(place, query, *blocks, *state)


def whole(a):
    return pl.BlockSpec(a.shape, lambda h: (0,) * a.ndim)


def gate(value, *refs):
    refs[-1][...] = value[...]


def gated(value, ready):
    return pl.pallas_call(
        gate,
        in_specs=[VMEM, ANY],
        out_specs=VMEM,
        out_shape=jax.ShapeDtypeStruct(value.shape, value.dtype),
        compiler_params=PARAMS,
    )(value, ready)


def widen(b0, b1, b2, b3, *refs):
    out = refs[-1]
    for j, block in enumerate((b0, b1, b2, b3)):
        out[:, j * 640 : (j + 1) * 640] = block[...]


def widened(blocks, *ready):
    return pl.pallas_call(
        widen,
        in_specs=[VMEM] * 4 + [ANY] * len(ready),
        out_specs=VMEM,
        out_shape=jax.ShapeDtypeStruct((80, 2560), BF16),
        compiler_params=PARAMS,
    )(*blocks, *ready)


def pack(place, *refs):
    blocks, out = refs[:-1], refs[-1]
    out[0] = blocks[0][...]
    for i in range(1, 4):
        out[i] = blocks[i][...]
    if len(blocks) > 4:

        @pl.when(place[2] == 1)
        def _():
            for i in range(1, 4):
                out[i] = blocks[i + 3][...]


def packed(place, *blocks):
    return pl.pallas_call(
        pack,
        in_specs=[SMEM] + [VMEM] * len(blocks),
        out_specs=VMEM,
        out_shape=jax.ShapeDtypeStruct((4, *blocks[0].shape), BF16),
        compiler_params=PARAMS,
    )(place, *blocks)


def project(place, c0, c1, c2, c3, columns, o0, o1, o2, o3, lines):
    contexts, outs = (c0, c1, c2, c3), (o0, o1, o2, o3)
    rows, depth = c0.shape[1:]

    def lay(pick):
        for d in range(4):
            for j in range(4):
                lines[d * rows : (d + 1) * rows, j * depth : (j + 1) * depth] = pick(d, j)

    @pl.when((pl.program_id(0) == 0) & (place[2] == 0))
    def _():
        lay(lambda d, j: contexts[j][(d - j) % 4])

    @pl.when((pl.program_id(0) == 0) & (place[2] == 1))
    def _():
        lay(lambda d, j: contexts[d][j])

    total = lax.dot_general(lines[...], columns[...], NT, preferred_element_type=F32)
    total = total.astype(BF16)
    for d, out in enumerate(outs):
        out[...] = total[d * rows : (d + 1) * rows]


def projected(place, contexts, columns):
    rows = contexts[0].shape[1]
    block = jax.ShapeDtypeStruct((rows, 1280), BF16)
    return pl.pallas_call(
        project,
        grid=(5,),
        in_specs=[SMEM]
        + [whole(c) for c in contexts]
        + [pl.BlockSpec((256, 2560), lambda n: (n, 0))],
        out_specs=[pl.BlockSpec((rows, 256), lambda n: (0, n))] * 4,
        out_shape=[block] * 4,
        scratch_shapes=[pltpu.VMEM((4 * rows, 2560), BF16)],
        compiler_params=pltpu.CompilerParams(vmem_limit_bytes=60 << 20),
        cost_estimate=pl.CostEstimate(
            flops=2 * 4 * rows * 2560 * 1280, bytes_accessed=10 << 20, transcendentals=0
        ),
    )(place, *contexts, columns)


def finish(place, p0, p1, p2, p3, residual, gain, attended, normed):
    quarter = place[0] + place[1]
    for d, part in enumerate((p0, p1, p2, p3)):
        at = pl.multiple_of(lax.rem(quarter + d, 4) * 1280, 1280)
        attended[:, pl.ds(at, 1280)] = part[...]
    for r in range(0, residual.shape[0], 16):
        stream = residual[r : r + 16].astype(F32) + attended[r : r + 16].astype(F32)
        power = jnp.mean(stream * stream, axis=-1, keepdims=True)
        normed[r : r + 16] = (stream * lax.rsqrt(power + 1e-06) * gain[...]).astype(BF16)


def finished(place, parts, residual, gain):
    block = jax.ShapeDtypeStruct((128, 5120), BF16)
    lines = 32
    wide = pl.BlockSpec((lines, 5120), lambda n: (n, 0))
    return pl.pallas_call(
        finish,
        grid=(128 // lines,),
        in_specs=[SMEM]
        + [pl.BlockSpec((lines, 1280), lambda n: (n, 0))] * 4
        + [wide, pl.BlockSpec((1, 5120), lambda n: (0, 0))],
        out_specs=[wide] * 2,
        out_shape=[block] * 2,
        compiler_params=PARAMS,
    )(place, *parts, residual, gain)


SWAP = [(i, i ^ 1) for i in range(16)]


def along(distance):
    return [
        (g, (g // 2 + (distance if g % 2 == 0 else -distance)) % 8 * 2 + g % 2) for g in range(16)
    ]


EVERY = ("dp", "group", "tensor")


def ring(step):
    pairs = []
    for y in range(4):
        for g in range(16):
            for x in range(4):
                to = (y, (x + step) % 4) if g % 2 == 0 else ((y + step) % 4, x)
                pairs.append(((y * 16 + g) * 4 + x, (to[0] * 16 + g) * 4 + to[1]))
    return pairs


SLANT = [(y * 4 + x, (y - x) % 4 * 4 + x) for y in range(4) for x in range(4)]


def around(axes, ways, behind, across, ahead):
    return [
        lax.ppermute(a, axes, way)
        for a, way in zip((behind, across, ahead), (ways(-1), ways(2), ways(1)))
    ]


def plain(step):
    return [(i, (i + step) % 4) for i in range(4)]


def shards(queries, comp_kv, prompt_kv, residual, out_weight, gain, lengths):
    x, y, group = lax.axis_index("tensor"), lax.axis_index("dp"), lax.axis_index("group")
    place = jnp.stack([x, y, group % 2, lengths[0, 0]]).astype(jnp.int32)
    query = queries[0, 0]
    swap = functools.partial(lax.ppermute, axis_name="group", perm=SWAP)

    with jax.named_scope("prompt"):
        piece = prompt_kv[0].transpose(1, 0, 2)[None]
        pair = jnp.concatenate([piece, swap(piece)], axis=0)

    weight = out_weight.T
    own = comp_kv[0, 0].transpose(1, 0, 2)
    with jax.named_scope("weights"):
        pieces = around("tensor", plain, weight, weight, weight)
        wide = widened([weight, *pieces])
        pieces = lax.ppermute(wide, ("dp", "tensor"), SLANT)
    with jax.named_scope("attention"):
        z1 = gated(lax.ppermute(pair, "group", along(1)), wide)
        z2 = lax.ppermute(z1, "group", along(1))
        *state, token = first_part(query, own, [pair, z1, swap(z1)])
        z2 = gated(z2, token)
    with jax.named_scope("weights"):
        columns = lax.all_gather(gated(pieces, z2), "group", axis=0, tiled=True)
    with jax.named_scope("attention"):
        z3 = lax.ppermute(z2, "group", along(1))
        *state, token = more_part(query, [z2, swap(z2)], state)
        z3 = gated(z3, token)
        z4 = lax.ppermute(z3[:1], "group", along(1))
        *state, token = more_part(query, [z3, swap(z3)], state)
        z4 = gated(z4, token)
        c0, c1, c2, c3 = last_part(place, query, [z4, swap(z4)], state)

    with jax.named_scope("exchange"):
        blocks = around("tensor", plain, c3, c2, c1)
        mixed = packed(place, c0, c1, c2, c3, *blocks)
        contexts = [mixed] + around(EVERY, ring, mixed, mixed, mixed)

    with jax.named_scope("project"):
        o0, o1, o2, o3 = projected(place, contexts, columns)
        parts = [o0] + around(EVERY, ring, o3, o2, o1)
    with jax.named_scope("finish"):
        attended, normed = finished(place, parts, residual[0, 0], gain[None])
    return (attended[None, None], normed[None, None])


def solution(mesh):
    in_specs = (
        P("dp", "group", None, "tensor"),
        P("dp", "group", None, None, "tensor"),
        P("dp", "group", None, "tensor"),
        P("dp", "group", "tensor", None),
        P("tensor", ("dp", "group")),
        P(),
        P("dp", "group"),
    )
    out_specs = (P("dp", "group", "tensor", None), P("dp", "group", "tensor", None))
    return jax.shard_map(shards, mesh=mesh, in_specs=in_specs, out_specs=out_specs, check_vma=False)
```

time: 271 us -> 130 us (0.48)
  waiting for transfers between devices: 193 us -> 43 us
  matrix products: 40.7 us -> 0 us
  Pallas kernels: 0 us -> 33.7 us
  starting transfers between devices: 0.12 us -> 30.4 us
  other arithmetic: 15.6 us -> 0.1 us
    psum x1 -> x0, waiting for transfers between devices: 111 us -> none  [shards(): summed = lax.psum(terms.astype(jnp.bfloat16), 'tensor').astype(jnp.float32)]
    all_gather x2 -> x1, waiting for transfers between devices: 81.4 us -> 0.01 us  [shards(): columns = lax.all_gather(gated(pieces, z2), 'group', axis=0, tiled=True)]
    ppermute x0 -> x22, waiting for transfers between devices: none -> 43 us  [the longest x12 40.6 us: around(): lax.ppermute(a, axes, way)]
    dot_general x11 -> x0, matrix products: 40.7 us -> none  [the longest x5 20.7 us: block_stats(): jnp.einsum('cgjh,lgh->gjcl', query_part, keys_part, preferred_element_typ...]
    pallas_call x0 -> x13, Pallas kernels: none -> 33.7 us  [the longest x1 8.59 us: first_part(): pl.pallas_call(functools.partial(attend_first, len(blocks)), in_specs=[VM...]
    ppermute x0 -> x22, starting transfers between devices: none -> 30.4 us  [the longest x12 15.3 us: around(): lax.ppermute(a, axes, way)]
    reduce_sum x6 -> x0, other arithmetic: 8.84 us -> none  [the longest x5 7.02 us: block_stats(): total = jnp.sum(weights, axis=-1, keepdims=True)]
    broadcast_in_dim x4 -> x0, other arithmetic: 5.34 us -> none  [the longest x2 5.33 us: shards(): return (attended[None, None], normed.astype(jnp.bfloat16)[None, None])]
  transfers between devices with their start and end apart: 3 -> 23, of which waited for: 3 -> 16; matrix products, arithmetic and copies ran while one was open for 17% -> 0% of each run, Pallas kernels for 0% -> 17%
where the time goes in v2:
time: 130 us; the launch traced here: 129 us
  waiting for transfers between devices  43 us (33%)
  Pallas kernels  33.7 us (26%)
  starting transfers between devices  30.4 us (23%)
  between operations  14.9 us (11%)
  local copies, waits for them, and re-layouts  7.4 us (6%)
    ppermute x12, waiting for transfers between devices, around(): lax.ppermute(a, axes, way)  40.6 us
    ppermute x12, starting transfers between devices, around(): lax.ppermute(a, axes, way)  15.3 us
    pallas_call x1, Pallas kernels, first_part(): pl.pallas_call(functools.partial(attend_first, len(blocks)), in_specs=[VM...  8.59 us
    pallas_call x1, Pallas kernels, projected(): pl.pallas_call(project, grid=(5,), in_specs=[SMEM] + [whole(c) for c in c...  8.41 us
    pallas_call x2, Pallas kernels, more_part(): pl.pallas_call(functools.partial(attend_more, len(blocks)), in_specs=[VME...  8.23 us
    unnamed x32, local copies, waits for them, and re-layouts  7.39 us
    pallas_call x1, Pallas kernels, last_part(): pl.pallas_call(functools.partial(attend_last, len(blocks)), in_specs=[SME...  4.14 us
    ppermute x1, starting transfers between devices, shards(): z1 = gated(lax.ppermute(pair, 'group', along(1)), wide)  3.92 us
  transfers between devices with their start and end apart: 23, of which 16 were waited for; matrix products, arithmetic and copies ran while one was open for 0% of the time, Pallas kernels for 17%

profile of v2, /device:TPU:1, one launch (start us, length us, event | category | flops | bytes accessed | tf_op | source)
XLA Modules:
  0.0 129.5 jit_solution(10588780349771165979)
XLA Ops:
  7.2 1.0 copy.14
  8.2 3.3 %collective-permute-start = (bf16[1,2,256,128]{3,2,1,0:T(8,128)(2,1)S(1)}, bf16[1,2,256,128]{3,2,1,0:T(8,128)(2,1)S(1)}, u32[]{:S(2)}, u32[]{:S(2)}) collective-permute-start(bf16[1,2,256,128]{3,2,1,0:T(8,128)(2,1)S(1)} %bitcast.34), channel_id=1, source_target_pairs={{0,4},{4,0},{8,12},{12,8},{16,20},{20,16},{24,28},{28,24},{32,36},... | collective-permute-start | bytes 393224 | tf_op jit(solution)/shard_map/prompt/ppermute | solution.py:347
  11.5 1.0 collective-permute-done
  12.6 3.9 %collective-permute-start.1 = (bf16[2,2,256,128]{3,2,1,0:T(8,128)(2,1)S(1)}, bf16[2,2,256,128]{3,2,1,0:T(8,128)(2,1)S(1)}, u32[]{:S(2)}, u32[]{:S(2)}) collective-permute-start(bf16[2,2,256,128]{3,2,1,0:T(8,128)(2,1)S(1)} %pad_maximum_fusion.refs_0_), channel_id=1, source_target_pairs={{0,8},{4,60},{8,16},{12,4},{16,24},{20,12},{24,32},{28,20},{32,40}... | collective-permute-start | bytes 786440 | tf_op jit(solution)/shard_map/attention/ppermute | solution.py:356
  16.5 2.5 %collective-permute-start.2 = (bf16[80,640]{1,0:T(8,128)(2,1)}, bf16[80,640]{1,0:T(8,128)(2,1)S(1)}, u32[]{:S(2)}, u32[]{:S(2)}) collective-permute-start(bf16[80,640]{1,0:T(8,128)(2,1)} %bitcast.25), channel_id=1, source_target_pairs={{0,3},{1,0},{2,1},{3,2},{4,7},{5,4},{6,5},{7,6},{8,11},{9,8},{10,9... | collective-permute-start | bytes 307208 | tf_op jit(solution)/shard_map/weights/ppermute | solution.py:330
  20.1 2.0 %collective-permute-done.2.b1 = bf16[80,640]{1,0:T(8,128)(2,1)S(1)} collective-permute-done((bf16[80,640]{1,0:T(8,128)(2,1)}, bf16[80,640]{1,0:T(8,128)(2,1)S(1)}, u32[]{:S(2)}, u32[]{:S(2)}) %collective-permute-start.2) | collective-permute-done | bytes 102432 | tf_op jit(solution)/shard_map/weights/ppermute | solution.py:330
  22.1 2.2 %collective-permute-done.3.b2 = bf16[80,640]{1,0:T(8,128)(2,1)S(1)} collective-permute-done((bf16[80,640]{1,0:T(8,128)(2,1)}, bf16[80,640]{1,0:T(8,128)(2,1)S(1)}, u32[]{:S(2)}, u32[]{:S(2)}) %collective-permute-start.3) | collective-permute-done | bytes 102432 | tf_op jit(solution)/shard_map/weights/ppermute | solution.py:330
  24.3 1.0 collective-permute-done.4.b3
  27.9 3.4 %collective-permute-start.5 = (bf16[2,2,256,128]{3,2,1,0:T(8,128)(2,1)S(1)}, bf16[2,2,256,128]{3,2,1,0:T(8,128)(2,1)S(1)}, u32[]{:S(2)}, u32[]{:S(2)}) collective-permute-start(bf16[2,2,256,128]{3,2,1,0:T(8,128)(2,1)S(1)} %attention.8.refs_1_), channel_id=1, source_target_pairs={{0,8},{4,60},{8,16},{12,4},{16,24},{20,12},{24,32},{28,20},{32,40}... | collective-permute-start | bytes 786440 | tf_op jit(solution)/shard_map/attention/ppermute | solution.py:357
  31.3 8.6 %attention.9 = (f32[5,512,128]{2,1,0:T(8,128)}, f32[5,512,128]{2,1,0:T(8,128)}, f32[8,128]{1,0:T(8,128)S(1)}) custom-call(bf16[512,640]{1,0:T(8,128)(2,1)S(1)} %bitcast.30, bf16[2,512,128]{2,1,0:T(8,128)(2,1)S(1)} %bitcast.24, bf16[2,2,256,128]{3,2,1,0:T(8,128)(2,1)S(1)} %pad_maximum_fusion.refs_0_, bf16[2,2,256,128]{3,2,1,0:T(8,128)(2,1)S(1)} %attention.8.refs_1_, ...), custom_call_target="tpu_custom_call" | custom-call | flops 16106127360 | bytes 12582912 | tf_op jit(solution)/shard_map/attention/pallas_call | solution.py:142
  42.4 1.3 %copy-done.11 = f32[5,512,128]{2,1,0:T(8,128)S(1)} copy-done((f32[5,512,128]{2,1,0:T(8,128)S(1)}, f32[5,512,128]{2,1,0:T(8,128)}, u32[]{:S(2)}) %copy-start.11) | copy-done | bytes 1310744
  43.7 4.0 %attention.11 = (f32[5,512,128]{2,1,0:T(8,128)S(1)}, f32[5,512,128]{2,1,0:T(8,128)S(1)}, f32[8,128]{1,0:T(8,128)S(1)}) custom-call(bf16[512,640]{1,0:T(8,128)(2,1)S(1)} %bitcast.31, bf16[2,2,256,128]{3,2,1,0:T(8,128)(2,1)S(1)} %attention.10.refs_0_, bf16[2,2,256,128]{3,2,1,0:T(8,128)(2,1)S(1)} %collective-permute-done.8.refs_1_, ...), custom_call_target="tpu_custom_call" | custom-call | flops 8053063680 | bytes 12582912 | tf_op jit(solution)/shard_map/attention/pallas_call | solution.py:154
  47.8 1.3 collective-permute-start.10
  50.2 4.2 %attention.13 = (f32[5,512,128]{2,1,0:T(8,128)S(1)}, f32[5,512,128]{2,1,0:T(8,128)S(1)}, f32[8,128]{1,0:T(8,128)S(1)}) custom-call(bf16[512,640]{1,0:T(8,128)(2,1)S(1)} %bitcast.32, bf16[2,2,256,128]{3,2,1,0:T(8,128)(2,1)S(1)} %attention.12.refs_0_, bf16[2,2,256,128]{3,2,1,0:T(8,128)(2,1)S(1)} %collective-permute-done.10.refs_1_, ...), custom_call_target="tpu_custom_call" | custom-call | flops 8053063680 | bytes 12582912 | tf_op jit(solution)/shard_map/attention/pallas_call | solution.py:154
  54.4 1.0 copy-done.8
  57.2 1.3 %copy-done.9 = f32[5,512,128]{2,1,0:T(8,128)S(1)} copy-done((f32[5,512,128]{2,1,0:T(8,128)S(1)}, f32[5,512,128]{2,1,0:T(8,128)}, u32[]{:S(2)}) %copy-start.9) | copy-done | bytes 1310744
  58.5 4.1 %attention.15 = (bf16[128,640]{1,0:T(8,128)(2,1)S(1)}, bf16[128,640]{1,0:T(8,128)(2,1)S(1)}, bf16[128,640]{1,0:T(8,128)(2,1)S(1)}, bf16[128,640]{1,0:T(8,128)(2,1)S(1)}) custom-call(s32[4]{0:T(128)S(1)} %pad_add_fusion.place, bf16[512,640]{1,0:T(8,128)(2,1)S(1)} %bitcast.33, bf16[1,2,256,128]{3,2,1,0:T(8,128)(2,1)S(1)} %attention.14.refs_0_, ...), custom_call_target="tpu_custom_call" | custom-call | flops 8053063680 | bytes 12582912 | tf_op jit(solution)/shard_map/attention/pallas_call | solution.py:166
  62.6 3.3 %collective-permute-start.12 = (bf16[128,640]{1,0:T(8,128)(2,1)S(1)}, bf16[128,640]{1,0:T(8,128)(2,1)S(1)}, u32[]{:S(2)}, u32[]{:S(2)}) collective-permute-start(bf16[128,640]{1,0:T(8,128)(2,1)S(1)} %get-tuple-element.33.refs_3_), channel_id=1, source_target_pairs={{0,3},{1,0},{2,1},{3,2},{4,7},{5,4},{6,5},{7,6},{8,11},{9,8},{10,9... | collective-permute-start | bytes 491528 | tf_op jit(solution)/shard_map/exchange/ppermute | solution.py:330
  66.0 3.8 %collective-permute-start.13 = (bf16[128,640]{1,0:T(8,128)(2,1)S(1)}, bf16[128,640]{1,0:T(8,128)(2,1)S(1)}, u32[]{:S(2)}, u32[]{:S(2)}) collective-permute-start(bf16[128,640]{1,0:T(8,128)(2,1)S(1)} %get-tuple-element.32.refs_2_), channel_id=1, source_target_pairs={{0,2},{1,3},{2,0},{3,1},{4,6},{5,7},{6,4},{7,5},{8,10},{9,11},{10,... | collective-permute-start | bytes 491528 | tf_op jit(solution)/shard_map/exchange/ppermute | solution.py:330
  71.2 2.9 %collective-permute-done.13.refs_5_ = bf16[128,640]{1,0:T(8,128)(2,1)S(1)} collective-permute-done((bf16[128,640]{1,0:T(8,128)(2,1)S(1)}, bf16[128,640]{1,0:T(8,128)(2,1)S(1)}, u32[]{:S(2)}, u32[]{:S(2)}) %collective-permute-start.13) | collective-permute-done | bytes 163872 | tf_op jit(solution)/shard_map/exchange/ppermute | solution.py:330
  74.1 3.7 %collective-permute-done.14.refs_6_ = bf16[128,640]{1,0:T(8,128)(2,1)S(1)} collective-permute-done((bf16[128,640]{1,0:T(8,128)(2,1)S(1)}, bf16[128,640]{1,0:T(8,128)(2,1)S(1)}, u32[]{:S(2)}, u32[]{:S(2)}) %collective-permute-start.14) | collective-permute-done | bytes 163872 | tf_op jit(solution)/shard_map/exchange/ppermute | solution.py:330
  78.5 1.4 %collective-permute-start.15 = (bf16[4,128,640]{2,1,0:T(8,128)(2,1)S(1)}, bf16[4,128,640]{2,1,0:T(8,128)(2,1)S(1)}, u32[]{:S(2)}, u32[]{:S(2)}) collective-permute-start(bf16[4,128,640]{2,1,0:T(8,128)(2,1)S(1)} %exchange.1.c0), channel_id=1, source_target_pairs={{0,3},{1,0},{2,1},{3,2},{4,196},{5,197},{6,198},{7,199},{8,11},{9,... | collective-permute-start | bytes 1966088 | tf_op jit(solution)/shard_map/exchange/ppermute | solution.py:330
  80.7 7.7 %collective-permute-done.15.c1 = bf16[4,128,640]{2,1,0:T(8,128)(2,1)S(1)} collective-permute-done((bf16[4,128,640]{2,1,0:T(8,128)(2,1)S(1)}, bf16[4,128,640]{2,1,0:T(8,128)(2,1)S(1)}, u32[]{:S(2)}, u32[]{:S(2)}) %collective-permute-start.15) | collective-permute-done | bytes 655392 | tf_op jit(solution)/shard_map/exchange/ppermute | solution.py:330
  88.4 2.8 %collective-permute-done.16.c2 = bf16[4,128,640]{2,1,0:T(8,128)(2,1)S(1)} collective-permute-done((bf16[4,128,640]{2,1,0:T(8,128)(2,1)S(1)}, bf16[4,128,640]{2,1,0:T(8,128)(2,1)S(1)}, u32[]{:S(2)}, u32[]{:S(2)}) %collective-permute-start.16) | collective-permute-done | bytes 655392 | tf_op jit(solution)/shard_map/exchange/ppermute | solution.py:330
  91.2 6.9 %collective-permute-done.17.c3 = bf16[4,128,640]{2,1,0:T(8,128)(2,1)} collective-permute-done((bf16[4,128,640]{2,1,0:T(8,128)(2,1)S(1)}, bf16[4,128,640]{2,1,0:T(8,128)(2,1)}, u32[]{:S(2)}, u32[]{:S(2)}) %collective-permute-start.17) | collective-permute-done | bytes 655392 | tf_op jit(solution)/shard_map/exchange/ppermute | solution.py:330
  98.1 8.4 %project.1 = (bf16[128,1280]{1,0:T(8,128)(2,1)}, bf16[128,1280]{1,0:T(8,128)(2,1)}, bf16[128,1280]{1,0:T(8,128)(2,1)}, bf16[128,1280]{1,0:T(8,128)(2,1)}) custom-call(s32[4]{0:T(128)} %copy-done.5, bf16[4,128,640]{2,1,0:T(8,128)(2,1)} %copy-done.1, bf16[4,128,640]{2,1,0:T(8,128)(2,1)} %copy-done.13, bf16[4,128,640]{2,1,0:T(8,128)(2,1)} %copy-done.14, ...), custom_call_target="tpu_custom_call" | custom-call | flops 3355443200 | bytes 10485760 | tf_op jit(solution)/shard_map/project/pallas_call | solution.py:260
  106.5 0.9 collective-permute-start.19
  108.1 4.8 %collective-permute-done.19.p1 = bf16[128,1280]{1,0:T(8,128)(2,1)S(1)} collective-permute-done((bf16[128,1280]{1,0:T(8,128)(2,1)}, bf16[128,1280]{1,0:T(8,128)(2,1)S(1)}, u32[]{:S(2)}, u32[]{:S(2)}) %collective-permute-start.19) | collective-permute-done | bytes 327712 | tf_op jit(solution)/shard_map/project/ppermute | solution.py:330
  112.9 2.5 %collective-permute-done.20.p2 = bf16[128,1280]{1,0:T(8,128)(2,1)S(1)} collective-permute-done((bf16[128,1280]{1,0:T(8,128)(2,1)}, bf16[128,1280]{1,0:T(8,128)(2,1)S(1)}, u32[]{:S(2)}, u32[]{:S(2)}) %collective-permute-start.20) | collective-permute-done | bytes 327712 | tf_op jit(solution)/shard_map/project/ppermute | solution.py:330
  115.4 3.4 %collective-permute-done.21.p3 = bf16[128,1280]{1,0:T(8,128)(2,1)S(1)} collective-permute-done((bf16[128,1280]{1,0:T(8,128)(2,1)}, bf16[128,1280]{1,0:T(8,128)(2,1)S(1)}, u32[]{:S(2)}, u32[]{:S(2)}) %collective-permute-start.21) | collective-permute-done | bytes 327712 | tf_op jit(solution)/shard_map/project/ppermute | solution.py:330
  118.9 1.0 copy-done.2
  119.8 2.8 %finish.1 = (bf16[128,5120]{1,0:T(8,128)(2,1)}, bf16[128,5120]{1,0:T(8,128)(2,1)}) custom-call(s32[4]{0:T(128)S(1)} %copy-done.6, bf16[128,1280]{1,0:T(8,128)(2,1)S(1)} %copy-done.2, bf16[128,1280]{1,0:T(8,128)(2,1)S(1)} %collective-permute-done.19.p1, bf16[128,1280]{1,0:T(8,128)(2,1)S(1)} %collective-permute-done.20.p2, ...), custom_call_target="tpu_custom_call" | custom-call | tf_op jit(solution)/shard_map/finish/pallas_call | solution.py:291
  (63 shorter events, 12.0 us)
Async XLA Ops:
  7.2 90.9 %all-gather.2.cloned.1.call-start = ((), (), s32[]{:S(2)}) async-start(), calls=%async_computation | async-start | bytes 6963200 | tf_op jit(solution)/shard_map/weights/all_gather | solution.py:361
  7.2 24.1 %copy-start.7 = (bf16[1,1,512,640]{3,2,1,0:T(8,128)(2,1)S(1)}, bf16[1,1,512,640]{3,2,1,0:T(8,128)(2,1)}, u32[]{:S(2)}) copy-start(bf16[1,1,512,640]{3,2,1,0:T(8,128)(2,1)} %param.7) | copy-start | bytes 1966084
  8.2 4.3 %collective-permute-start = (bf16[1,2,256,128]{3,2,1,0:T(8,128)(2,1)S(1)}, bf16[1,2,256,128]{3,2,1,0:T(8,128)(2,1)S(1)}, u32[]{:S(2)}, u32[]{:S(2)}) collective-permute-start(bf16[1,2,256,128]{3,2,1,0:T(8,128)(2,1)S(1)} %bitcast.34), channel_id=1, source_target_pairs={{0,4},{4,0},{8,12},{12,8},{16,20},{20,16},{24,28},{28,24},{32,36},... | collective-permute-start | bytes 393224 | tf_op jit(solution)/shard_map/prompt/ppermute | solution.py:347
  12.6 13.7 %collective-permute-start.1 = (bf16[2,2,256,128]{3,2,1,0:T(8,128)(2,1)S(1)}, bf16[2,2,256,128]{3,2,1,0:T(8,128)(2,1)S(1)}, u32[]{:S(2)}, u32[]{:S(2)}) collective-permute-start(bf16[2,2,256,128]{3,2,1,0:T(8,128)(2,1)S(1)} %pad_maximum_fusion.refs_0_), channel_id=1, source_target_pairs={{0,8},{4,60},{8,16},{12,4},{16,24},{20,12},{24,32},{28,20},{32,40}... | collective-permute-start | bytes 786440 | tf_op jit(solution)/shard_map/attention/ppermute | solution.py:356
  16.5 5.6 %collective-permute-start.2 = (bf16[80,640]{1,0:T(8,128)(2,1)}, bf16[80,640]{1,0:T(8,128)(2,1)S(1)}, u32[]{:S(2)}, u32[]{:S(2)}) collective-permute-start(bf16[80,640]{1,0:T(8,128)(2,1)} %bitcast.25), channel_id=1, source_target_pairs={{0,3},{1,0},{2,1},{3,2},{4,7},{5,4},{6,5},{7,6},{8,11},{9,8},{10,9... | collective-permute-start | bytes 307208 | tf_op jit(solution)/shard_map/weights/ppermute | solution.py:330
  18.9 5.3 %collective-permute-start.3 = (bf16[80,640]{1,0:T(8,128)(2,1)}, bf16[80,640]{1,0:T(8,128)(2,1)S(1)}, u32[]{:S(2)}, u32[]{:S(2)}) collective-permute-start(bf16[80,640]{1,0:T(8,128)(2,1)} %bitcast.26), channel_id=1, source_target_pairs={{0,2},{1,3},{2,0},{3,1},{4,6},{5,7},{6,4},{7,5},{8,10},{9,11},{10,... | collective-permute-start | bytes 307208 | tf_op jit(solution)/shard_map/weights/ppermute | solution.py:330
  19.5 5.8 %collective-permute-start.4 = (bf16[80,640]{1,0:T(8,128)(2,1)}, bf16[80,640]{1,0:T(8,128)(2,1)S(1)}, u32[]{:S(2)}, u32[]{:S(2)}) collective-permute-start(bf16[80,640]{1,0:T(8,128)(2,1)} %bitcast.27), channel_id=1, source_target_pairs={{0,1},{1,2},{2,3},{3,0},{4,5},{5,6},{6,7},{7,4},{8,9},{9,10},{10,1... | collective-permute-start | bytes 307208 | tf_op jit(solution)/shard_map/weights/ppermute | solution.py:330
  26.2 5.0 %collective-permute-start.6 = (bf16[2,2,256,128]{3,2,1,0:T(8,128)(2,1)S(1)}, bf16[2,2,256,128]{3,2,1,0:T(8,128)(2,1)S(1)}, u32[]{:S(2)}, u32[]{:S(2)}) collective-permute-start(bf16[2,2,256,128]{3,2,1,0:T(8,128)(2,1)S(1)} %attention.8.refs_1_), channel_id=1, source_target_pairs={{0,4},{4,0},{8,12},{12,8},{16,20},{20,16},{24,28},{28,24},{32,36},... | collective-permute-start | bytes 786440 | tf_op jit(solution)/shard_map/attention/ppermute | solution.py:358
  27.2 12.7 %collective-permute-start.18 = (bf16[80,2560]{1,0:T(8,128)(2,1)S(1)}, bf16[80,2560]{1,0:T(8,128)(2,1)S(1)}, u32[]{:S(2)}, u32[]{:S(2)}) collective-permute-start(bf16[80,2560]{1,0:T(8,128)(2,1)S(1)} %weights.2.refs_0_), channel_id=1, source_target_pairs={{0,0},{1,193},{2,130},{3,67},{64,64},{65,1},{66,194},{67,131},{128... | collective-permute-start | bytes 1228808 | tf_op jit(solution)/shard_map/weights/ppermute | solution.py:354
  27.9 12.0 %collective-permute-start.5 = (bf16[2,2,256,128]{3,2,1,0:T(8,128)(2,1)S(1)}, bf16[2,2,256,128]{3,2,1,0:T(8,128)(2,1)S(1)}, u32[]{:S(2)}, u32[]{:S(2)}) collective-permute-start(bf16[2,2,256,128]{3,2,1,0:T(8,128)(2,1)S(1)} %attention.8.refs_1_), channel_id=1, source_target_pairs={{0,8},{4,60},{8,16},{12,4},{16,24},{20,12},{24,32},{28,20},{32,40}... | collective-permute-start | bytes 786440 | tf_op jit(solution)/shard_map/attention/ppermute | solution.py:357
  39.9 2.5 %copy-start.10 = (f32[5,512,128]{2,1,0:T(8,128)S(1)}, f32[5,512,128]{2,1,0:T(8,128)}, u32[]{:S(2)}) copy-start(f32[5,512,128]{2,1,0:T(8,128)} %get-tuple-element.22.refs_2_) | copy-start | bytes 3932164
  40.7 1.6 %collective-permute-start.8 = (bf16[2,2,256,128]{3,2,1,0:T(8,128)(2,1)S(1)}, bf16[2,2,256,128]{3,2,1,0:T(8,128)(2,1)S(1)}, u32[]{:S(2)}, u32[]{:S(2)}) collective-permute-start(bf16[2,2,256,128]{3,2,1,0:T(8,128)(2,1)S(1)} %attention.10.refs_0_), channel_id=1, source_target_pairs={{0,4},{4,0},{8,12},{12,8},{16,20},{20,16},{24,28},{28,24},{32,36},... | collective-permute-start | bytes 786440 | tf_op jit(solution)/shard_map/attention/ppermute | solution.py:364
  40.8 6.9 %collective-permute-start.7 = (bf16[2,2,256,128]{3,2,1,0:T(8,128)(2,1)S(1)}, bf16[2,2,256,128]{3,2,1,0:T(8,128)(2,1)S(1)}, u32[]{:S(2)}, u32[]{:S(2)}) collective-permute-start(bf16[2,2,256,128]{3,2,1,0:T(8,128)(2,1)S(1)} %attention.10.refs_0_), channel_id=1, source_target_pairs={{0,8},{4,60},{8,16},{12,4},{16,24},{20,12},{24,32},{28,20},{32,40}... | collective-permute-start | bytes 786440 | tf_op jit(solution)/shard_map/attention/ppermute | solution.py:363
  47.8 2.4 %collective-permute-start.10 = (bf16[2,2,256,128]{3,2,1,0:T(8,128)(2,1)S(1)}, bf16[2,2,256,128]{3,2,1,0:T(8,128)(2,1)S(1)}, u32[]{:S(2)}, u32[]{:S(2)}) collective-permute-start(bf16[2,2,256,128]{3,2,1,0:T(8,128)(2,1)S(1)} %attention.12.refs_0_), channel_id=1, source_target_pairs={{0,4},{4,0},{8,12},{12,8},{16,20},{20,16},{24,28},{28,24},{32,36},... | collective-permute-start | bytes 786440 | tf_op jit(solution)/shard_map/attention/ppermute | solution.py:367
  49.0 6.4 %collective-permute-start.9 = (bf16[1,2,256,128]{3,2,1,0:T(8,128)(2,1)S(1)}, bf16[1,2,256,128]{3,2,1,0:T(8,128)(2,1)S(1)}, u32[]{:S(2)}, u32[]{:S(2)}) collective-permute-start(bf16[1,2,256,128]{3,2,1,0:T(8,128)(2,1)S(1)} %slice.4), channel_id=1, source_target_pairs={{0,8},{4,60},{8,16},{12,4},{16,24},{20,12},{24,32},{28,20},{32,40}... | collective-permute-start | bytes 393224 | tf_op jit(solution)/shard_map/attention/ppermute | solution.py:366
  55.4 1.7 %collective-permute-start.11 = (bf16[1,2,256,128]{3,2,1,0:T(8,128)(2,1)S(1)}, bf16[1,2,256,128]{3,2,1,0:T(8,128)(2,1)S(1)}, u32[]{:S(2)}, u32[]{:S(2)}) collective-permute-start(bf16[1,2,256,128]{3,2,1,0:T(8,128)(2,1)S(1)} %attention.14.refs_0_), channel_id=1, source_target_pairs={{0,4},{4,0},{8,12},{12,8},{16,20},{20,16},{24,28},{28,24},{32,36},... | collective-permute-start | bytes 393224 | tf_op jit(solution)/shard_map/attention/ppermute | solution.py:369
  56.9 20.9 %copy-start.5 = (s32[4]{0:T(128)}, s32[4]{0:T(128)S(1)}, u32[]{:S(2)}) copy-start(s32[4]{0:T(128)S(1)} %pad_add_fusion.place) | copy-start | bytes 52
  62.6 8.6 %collective-permute-start.12 = (bf16[128,640]{1,0:T(8,128)(2,1)S(1)}, bf16[128,640]{1,0:T(8,128)(2,1)S(1)}, u32[]{:S(2)}, u32[]{:S(2)}) collective-permute-start(bf16[128,640]{1,0:T(8,128)(2,1)S(1)} %get-tuple-element.33.refs_3_), channel_id=1, source_target_pairs={{0,3},{1,0},{2,1},{3,2},{4,7},{5,4},{6,5},{7,6},{8,11},{9,8},{10,9... | collective-permute-start | bytes 491528 | tf_op jit(solution)/shard_map/exchange/ppermute | solution.py:330
  66.0 8.1 %collective-permute-start.13 = (bf16[128,640]{1,0:T(8,128)(2,1)S(1)}, bf16[128,640]{1,0:T(8,128)(2,1)S(1)}, u32[]{:S(2)}, u32[]{:S(2)}) collective-permute-start(bf16[128,640]{1,0:T(8,128)(2,1)S(1)} %get-tuple-element.32.refs_2_), channel_id=1, source_target_pairs={{0,2},{1,3},{2,0},{3,1},{4,6},{5,7},{6,4},{7,5},{8,10},{9,11},{10,... | collective-permute-start | bytes 491528 | tf_op jit(solution)/shard_map/exchange/ppermute | solution.py:330
  69.8 8.0 %collective-permute-start.14 = (bf16[128,640]{1,0:T(8,128)(2,1)S(1)}, bf16[128,640]{1,0:T(8,128)(2,1)S(1)}, u32[]{:S(2)}, u32[]{:S(2)}) collective-permute-start(bf16[128,640]{1,0:T(8,128)(2,1)S(1)} %get-tuple-element.31.refs_1_), channel_id=1, source_target_pairs={{0,1},{1,2},{2,3},{3,0},{4,5},{5,6},{6,7},{7,4},{8,9},{9,10},{10,1... | collective-permute-start | bytes 491528 | tf_op jit(solution)/shard_map/exchange/ppermute | solution.py:330
  78.5 19.6 %copy-start.1 = (bf16[4,128,640]{2,1,0:T(8,128)(2,1)}, bf16[4,128,640]{2,1,0:T(8,128)(2,1)S(1)}, u32[]{:S(2)}) copy-start(bf16[4,128,640]{2,1,0:T(8,128)(2,1)S(1)} %exchange.1.c0) | copy-start | bytes 1966084
  78.5 40.4 %copy-start = (bf16[1,1,128,5120]{3,2,1,0:T(8,128)(2,1)S(1)}, bf16[1,1,128,5120]{3,2,1,0:T(8,128)(2,1)}, u32[]{:S(2)}) copy-start(bf16[1,1,128,5120]{3,2,1,0:T(8,128)(2,1)} %param.10) | copy-start | bytes 3932164
  78.5 40.4 %copy-start.4 = (f32[5120]{0:T(1024)S(1)}, f32[5120]{0:T(1024)}, u32[]{:S(2)}) copy-start(f32[5120]{0:T(1024)} %param.12) | copy-start | bytes 61444
  78.5 40.4 %copy-start.6 = (s32[4]{0:T(128)S(1)}, s32[4]{0:T(128)}, u32[]{:S(2)}) copy-start(s32[4]{0:T(128)} %copy-done.5) | copy-start | bytes 52
  78.5 9.9 %collective-permute-start.15 = (bf16[4,128,640]{2,1,0:T(8,128)(2,1)S(1)}, bf16[4,128,640]{2,1,0:T(8,128)(2,1)S(1)}, u32[]{:S(2)}, u32[]{:S(2)}) collective-permute-start(bf16[4,128,640]{2,1,0:T(8,128)(2,1)S(1)} %exchange.1.c0), channel_id=1, source_target_pairs={{0,3},{1,0},{2,1},{3,2},{4,196},{5,197},{6,198},{7,199},{8,11},{9,... | collective-permute-start | bytes 1966088 | tf_op jit(solution)/shard_map/exchange/ppermute | solution.py:330
  79.9 11.3 %collective-permute-start.16 = (bf16[4,128,640]{2,1,0:T(8,128)(2,1)S(1)}, bf16[4,128,640]{2,1,0:T(8,128)(2,1)S(1)}, u32[]{:S(2)}, u32[]{:S(2)}) collective-permute-start(bf16[4,128,640]{2,1,0:T(8,128)(2,1)S(1)} %exchange.1.c0), channel_id=1, source_target_pairs={{0,2},{1,3},{2,0},{3,1},{4,132},{5,133},{6,134},{7,135},{8,10},{9,... | collective-permute-start | bytes 1966088 | tf_op jit(solution)/shard_map/exchange/ppermute | solution.py:330
  80.0 18.1 %collective-permute-start.17 = (bf16[4,128,640]{2,1,0:T(8,128)(2,1)S(1)}, bf16[4,128,640]{2,1,0:T(8,128)(2,1)}, u32[]{:S(2)}, u32[]{:S(2)}) collective-permute-start(bf16[4,128,640]{2,1,0:T(8,128)(2,1)S(1)} %exchange.1.c0), channel_id=1, source_target_pairs={{0,1},{1,2},{2,3},{3,0},{4,68},{5,69},{6,70},{7,71},{8,9},{9,10},{... | collective-permute-start | bytes 1966088 | tf_op jit(solution)/shard_map/exchange/ppermute | solution.py:330
  88.4 9.7 %copy-start.13 = (bf16[4,128,640]{2,1,0:T(8,128)(2,1)}, bf16[4,128,640]{2,1,0:T(8,128)(2,1)S(1)}, u32[]{:S(2)}) copy-start(bf16[4,128,640]{2,1,0:T(8,128)(2,1)S(1)} %collective-permute-done.15.c1) | copy-start | bytes 1966084
  91.2 6.9 %copy-start.14 = (bf16[4,128,640]{2,1,0:T(8,128)(2,1)}, bf16[4,128,640]{2,1,0:T(8,128)(2,1)S(1)}, u32[]{:S(2)}) copy-start(bf16[4,128,640]{2,1,0:T(8,128)(2,1)S(1)} %collective-permute-done.16.c2) | copy-start | bytes 1966084
  106.5 6.4 %collective-permute-start.19 = (bf16[128,1280]{1,0:T(8,128)(2,1)}, bf16[128,1280]{1,0:T(8,128)(2,1)S(1)}, u32[]{:S(2)}, u32[]{:S(2)}) collective-permute-start(bf16[128,1280]{1,0:T(8,128)(2,1)} %get-tuple-element.35), channel_id=1, source_target_pairs={{0,3},{1,0},{2,1},{3,2},{4,196},{5,197},{6,198},{7,199},{8,11},{9,... | collective-permute-start | bytes 983048 | tf_op jit(solution)/shard_map/project/ppermute | solution.py:330
  107.4 8.0 %collective-permute-start.20 = (bf16[128,1280]{1,0:T(8,128)(2,1)}, bf16[128,1280]{1,0:T(8,128)(2,1)S(1)}, u32[]{:S(2)}, u32[]{:S(2)}) collective-permute-start(bf16[128,1280]{1,0:T(8,128)(2,1)} %get-tuple-element.36), channel_id=1, source_target_pairs={{0,2},{1,3},{2,0},{3,1},{4,132},{5,133},{6,134},{7,135},{8,10},{9,... | collective-permute-start | bytes 983048 | tf_op jit(solution)/shard_map/project/ppermute | solution.py:330
  107.5 11.4 %collective-permute-start.21 = (bf16[128,1280]{1,0:T(8,128)(2,1)}, bf16[128,1280]{1,0:T(8,128)(2,1)S(1)}, u32[]{:S(2)}, u32[]{:S(2)}) collective-permute-start(bf16[128,1280]{1,0:T(8,128)(2,1)} %get-tuple-element.37), channel_id=1, source_target_pairs={{0,1},{1,2},{2,3},{3,0},{4,68},{5,69},{6,70},{7,71},{8,9},{9,10},{... | collective-permute-start | bytes 983048 | tf_op jit(solution)/shard_map/project/ppermute | solution.py:330
  (6 other events, 6.5 us)
Sparse Core Ops, SparseCore 0:
  40.8 47.1 all-gather.1

commit v3 on v2

--- a/solution.py
+++ b/solution.py
@@ -71,22 +71,16 @@
     for h in range(GROUPS):
         for r in range(0, CLEN, TILE):
             lines = head(query, r, h)
-            best, mixed = absorb(lines, keys[:1024], values[:1024], None, None)
-            extent = prompt + r + TILE - 1024
+            extent = prompt + r + TILE
             column = lax.broadcasted_iota(jnp.int32, (TILE, extent), 1)
             row = lax.broadcasted_iota(jnp.int32, (TILE, extent), 0)
             best, mixed = absorb(
-                lines,
-                keys[1024 : 1024 + extent],
-                values[1024 : 1024 + extent],
-                best,
-                mixed,
-                column - row <= extent - TILE,
+                lines, keys[:extent], values[:extent], None, None, column - row <= extent - TILE
             )
             top_out[h, r : r + TILE], mixed_out[h, r : r + TILE] = store_state(best, mixed)
 
 
-def attend_more(count, query, *refs):
+def attend_more(count, width, query, *refs):
     blocks, (top_in, mixed_in, top_out, mixed_out, token, keys, values) = (
         refs[:count],
         refs[count:],
@@ -98,7 +92,10 @@
     for h in range(GROUPS):
         for r in range(0, CLEN, TILE):
             best, mixed = load_state(top_in[h, r : r + TILE], mixed_in[h, r : r + TILE])
-            best, mixed = absorb(head(query, r, h), keys[...], values[...], best, mixed)
+            for at in range(0, keys.shape[0], width):
+                best, mixed = absorb(
+                    head(query, r, h), keys[at : at + width], values[at : at + width], best, mixed
+                )
             top_out[h, r : r + TILE], mixed_out[h, r : r + TILE] = store_state(best, mixed)
 
 
@@ -112,13 +109,13 @@
     values[:, HD:] = jnp.ones((values.shape[0], HD), BF16)
 
     for h in range(GROUPS):
-        best, mixed = load_state(top_in[h], mixed_in[h])
-        lines = query[:, h * HD : (h + 1) * HD]
-        best, mixed = absorb(lines, keys[...], values[...], best, mixed)
-        line = lax.broadcasted_iota(jnp.int32, (CLEN, HD), 0)
-        context[:, h * HD : (h + 1) * HD] = jnp.where(
-            line < live, mixed[:, :HD] / mixed[:, HD:], 0.0
-        ).astype(BF16)
+        for r in range(0, CLEN, TILE):
+            best, mixed = load_state(top_in[h, r : r + TILE], mixed_in[h, r : r + TILE])
+            best, mixed = absorb(head(query, r, h), keys[...], values[...], best, mixed)
+            line = lax.broadcasted_iota(jnp.int32, (TILE, HD), 0) + r
+            context[r : r + TILE, h * HD : (h + 1) * HD] = jnp.where(
+                line < live, mixed[:, :HD] / mixed[:, HD:], 0.0
+            ).astype(BF16)
     for d, out in enumerate((o0, o1, o2, o3)):
         out[...] = context[pl.ds(pl.multiple_of(lax.rem(x + d, 4) * 128, 128), 128)]
 
@@ -143,19 +140,19 @@
         functools.partial(attend_first, len(blocks)),
         in_specs=[VMEM] * (2 + len(blocks)),
         out_specs=[VMEM] * 3,
-        out_shape=[pltpu.HBM(s.shape, s.dtype) for s in STATE] + [TOKEN],
+        out_shape=STATE + [TOKEN],
         scratch_shapes=room(blocks, CLEN),
         compiler_params=PARAMS,
         cost_estimate=cost(GROUPS * CLEN, 2048),
     )(query, own, *blocks)
 
 
-def more_part(query, blocks, state):
-    return pl.pallas_call(
-        functools.partial(attend_more, len(blocks)),
+def more_part(query, blocks, state, width, leave=False):
+    return pl.pallas_call(
+        functools.partial(attend_more, len(blocks), width),
         in_specs=[VMEM] * (3 + len(blocks)),
         out_specs=[VMEM] * 3,
-        out_shape=STATE + [TOKEN],
+        out_shape=([pltpu.HBM(s.shape, s.dtype) for s in STATE] if leave else STATE) + [TOKEN],
         scratch_shapes=room(blocks),
         compiler_params=PARAMS,
         cost_estimate=cost(GROUPS * CLEN, 1024),
@@ -266,7 +263,7 @@
         out_specs=[pl.BlockSpec((rows, 256), lambda n: (0, n))] * 4,
         out_shape=[block] * 4,
         scratch_shapes=[pltpu.VMEM((4 * rows, 2560), BF16)],
-        compiler_params=pltpu.CompilerParams(vmem_limit_bytes=60 << 20),
+        compiler_params=pltpu.CompilerParams(vmem_limit_bytes=24 << 20),
         cost_estimate=pl.CostEstimate(
             flops=2 * 4 * rows * 2560 * 1280, bytes_accessed=10 << 20, transcendentals=0
         ),
@@ -336,6 +333,10 @@
     return [(i, (i + step) % 4) for i in range(4)]
 
 
+def kept(state):
+    return [pltpu.with_memory_space_constraint(a, pltpu.HBM) for a in state]
+
+
 def shards(queries, comp_kv, prompt_kv, residual, out_weight, gain, lengths):
     x, y, group = lax.axis_index("tensor"), lax.axis_index("dp"), lax.axis_index("group")
     place = jnp.stack([x, y, group % 2, lengths[0, 0]]).astype(jnp.int32)
@@ -350,23 +351,28 @@
     own = comp_kv[0, 0].transpose(1, 0, 2)
     with jax.named_scope("weights"):
         pieces = around("tensor", plain, weight, weight, weight)
-        wide = widened([weight, *pieces])
+    with jax.named_scope("attention"):
+        z1 = lax.ppermute(pair, "group", along(1))
+        *state, token = first_part(query, own, [pair])
+    with jax.named_scope("weights"):
+        wide = widened([weight, *pieces], token)
         pieces = lax.ppermute(wide, ("dp", "tensor"), SLANT)
     with jax.named_scope("attention"):
-        z1 = gated(lax.ppermute(pair, "group", along(1)), wide)
+        z1 = gated(z1, wide)
         z2 = lax.ppermute(z1, "group", along(1))
-        *state, token = first_part(query, own, [pair, z1, swap(z1)])
+        z4 = lax.ppermute(z1[:1], "group", along(3))
+        *state, token = more_part(query, [z1, swap(z1)], state, 1024, True)
         z2 = gated(z2, token)
+        z4 = gated(z4, z2)
     with jax.named_scope("weights"):
-        columns = lax.all_gather(gated(pieces, z2), "group", axis=0, tiled=True)
+        columns = lax.all_gather(gated(pieces, z4), "group", axis=0, tiled=True)
     with jax.named_scope("attention"):
         z3 = lax.ppermute(z2, "group", along(1))
-        *state, token = more_part(query, [z2, swap(z2)], state)
+        *state, token = more_part(
+            query, [z2, z4, swap(z2), swap(z4)], kept(state), 1536, True
+        )
         z3 = gated(z3, token)
-        z4 = lax.ppermute(z3[:1], "group", along(1))
-        *state, token = more_part(query, [z3, swap(z3)], state)
-        z4 = gated(z4, token)
-        c0, c1, c2, c3 = last_part(place, query, [z4, swap(z4)], state)
+        c0, c1, c2, c3 = last_part(place, query, [z3, swap(z3)], kept(state))
 
     with jax.named_scope("exchange"):
         blocks = around("tensor", plain, c3, c2, c1)
@@ -374,7 +380,9 @@
         contexts = [mixed] + around(EVERY, ring, mixed, mixed, mixed)
 
     with jax.named_scope("project"):
-        o0, o1, o2, o3 = projected(place, contexts, columns)
+        o0, o1, o2, o3 = projected(
+            place, contexts, pltpu.with_memory_space_constraint(columns, pltpu.HBM)
+        )
         parts = [o0] + around(EVERY, ring, o3, o2, o1)
     with jax.named_scope("finish"):
         attended, normed = finished(place, parts, residual[0, 0], gain[None])

time: 130 us -> 124 us (0.954)
  waiting for transfers between devices: 43 us -> 32 us
  starting transfers between devices: 30.4 us -> 36.7 us
  local copies, waits for them, and re-layouts: 7.4 us -> 3.92 us
  Pallas kernels: 33.7 us -> 35.6 us
    ppermute x12, waiting for transfers between devices: 40.6 us -> 31.1 us  [around(): lax.ppermute(a, axes, way)]
    pallas_call x2, Pallas kernels: 8.23 us -> 14.4 us  [more_part(): pl.pallas_call(functools.partial(attend_more, len(blocks), width), in_spe...]
    ppermute x6, starting transfers between devices: 6.92 us -> 13 us  [the longest x1 5.65 us: shards(): z1 = lax.ppermute(pair, 'group', along(1))]
    pallas_call x1, Pallas kernels: 8.59 us -> 3.89 us  [first_part(): pl.pallas_call(functools.partial(attend_first, len(blocks)), in_specs=[VM...]
    unnamed x32 -> x14, local copies, waits for them, and re-layouts: 7.39 us -> 3.91 us
    pallas_call x1, Pallas kernels: 4.14 us -> 5.97 us  [last_part(): pl.pallas_call(functools.partial(attend_last, len(blocks)), in_specs=[SME...]
    ppermute x12, starting transfers between devices: 15.3 us -> 17 us  [around(): lax.ppermute(a, axes, way)]
    ppermute x1, starting transfers between devices: 3.4 us -> 1.82 us  [shards(): z2 = lax.ppermute(z1, 'group', along(1))]
  transfers between devices with their start and end apart: 23 -> 23, of which waited for: 16 -> 10; matrix products, arithmetic and copies ran while one was open for 0% -> 1% of each run, Pallas kernels for 17% -> 20%
where the time goes in v3:
time: 124 us; the launch traced here: 123 us
  starting transfers between devices  36.7 us (30%)
  Pallas kernels  35.6 us (29%)
  waiting for transfers between devices  32 us (26%)
  between operations  14.9 us (12%)
  local copies, waits for them, and re-layouts  3.92 us (3%)
    ppermute x12, waiting for transfers between devices, around(): lax.ppermute(a, axes, way)  31.1 us
    ppermute x12, starting transfers between devices, around(): lax.ppermute(a, axes, way)  17 us
    pallas_call x2, Pallas kernels, more_part(): pl.pallas_call(functools.partial(attend_more, len(blocks), width), in_spe...  14.4 us
    pallas_call x1, Pallas kernels, projected(): pl.pallas_call(project, grid=(5,), in_specs=[SMEM] + [whole(c) for c in c...  6.96 us
    pallas_call x1, Pallas kernels, last_part(): pl.pallas_call(functools.partial(attend_last, len(blocks)), in_specs=[SME...  5.97 us
    ppermute x1, starting transfers between devices, shards(): z1 = lax.ppermute(pair, 'group', along(1))  5.65 us
    unnamed x14, local copies, waits for them, and re-layouts  3.91 us
    pallas_call x1, Pallas kernels, first_part(): pl.pallas_call(functools.partial(attend_first, len(blocks)), in_specs=[VM...  3.89 us
  transfers between devices with their start and end apart: 23, of which 10 were waited for; matrix products, arithmetic and copies ran while one was open for 1% of the time, Pallas kernels for 20%

profile of v3, /device:TPU:1, one launch (start us, length us, event | category | flops | bytes accessed | tf_op | source)
XLA Modules:
  0.0 123.1 jit_solution(17494236567515932310)
XLA Ops:
  7.2 1.0 copy.14
  8.2 3.3 %collective-permute-start = (bf16[1,2,256,128]{3,2,1,0:T(8,128)(2,1)S(1)}, bf16[1,2,256,128]{3,2,1,0:T(8,128)(2,1)S(1)}, u32[]{:S(2)}, u32[]{:S(2)}) collective-permute-start(bf16[1,2,256,128]{3,2,1,0:T(8,128)(2,1)S(1)} %bitcast.34), channel_id=1, source_target_pairs={{0,4},{4,0},{8,12},{12,8},{16,20},{20,16},{24,28},{28,24},{32,36},... | collective-permute-start | bytes 393224 | tf_op jit(solution)/shard_map/prompt/ppermute | solution.py:348
  11.5 1.9 %collective-permute-start.3 = (bf16[80,640]{1,0:T(8,128)(2,1)}, bf16[80,640]{1,0:T(8,128)(2,1)S(1)}, u32[]{:S(2)}, u32[]{:S(2)}) collective-permute-start(bf16[80,640]{1,0:T(8,128)(2,1)} %bitcast.26), channel_id=1, source_target_pairs={{0,2},{1,3},{2,0},{3,1},{4,6},{5,7},{6,4},{7,5},{8,10},{9,11},{10,... | collective-permute-start | bytes 307208 | tf_op jit(solution)/shard_map/weights/ppermute | solution.py:327
  13.5 1.2 collective-permute-start.2
  14.6 1.0 copy.13
  15.7 5.7 %collective-permute-start.1 = (bf16[2,2,256,128]{3,2,1,0:T(8,128)(2,1)S(1)}, bf16[2,2,256,128]{3,2,1,0:T(8,128)(2,1)S(1)}, u32[]{:S(2)}, u32[]{:S(2)}) collective-permute-start(bf16[2,2,256,128]{3,2,1,0:T(8,128)(2,1)S(1)} %pad_maximum_fusion.refs_0_), channel_id=1, source_target_pairs={{0,8},{4,60},{8,16},{12,4},{16,24},{20,12},{24,32},{28,20},{32,40}... | collective-permute-start | bytes 786440 | tf_op jit(solution)/shard_map/attention/ppermute | solution.py:355
  21.3 3.9 %attention.8 = (f32[5,512,128]{2,1,0:T(8,128)S(1)}, f32[5,512,128]{2,1,0:T(8,128)S(1)}, f32[8,128]{1,0:T(8,128)S(1)}) custom-call(bf16[512,640]{1,0:T(8,128)(2,1)S(1)} %bitcast.30, bf16[2,512,128]{2,1,0:T(8,128)(2,1)S(1)} %bitcast.24, bf16[2,2,256,128]{3,2,1,0:T(8,128)(2,1)S(1)} %pad_maximum_fusion.refs_0_), custom_call_target="tpu_custom_call" | custom-call | flops 16106127360 | bytes 12582912 | tf_op jit(solution)/shard_map/attention/pallas_call | solution.py:139
  25.3 1.6 %collective-permute-start.6 = (bf16[2,2,256,128]{3,2,1,0:T(8,128)(2,1)S(1)}, bf16[2,2,256,128]{3,2,1,0:T(8,128)(2,1)S(1)}, u32[]{:S(2)}, u32[]{:S(2)}) collective-permute-start(bf16[2,2,256,128]{3,2,1,0:T(8,128)(2,1)S(1)} %attention.9.refs_0_), channel_id=1, source_target_pairs={{0,4},{4,0},{8,12},{12,8},{16,20},{20,16},{24,28},{28,24},{32,36},... | collective-permute-start | bytes 786440 | tf_op jit(solution)/shard_map/attention/ppermute | solution.py:364
  27.0 0.7 collective-permute-start.18
  27.7 1.8 %collective-permute-start.5 = (bf16[2,2,256,128]{3,2,1,0:T(8,128)(2,1)S(1)}, bf16[2,2,256,128]{3,2,1,0:T(8,128)(2,1)S(1)}, u32[]{:S(2)}, u32[]{:S(2)}) collective-permute-start(bf16[2,2,256,128]{3,2,1,0:T(8,128)(2,1)S(1)} %attention.9.refs_0_), channel_id=1, source_target_pairs={{0,8},{4,60},{8,16},{12,4},{16,24},{20,12},{24,32},{28,20},{32,40}... | collective-permute-start | bytes 786440 | tf_op jit(solution)/shard_map/attention/ppermute | solution.py:362
  29.5 2.8 %collective-permute-start.8 = (bf16[1,2,256,128]{3,2,1,0:T(8,128)(2,1)S(1)}, bf16[1,2,256,128]{3,2,1,0:T(8,128)(2,1)S(1)}, u32[]{:S(2)}, u32[]{:S(2)}) collective-permute-start(bf16[1,2,256,128]{3,2,1,0:T(8,128)(2,1)S(1)} %slice.4), channel_id=1, source_target_pairs={{0,24},{4,44},{8,32},{12,52},{16,40},{20,60},{24,48},{28,4},{32,56... | collective-permute-start | bytes 393224 | tf_op jit(solution)/shard_map/attention/ppermute | solution.py:363
  32.3 5.8 %attention.10 = (f32[5,512,128]{2,1,0:T(8,128)}, f32[5,512,128]{2,1,0:T(8,128)}, f32[8,128]{1,0:T(8,128)S(1)}) custom-call(bf16[512,640]{1,0:T(8,128)(2,1)S(1)} %bitcast.31, bf16[2,2,256,128]{3,2,1,0:T(8,128)(2,1)S(1)} %attention.9.refs_0_, bf16[2,2,256,128]{3,2,1,0:T(8,128)(2,1)S(1)} %collective-permute-done.6.refs_1_, ...), custom_call_target="tpu_custom_call" | custom-call | flops 8053063680 | bytes 12582912 | tf_op jit(solution)/shard_map/attention/pallas_call | solution.py:151
  38.2 0.8 weights.3
  39.0 0.7 collective-permute-start.9
  39.8 0.9 collective-permute-start.7
  41.0 8.6 %attention.13 = (f32[5,512,128]{2,1,0:T(8,128)}, f32[5,512,128]{2,1,0:T(8,128)}, f32[8,128]{1,0:T(8,128)S(1)}) custom-call(bf16[512,640]{1,0:T(8,128)(2,1)S(1)} %bitcast.32, bf16[2,2,256,128]{3,2,1,0:T(8,128)(2,1)S(1)} %attention.11.refs_0_, bf16[1,2,256,128]{3,2,1,0:T(8,128)(2,1)S(1)} %attention.12.refs_1_.refs_0_, ...), custom_call_target="tpu_custom_call" | custom-call | flops 8053063680 | bytes 12582912 | tf_op jit(solution)/shard_map/attention/pallas_call | solution.py:151
  49.6 2.1 %collective-permute-start.11 = (bf16[2,2,256,128]{3,2,1,0:T(8,128)(2,1)S(1)}, bf16[2,2,256,128]{3,2,1,0:T(8,128)(2,1)S(1)}, u32[]{:S(2)}, u32[]{:S(2)}) collective-permute-start(bf16[2,2,256,128]{3,2,1,0:T(8,128)(2,1)S(1)} %attention.14.refs_0_), channel_id=1, source_target_pairs={{0,4},{4,0},{8,12},{12,8},{16,20},{20,16},{24,28},{28,24},{32,36},... | collective-permute-start | bytes 786440 | tf_op jit(solution)/shard_map/attention/ppermute | solution.py:375
  52.9 6.0 %attention.15 = (bf16[128,640]{1,0:T(8,128)(2,1)S(1)}, bf16[128,640]{1,0:T(8,128)(2,1)S(1)}, bf16[128,640]{1,0:T(8,128)(2,1)S(1)}, bf16[128,640]{1,0:T(8,128)(2,1)S(1)}) custom-call(s32[4]{0:T(128)S(1)} %pad_add_fusion.place, bf16[512,640]{1,0:T(8,128)(2,1)S(1)} %bitcast.33, bf16[2,2,256,128]{3,2,1,0:T(8,128)(2,1)S(1)} %attention.14.refs_0_, ...), custom_call_target="tpu_custom_call" | custom-call | flops 8053063680 | bytes 12582912 | tf_op jit(solution)/shard_map/attention/pallas_call | solution.py:163
  58.9 4.7 %collective-permute-start.14 = (bf16[128,640]{1,0:T(8,128)(2,1)S(1)}, bf16[128,640]{1,0:T(8,128)(2,1)S(1)}, u32[]{:S(2)}, u32[]{:S(2)}) collective-permute-start(bf16[128,640]{1,0:T(8,128)(2,1)S(1)} %get-tuple-element.31.refs_1_), channel_id=1, source_target_pairs={{0,1},{1,2},{2,3},{3,0},{4,5},{5,6},{6,7},{7,4},{8,9},{9,10},{10,1... | collective-permute-start | bytes 491528 | tf_op jit(solution)/shard_map/exchange/ppermute | solution.py:327
  63.7 2.3 %collective-permute-start.12 = (bf16[128,640]{1,0:T(8,128)(2,1)S(1)}, bf16[128,640]{1,0:T(8,128)(2,1)S(1)}, u32[]{:S(2)}, u32[]{:S(2)}) collective-permute-start(bf16[128,640]{1,0:T(8,128)(2,1)S(1)} %get-tuple-element.33.refs_3_), channel_id=1, source_target_pairs={{0,3},{1,0},{2,1},{3,2},{4,7},{5,4},{6,5},{7,6},{8,11},{9,8},{10,9... | collective-permute-start | bytes 491528 | tf_op jit(solution)/shard_map/exchange/ppermute | solution.py:327
  66.0 0.8 collective-permute-done.14.refs_6_
  66.8 4.6 %collective-permute-done.13.refs_5_ = bf16[128,640]{1,0:T(8,128)(2,1)S(1)} collective-permute-done((bf16[128,640]{1,0:T(8,128)(2,1)S(1)}, bf16[128,640]{1,0:T(8,128)(2,1)S(1)}, u32[]{:S(2)}, u32[]{:S(2)}) %collective-permute-start.13) | collective-permute-done | bytes 163872 | tf_op jit(solution)/shard_map/exchange/ppermute | solution.py:327
  72.3 2.0 %collective-permute-start.16 = (bf16[4,128,640]{2,1,0:T(8,128)(2,1)S(1)}, bf16[4,128,640]{2,1,0:T(8,128)(2,1)S(1)}, u32[]{:S(2)}, u32[]{:S(2)}) collective-permute-start(bf16[4,128,640]{2,1,0:T(8,128)(2,1)S(1)} %exchange.1.c0), channel_id=1, source_target_pairs={{0,2},{1,3},{2,0},{3,1},{4,132},{5,133},{6,134},{7,135},{8,10},{9,... | collective-permute-start | bytes 1966088 | tf_op jit(solution)/shard_map/exchange/ppermute | solution.py:327
  74.3 1.6 %collective-permute-start.15 = (bf16[4,128,640]{2,1,0:T(8,128)(2,1)S(1)}, bf16[4,128,640]{2,1,0:T(8,128)(2,1)S(1)}, u32[]{:S(2)}, u32[]{:S(2)}) collective-permute-start(bf16[4,128,640]{2,1,0:T(8,128)(2,1)S(1)} %exchange.1.c0), channel_id=1, source_target_pairs={{0,3},{1,0},{2,1},{3,2},{4,196},{5,197},{6,198},{7,199},{8,11},{9,... | collective-permute-start | bytes 1966088 | tf_op jit(solution)/shard_map/exchange/ppermute | solution.py:327
  75.9 14.4 %collective-permute-done.17.c3 = bf16[4,128,640]{2,1,0:T(8,128)(2,1)S(1)} collective-permute-done((bf16[4,128,640]{2,1,0:T(8,128)(2,1)S(1)}, bf16[4,128,640]{2,1,0:T(8,128)(2,1)S(1)}, u32[]{:S(2)}, u32[]{:S(2)}) %collective-permute-start.17) | collective-permute-done | bytes 655392 | tf_op jit(solution)/shard_map/exchange/ppermute | solution.py:327
  90.9 0.8 copy-done.4
  91.7 1.1 copy-done.5
  92.8 7.0 %project.1 = (bf16[128,1280]{1,0:T(8,128)(2,1)S(1)}, bf16[128,1280]{1,0:T(8,128)(2,1)S(1)}, bf16[128,1280]{1,0:T(8,128)(2,1)S(1)}, bf16[128,1280]{1,0:T(8,128)(2,1)S(1)}) custom-call(s32[4]{0:T(128)S(1)} %pad_add_fusion.place, bf16[4,128,640]{2,1,0:T(8,128)(2,1)S(1)} %exchange.1.c0, bf16[4,128,640]{2,1,0:T(8,128)(2,1)S(1)} %copy-done.5, ...), custom_call_target="tpu_custom_call" | custom-call | flops 3355443200 | bytes 10485760 | tf_op jit(solution)/shard_map/project/pallas_call | solution.py:257
  99.8 2.4 %collective-permute-start.19 = (bf16[128,1280]{1,0:T(8,128)(2,1)S(1)}, bf16[128,1280]{1,0:T(8,128)(2,1)S(1)}, u32[]{:S(2)}, u32[]{:S(2)}) collective-permute-start(bf16[128,1280]{1,0:T(8,128)(2,1)S(1)} %get-tuple-element.35), channel_id=1, source_target_pairs={{0,3},{1,0},{2,1},{3,2},{4,196},{5,197},{6,198},{7,199},{8,11},{9,... | collective-permute-start | bytes 983048 | tf_op jit(solution)/shard_map/project/ppermute | solution.py:327
  102.9 6.9 %collective-permute-done.19.p1 = bf16[128,1280]{1,0:T(8,128)(2,1)S(1)} collective-permute-done((bf16[128,1280]{1,0:T(8,128)(2,1)S(1)}, bf16[128,1280]{1,0:T(8,128)(2,1)S(1)}, u32[]{:S(2)}, u32[]{:S(2)}) %collective-permute-start.19) | collective-permute-done | bytes 327712 | tf_op jit(solution)/shard_map/project/ppermute | solution.py:327
  110.0 3.5 %collective-permute-done.21.p3 = bf16[128,1280]{1,0:T(8,128)(2,1)S(1)} collective-permute-done((bf16[128,1280]{1,0:T(8,128)(2,1)S(1)}, bf16[128,1280]{1,0:T(8,128)(2,1)S(1)}, u32[]{:S(2)}, u32[]{:S(2)}) %collective-permute-start.21) | collective-permute-done | bytes 327712 | tf_op jit(solution)/shard_map/project/ppermute | solution.py:327
  113.5 2.8 %finish.1 = (bf16[128,5120]{1,0:T(8,128)(2,1)}, bf16[128,5120]{1,0:T(8,128)(2,1)}) custom-call(s32[4]{0:T(128)S(1)} %pad_add_fusion.place, bf16[128,1280]{1,0:T(8,128)(2,1)S(1)} %get-tuple-element.34.p0, bf16[128,1280]{1,0:T(8,128)(2,1)S(1)} %collective-permute-done.19.p1, bf16[128,1280]{1,0:T(8,128)(2,1)S(1)} %collective-permute-done.20.p2, ...), custom_call_target="tpu_custom_call" | custom-call | tf_op jit(solution)/shard_map/finish/pallas_call | solution.py:288
  (45 shorter events, 3.9 us)
Async XLA Ops:
  7.2 14.1 %copy-start.3 = (bf16[1,1,512,640]{3,2,1,0:T(8,128)(2,1)S(1)}, bf16[1,1,512,640]{3,2,1,0:T(8,128)(2,1)}, u32[]{:S(2)}) copy-start(bf16[1,1,512,640]{3,2,1,0:T(8,128)(2,1)} %param.7) | copy-start | bytes 1966084
  7.2 84.6 %all-gather.2.cloned.1.call-start = ((), (), s32[]{:S(2)}) async-start(), calls=%async_computation | async-start | bytes 6963200 | tf_op jit(solution)/shard_map/weights/all_gather | solution.py:368
  8.2 7.4 %collective-permute-start = (bf16[1,2,256,128]{3,2,1,0:T(8,128)(2,1)S(1)}, bf16[1,2,256,128]{3,2,1,0:T(8,128)(2,1)S(1)}, u32[]{:S(2)}, u32[]{:S(2)}) collective-permute-start(bf16[1,2,256,128]{3,2,1,0:T(8,128)(2,1)S(1)} %bitcast.34), channel_id=1, source_target_pairs={{0,4},{4,0},{8,12},{12,8},{16,20},{20,16},{24,28},{28,24},{32,36},... | collective-permute-start | bytes 393224 | tf_op jit(solution)/shard_map/prompt/ppermute | solution.py:348
  11.5 13.7 %collective-permute-start.4 = (bf16[80,640]{1,0:T(8,128)(2,1)}, bf16[80,640]{1,0:T(8,128)(2,1)S(1)}, u32[]{:S(2)}, u32[]{:S(2)}) collective-permute-start(bf16[80,640]{1,0:T(8,128)(2,1)} %bitcast.25), channel_id=1, source_target_pairs={{0,1},{1,2},{2,3},{3,0},{4,5},{5,6},{6,7},{7,4},{8,9},{9,10},{10,1... | collective-permute-start | bytes 307208 | tf_op jit(solution)/shard_map/weights/ppermute | solution.py:327
  11.5 13.7 %collective-permute-start.3 = (bf16[80,640]{1,0:T(8,128)(2,1)}, bf16[80,640]{1,0:T(8,128)(2,1)S(1)}, u32[]{:S(2)}, u32[]{:S(2)}) collective-permute-start(bf16[80,640]{1,0:T(8,128)(2,1)} %bitcast.26), channel_id=1, source_target_pairs={{0,2},{1,3},{2,0},{3,1},{4,6},{5,7},{6,4},{7,5},{8,10},{9,11},{10,... | collective-permute-start | bytes 307208 | tf_op jit(solution)/shard_map/weights/ppermute | solution.py:327
  13.5 11.8 %collective-permute-start.2 = (bf16[80,640]{1,0:T(8,128)(2,1)}, bf16[80,640]{1,0:T(8,128)(2,1)S(1)}, u32[]{:S(2)}, u32[]{:S(2)}) collective-permute-start(bf16[80,640]{1,0:T(8,128)(2,1)} %bitcast.27), channel_id=1, source_target_pairs={{0,3},{1,0},{2,1},{3,2},{4,7},{5,4},{6,5},{7,6},{8,11},{9,8},{10,9... | collective-permute-start | bytes 307208 | tf_op jit(solution)/shard_map/weights/ppermute | solution.py:327
  15.7 9.6 %collective-permute-start.1 = (bf16[2,2,256,128]{3,2,1,0:T(8,128)(2,1)S(1)}, bf16[2,2,256,128]{3,2,1,0:T(8,128)(2,1)S(1)}, u32[]{:S(2)}, u32[]{:S(2)}) collective-permute-start(bf16[2,2,256,128]{3,2,1,0:T(8,128)(2,1)S(1)} %pad_maximum_fusion.refs_0_), channel_id=1, source_target_pairs={{0,8},{4,60},{8,16},{12,4},{16,24},{20,12},{24,32},{28,20},{32,40}... | collective-permute-start | bytes 786440 | tf_op jit(solution)/shard_map/attention/ppermute | solution.py:355
  21.3 3.9 %copy-start.1 = (bf16[640,80]{0,1:T(8,128)(2,1)S(1)}, bf16[640,80]{0,1:T(8,128)(2,1)}, u32[]{:S(2)}) copy-start(bf16[640,80]{0,1:T(8,128)(2,1)} %param.11) | copy-start | bytes 307204
  25.3 7.0 %collective-permute-start.6 = (bf16[2,2,256,128]{3,2,1,0:T(8,128)(2,1)S(1)}, bf16[2,2,256,128]{3,2,1,0:T(8,128)(2,1)S(1)}, u32[]{:S(2)}, u32[]{:S(2)}) collective-permute-start(bf16[2,2,256,128]{3,2,1,0:T(8,128)(2,1)S(1)} %attention.9.refs_0_), channel_id=1, source_target_pairs={{0,4},{4,0},{8,12},{12,8},{16,20},{20,16},{24,28},{28,24},{32,36},... | collective-permute-start | bytes 786440 | tf_op jit(solution)/shard_map/attention/ppermute | solution.py:364
  27.0 11.2 %collective-permute-start.18 = (bf16[80,2560]{1,0:T(8,128)(2,1)S(1)}, bf16[80,2560]{1,0:T(8,128)(2,1)S(1)}, u32[]{:S(2)}, u32[]{:S(2)}) collective-permute-start(bf16[80,2560]{1,0:T(8,128)(2,1)S(1)} %weights.2.refs_0_), channel_id=1, source_target_pairs={{0,0},{1,193},{2,130},{3,67},{64,64},{65,1},{66,194},{67,131},{128... | collective-permute-start | bytes 1228808 | tf_op jit(solution)/shard_map/weights/ppermute | solution.py:359
  27.7 10.4 %collective-permute-start.5 = (bf16[2,2,256,128]{3,2,1,0:T(8,128)(2,1)S(1)}, bf16[2,2,256,128]{3,2,1,0:T(8,128)(2,1)S(1)}, u32[]{:S(2)}, u32[]{:S(2)}) collective-permute-start(bf16[2,2,256,128]{3,2,1,0:T(8,128)(2,1)S(1)} %attention.9.refs_0_), channel_id=1, source_target_pairs={{0,8},{4,60},{8,16},{12,4},{16,24},{20,12},{24,32},{28,20},{32,40}... | collective-permute-start | bytes 786440 | tf_op jit(solution)/shard_map/attention/ppermute | solution.py:362
  29.5 8.6 %collective-permute-start.8 = (bf16[1,2,256,128]{3,2,1,0:T(8,128)(2,1)S(1)}, bf16[1,2,256,128]{3,2,1,0:T(8,128)(2,1)S(1)}, u32[]{:S(2)}, u32[]{:S(2)}) collective-permute-start(bf16[1,2,256,128]{3,2,1,0:T(8,128)(2,1)S(1)} %slice.4), channel_id=1, source_target_pairs={{0,24},{4,44},{8,32},{12,52},{16,40},{20,60},{24,48},{28,4},{32,56... | collective-permute-start | bytes 393224 | tf_op jit(solution)/shard_map/attention/ppermute | solution.py:363
  39.0 2.0 %collective-permute-start.9 = (bf16[2,2,256,128]{3,2,1,0:T(8,128)(2,1)S(1)}, bf16[2,2,256,128]{3,2,1,0:T(8,128)(2,1)S(1)}, u32[]{:S(2)}, u32[]{:S(2)}) collective-permute-start(bf16[2,2,256,128]{3,2,1,0:T(8,128)(2,1)S(1)} %attention.11.refs_0_), channel_id=1, source_target_pairs={{0,4},{4,0},{8,12},{12,8},{16,20},{20,16},{24,28},{28,24},{32,36},... | collective-permute-start | bytes 786440 | tf_op jit(solution)/shard_map/attention/ppermute | solution.py:372
  39.7 1.3 %collective-permute-start.10 = (bf16[1,2,256,128]{3,2,1,0:T(8,128)(2,1)S(1)}, bf16[1,2,256,128]{3,2,1,0:T(8,128)(2,1)S(1)}, u32[]{:S(2)}, u32[]{:S(2)}) collective-permute-start(bf16[1,2,256,128]{3,2,1,0:T(8,128)(2,1)S(1)} %attention.12.refs_1_.refs_0_), channel_id=1, source_target_pairs={{0,4},{4,0},{8,12},{12,8},{16,20},{20,16},{24,28},{28,24},{32,36},... | collective-permute-start | bytes 393224 | tf_op jit(solution)/shard_map/attention/ppermute | solution.py:372
  39.8 9.9 %collective-permute-start.7 = (bf16[2,2,256,128]{3,2,1,0:T(8,128)(2,1)S(1)}, bf16[2,2,256,128]{3,2,1,0:T(8,128)(2,1)S(1)}, u32[]{:S(2)}, u32[]{:S(2)}) collective-permute-start(bf16[2,2,256,128]{3,2,1,0:T(8,128)(2,1)S(1)} %attention.11.refs_0_), channel_id=1, source_target_pairs={{0,8},{4,60},{8,16},{12,4},{16,24},{20,12},{24,32},{28,20},{32,40}... | collective-permute-start | bytes 786440 | tf_op jit(solution)/shard_map/attention/ppermute | solution.py:370
  49.6 3.2 %collective-permute-start.11 = (bf16[2,2,256,128]{3,2,1,0:T(8,128)(2,1)S(1)}, bf16[2,2,256,128]{3,2,1,0:T(8,128)(2,1)S(1)}, u32[]{:S(2)}, u32[]{:S(2)}) collective-permute-start(bf16[2,2,256,128]{3,2,1,0:T(8,128)(2,1)S(1)} %attention.14.refs_0_), channel_id=1, source_target_pairs={{0,4},{4,0},{8,12},{12,8},{16,20},{20,16},{24,28},{28,24},{32,36},... | collective-permute-start | bytes 786440 | tf_op jit(solution)/shard_map/attention/ppermute | solution.py:375
  58.9 7.9 %collective-permute-start.14 = (bf16[128,640]{1,0:T(8,128)(2,1)S(1)}, bf16[128,640]{1,0:T(8,128)(2,1)S(1)}, u32[]{:S(2)}, u32[]{:S(2)}) collective-permute-start(bf16[128,640]{1,0:T(8,128)(2,1)S(1)} %get-tuple-element.31.refs_1_), channel_id=1, source_target_pairs={{0,1},{1,2},{2,3},{3,0},{4,5},{5,6},{6,7},{7,4},{8,9},{9,10},{10,1... | collective-permute-start | bytes 491528 | tf_op jit(solution)/shard_map/exchange/ppermute | solution.py:327
  63.5 7.8 %collective-permute-start.13 = (bf16[128,640]{1,0:T(8,128)(2,1)S(1)}, bf16[128,640]{1,0:T(8,128)(2,1)S(1)}, u32[]{:S(2)}, u32[]{:S(2)}) collective-permute-start(bf16[128,640]{1,0:T(8,128)(2,1)S(1)} %get-tuple-element.32.refs_2_), channel_id=1, source_target_pairs={{0,2},{1,3},{2,0},{3,1},{4,6},{5,7},{6,4},{7,5},{8,10},{9,11},{10,... | collective-permute-start | bytes 491528 | tf_op jit(solution)/shard_map/exchange/ppermute | solution.py:327
  63.7 7.9 %collective-permute-start.12 = (bf16[128,640]{1,0:T(8,128)(2,1)S(1)}, bf16[128,640]{1,0:T(8,128)(2,1)S(1)}, u32[]{:S(2)}, u32[]{:S(2)}) collective-permute-start(bf16[128,640]{1,0:T(8,128)(2,1)S(1)} %get-tuple-element.33.refs_3_), channel_id=1, source_target_pairs={{0,3},{1,0},{2,1},{3,2},{4,7},{5,4},{6,5},{7,6},{8,11},{9,8},{10,9... | collective-permute-start | bytes 491528 | tf_op jit(solution)/shard_map/exchange/ppermute | solution.py:327
  72.2 41.2 %copy-start = (bf16[1,1,128,5120]{3,2,1,0:T(8,128)(2,1)S(1)}, bf16[1,1,128,5120]{3,2,1,0:T(8,128)(2,1)}, u32[]{:S(2)}) copy-start(bf16[1,1,128,5120]{3,2,1,0:T(8,128)(2,1)} %param.10) | copy-start | bytes 3932164
  72.2 41.2 %copy-start.2 = (f32[5120]{0:T(1024)S(1)}, f32[5120]{0:T(1024)}, u32[]{:S(2)}) copy-start(f32[5120]{0:T(1024)} %param.12) | copy-start | bytes 61444
  72.2 18.0 %collective-permute-start.17 = (bf16[4,128,640]{2,1,0:T(8,128)(2,1)S(1)}, bf16[4,128,640]{2,1,0:T(8,128)(2,1)S(1)}, u32[]{:S(2)}, u32[]{:S(2)}) collective-permute-start(bf16[4,128,640]{2,1,0:T(8,128)(2,1)S(1)} %exchange.1.c0), channel_id=1, source_target_pairs={{0,1},{1,2},{2,3},{3,0},{4,68},{5,69},{6,70},{7,71},{8,9},{9,10},{... | collective-permute-start | bytes 1966088 | tf_op jit(solution)/shard_map/exchange/ppermute | solution.py:327
  72.3 17.9 %collective-permute-start.16 = (bf16[4,128,640]{2,1,0:T(8,128)(2,1)S(1)}, bf16[4,128,640]{2,1,0:T(8,128)(2,1)S(1)}, u32[]{:S(2)}, u32[]{:S(2)}) collective-permute-start(bf16[4,128,640]{2,1,0:T(8,128)(2,1)S(1)} %exchange.1.c0), channel_id=1, source_target_pairs={{0,2},{1,3},{2,0},{3,1},{4,132},{5,133},{6,134},{7,135},{8,10},{9,... | collective-permute-start | bytes 1966088 | tf_op jit(solution)/shard_map/exchange/ppermute | solution.py:327
  74.3 16.6 %collective-permute-start.15 = (bf16[4,128,640]{2,1,0:T(8,128)(2,1)S(1)}, bf16[4,128,640]{2,1,0:T(8,128)(2,1)S(1)}, u32[]{:S(2)}, u32[]{:S(2)}) collective-permute-start(bf16[4,128,640]{2,1,0:T(8,128)(2,1)S(1)} %exchange.1.c0), channel_id=1, source_target_pairs={{0,3},{1,0},{2,1},{3,2},{4,196},{5,197},{6,198},{7,199},{8,11},{9,... | collective-permute-start | bytes 1966088 | tf_op jit(solution)/shard_map/exchange/ppermute | solution.py:327
  90.9 0.8 copy-start.4
  91.7 1.1 copy-start.5
  99.8 10.0 %collective-permute-start.19 = (bf16[128,1280]{1,0:T(8,128)(2,1)S(1)}, bf16[128,1280]{1,0:T(8,128)(2,1)S(1)}, u32[]{:S(2)}, u32[]{:S(2)}) collective-permute-start(bf16[128,1280]{1,0:T(8,128)(2,1)S(1)} %get-tuple-element.35), channel_id=1, source_target_pairs={{0,3},{1,0},{2,1},{3,2},{4,196},{5,197},{6,198},{7,199},{8,11},{9,... | collective-permute-start | bytes 983048 | tf_op jit(solution)/shard_map/project/ppermute | solution.py:327
  102.2 7.8 %collective-permute-start.20 = (bf16[128,1280]{1,0:T(8,128)(2,1)S(1)}, bf16[128,1280]{1,0:T(8,128)(2,1)S(1)}, u32[]{:S(2)}, u32[]{:S(2)}) collective-permute-start(bf16[128,1280]{1,0:T(8,128)(2,1)S(1)} %get-tuple-element.36), channel_id=1, source_target_pairs={{0,2},{1,3},{2,0},{3,1},{4,132},{5,133},{6,134},{7,135},{8,10},{9,... | collective-permute-start | bytes 983048 | tf_op jit(solution)/shard_map/project/ppermute | solution.py:327
  102.5 10.9 %collective-permute-start.21 = (bf16[128,1280]{1,0:T(8,128)(2,1)S(1)}, bf16[128,1280]{1,0:T(8,128)(2,1)S(1)}, u32[]{:S(2)}, u32[]{:S(2)}) collective-permute-start(bf16[128,1280]{1,0:T(8,128)(2,1)S(1)} %get-tuple-element.37), channel_id=1, source_target_pairs={{0,1},{1,2},{2,3},{3,0},{4,68},{5,69},{6,70},{7,71},{8,9},{9,10},{... | collective-permute-start | bytes 983048 | tf_op jit(solution)/shard_map/project/ppermute | solution.py:327
Sparse Core Ops, SparseCore 0:
  39.1 48.9 all-gather.1

commit v4 on v3

--- a/solution.py
+++ b/solution.py
@@ -283,7 +283,7 @@
 
 def finished(place, parts, residual, gain):
     block = jax.ShapeDtypeStruct((128, 5120), BF16)
-    lines = 32
+    lines = 64
     wide = pl.BlockSpec((lines, 5120), lambda n: (n, 0))
     return pl.pallas_call(
         finish,
@@ -333,8 +333,8 @@
     return [(i, (i + step) % 4) for i in range(4)]
 
 
-def kept(state):
-    return [pltpu.with_memory_space_constraint(a, pltpu.HBM) for a in state]
+def kept(arrays):
+    return [pltpu.with_memory_space_constraint(a, pltpu.HBM) for a in arrays]
 
 
 def shards(queries, comp_kv, prompt_kv, residual, out_weight, gain, lengths):
@@ -380,9 +380,7 @@
         contexts = [mixed] + around(EVERY, ring, mixed, mixed, mixed)
 
     with jax.named_scope("project"):
-        o0, o1, o2, o3 = projected(
-            place, contexts, pltpu.with_memory_space_constraint(columns, pltpu.HBM)
-        )
+        o0, o1, o2, o3 = projected(place, kept(contexts), *kept([columns]))
         parts = [o0] + around(EVERY, ring, o3, o2, o1)
     with jax.named_scope("finish"):
         attended, normed = finished(place, parts, residual[0, 0], gain[None])

time: 124 us -> 123 us (level)
  local copies, waits for them, and re-layouts: 3.92 us -> 2.33 us
    unnamed x14 -> x16, local copies, waits for them, and re-layouts: 3.91 us -> 2.31 us
  transfers between devices with their start and end apart: 23 -> 23, of which waited for: 10 -> 10; matrix products, arithmetic and copies ran while one was open for 1% -> 1% of each run, Pallas kernels for 20% -> 21%
where the time goes in v4:
time: 123 us; the launch traced here: 122 us
  starting transfers between devices  36.3 us (30%)
  Pallas kernels  35.9 us (29%)
  waiting for transfers between devices  32.1 us (26%)
  between operations  14.9 us (12%)
  local copies, waits for them, and re-layouts  2.33 us (2%)
    ppermute x12, waiting for transfers between devices, around(): lax.ppermute(a, axes, way)  31.2 us
    ppermute x12, starting transfers between devices, around(): lax.ppermute(a, axes, way)  16.6 us
    pallas_call x2, Pallas kernels, more_part(): pl.pallas_call(functools.partial(attend_more, len(blocks), width), in_spe...  14.4 us
    pallas_call x1, Pallas kernels, projected(): pl.pallas_call(project, grid=(5,), in_specs=[SMEM] + [whole(c) for c in c...  7.74 us
    pallas_call x1, Pallas kernels, last_part(): pl.pallas_call(functools.partial(attend_last, len(blocks)), in_specs=[SME...  5.97 us
    ppermute x1, starting transfers between devices, shards(): z1 = lax.ppermute(pair, 'group', along(1))  5.65 us
    pallas_call x1, Pallas kernels, first_part(): pl.pallas_call(functools.partial(attend_first, len(blocks)), in_specs=[VM...  3.89 us
    ppermute x1, starting transfers between devices, shards(): pair = jnp.concatenate([piece, swap(piece)], axis=0)  3.33 us
  transfers between devices with their start and end apart: 23, of which 10 were waited for; matrix products, arithmetic and copies ran while one was open for 1% of the time, Pallas kernels for 21%

profile of v4, /device:TPU:1, one launch (start us, length us, event | category | flops | bytes accessed | tf_op | source)
XLA Modules:
  0.0 121.6 jit_solution(5031105843229906469)
XLA Ops:
  7.2 1.0 copy.14
  8.2 3.3 %collective-permute-start = (bf16[1,2,256,128]{3,2,1,0:T(8,128)(2,1)S(1)}, bf16[1,2,256,128]{3,2,1,0:T(8,128)(2,1)S(1)}, u32[]{:S(2)}, u32[]{:S(2)}) collective-permute-start(bf16[1,2,256,128]{3,2,1,0:T(8,128)(2,1)S(1)} %bitcast.34), channel_id=1, source_target_pairs={{0,4},{4,0},{8,12},{12,8},{16,20},{20,16},{24,28},{28,24},{32,36},... | collective-permute-start | bytes 393224 | tf_op jit(solution)/shard_map/prompt/ppermute | solution.py:348
  11.5 1.9 %collective-permute-start.3 = (bf16[80,640]{1,0:T(8,128)(2,1)}, bf16[80,640]{1,0:T(8,128)(2,1)S(1)}, u32[]{:S(2)}, u32[]{:S(2)}) collective-permute-start(bf16[80,640]{1,0:T(8,128)(2,1)} %bitcast.26), channel_id=1, source_target_pairs={{0,2},{1,3},{2,0},{3,1},{4,6},{5,7},{6,4},{7,5},{8,10},{9,11},{10,... | collective-permute-start | bytes 307208 | tf_op jit(solution)/shard_map/weights/ppermute | solution.py:327
  13.5 1.2 collective-permute-start.2
  14.6 1.0 copy.13
  15.7 5.7 %collective-permute-start.1 = (bf16[2,2,256,128]{3,2,1,0:T(8,128)(2,1)S(1)}, bf16[2,2,256,128]{3,2,1,0:T(8,128)(2,1)S(1)}, u32[]{:S(2)}, u32[]{:S(2)}) collective-permute-start(bf16[2,2,256,128]{3,2,1,0:T(8,128)(2,1)S(1)} %pad_maximum_fusion.refs_0_), channel_id=1, source_target_pairs={{0,8},{4,60},{8,16},{12,4},{16,24},{20,12},{24,32},{28,20},{32,40}... | collective-permute-start | bytes 786440 | tf_op jit(solution)/shard_map/attention/ppermute | solution.py:355
  21.3 3.9 %attention.8 = (f32[5,512,128]{2,1,0:T(8,128)S(1)}, f32[5,512,128]{2,1,0:T(8,128)S(1)}, f32[8,128]{1,0:T(8,128)S(1)}) custom-call(bf16[512,640]{1,0:T(8,128)(2,1)S(1)} %bitcast.30, bf16[2,512,128]{2,1,0:T(8,128)(2,1)S(1)} %bitcast.24, bf16[2,2,256,128]{3,2,1,0:T(8,128)(2,1)S(1)} %pad_maximum_fusion.refs_0_), custom_call_target="tpu_custom_call" | custom-call | flops 16106127360 | bytes 12582912 | tf_op jit(solution)/shard_map/attention/pallas_call | solution.py:139
  25.3 1.6 %collective-permute-start.6 = (bf16[2,2,256,128]{3,2,1,0:T(8,128)(2,1)S(1)}, bf16[2,2,256,128]{3,2,1,0:T(8,128)(2,1)S(1)}, u32[]{:S(2)}, u32[]{:S(2)}) collective-permute-start(bf16[2,2,256,128]{3,2,1,0:T(8,128)(2,1)S(1)} %attention.9.refs_0_), channel_id=1, source_target_pairs={{0,4},{4,0},{8,12},{12,8},{16,20},{20,16},{24,28},{28,24},{32,36},... | collective-permute-start | bytes 786440 | tf_op jit(solution)/shard_map/attention/ppermute | solution.py:364
  27.0 0.7 collective-permute-start.18
  27.7 1.8 %collective-permute-start.5 = (bf16[2,2,256,128]{3,2,1,0:T(8,128)(2,1)S(1)}, bf16[2,2,256,128]{3,2,1,0:T(8,128)(2,1)S(1)}, u32[]{:S(2)}, u32[]{:S(2)}) collective-permute-start(bf16[2,2,256,128]{3,2,1,0:T(8,128)(2,1)S(1)} %attention.9.refs_0_), channel_id=1, source_target_pairs={{0,8},{4,60},{8,16},{12,4},{16,24},{20,12},{24,32},{28,20},{32,40}... | collective-permute-start | bytes 786440 | tf_op jit(solution)/shard_map/attention/ppermute | solution.py:362
  29.5 2.8 %collective-permute-start.8 = (bf16[1,2,256,128]{3,2,1,0:T(8,128)(2,1)S(1)}, bf16[1,2,256,128]{3,2,1,0:T(8,128)(2,1)S(1)}, u32[]{:S(2)}, u32[]{:S(2)}) collective-permute-start(bf16[1,2,256,128]{3,2,1,0:T(8,128)(2,1)S(1)} %slice.4), channel_id=1, source_target_pairs={{0,24},{4,44},{8,32},{12,52},{16,40},{20,60},{24,48},{28,4},{32,56... | collective-permute-start | bytes 393224 | tf_op jit(solution)/shard_map/attention/ppermute | solution.py:363
  32.3 5.8 %attention.10 = (f32[5,512,128]{2,1,0:T(8,128)}, f32[5,512,128]{2,1,0:T(8,128)}, f32[8,128]{1,0:T(8,128)S(1)}) custom-call(bf16[512,640]{1,0:T(8,128)(2,1)S(1)} %bitcast.31, bf16[2,2,256,128]{3,2,1,0:T(8,128)(2,1)S(1)} %attention.9.refs_0_, bf16[2,2,256,128]{3,2,1,0:T(8,128)(2,1)S(1)} %collective-permute-done.6.refs_1_, ...), custom_call_target="tpu_custom_call" | custom-call | flops 8053063680 | bytes 12582912 | tf_op jit(solution)/shard_map/attention/pallas_call | solution.py:151
  38.2 0.8 weights.3
  39.0 0.7 collective-permute-start.9
  39.8 0.9 collective-permute-start.7
  41.0 8.6 %attention.13 = (f32[5,512,128]{2,1,0:T(8,128)}, f32[5,512,128]{2,1,0:T(8,128)}, f32[8,128]{1,0:T(8,128)S(1)}) custom-call(bf16[512,640]{1,0:T(8,128)(2,1)S(1)} %bitcast.32, bf16[2,2,256,128]{3,2,1,0:T(8,128)(2,1)S(1)} %attention.11.refs_0_, bf16[1,2,256,128]{3,2,1,0:T(8,128)(2,1)S(1)} %attention.12.refs_1_.refs_0_, ...), custom_call_target="tpu_custom_call" | custom-call | flops 8053063680 | bytes 12582912 | tf_op jit(solution)/shard_map/attention/pallas_call | solution.py:151
  49.6 2.1 %collective-permute-start.11 = (bf16[2,2,256,128]{3,2,1,0:T(8,128)(2,1)S(1)}, bf16[2,2,256,128]{3,2,1,0:T(8,128)(2,1)S(1)}, u32[]{:S(2)}, u32[]{:S(2)}) collective-permute-start(bf16[2,2,256,128]{3,2,1,0:T(8,128)(2,1)S(1)} %attention.14.refs_0_), channel_id=1, source_target_pairs={{0,4},{4,0},{8,12},{12,8},{16,20},{20,16},{24,28},{28,24},{32,36},... | collective-permute-start | bytes 786440 | tf_op jit(solution)/shard_map/attention/ppermute | solution.py:375
  52.9 6.0 %attention.15 = (bf16[128,640]{1,0:T(8,128)(2,1)S(1)}, bf16[128,640]{1,0:T(8,128)(2,1)S(1)}, bf16[128,640]{1,0:T(8,128)(2,1)S(1)}, bf16[128,640]{1,0:T(8,128)(2,1)S(1)}) custom-call(s32[4]{0:T(128)S(1)} %pad_add_fusion.place, bf16[512,640]{1,0:T(8,128)(2,1)S(1)} %bitcast.33, bf16[2,2,256,128]{3,2,1,0:T(8,128)(2,1)S(1)} %attention.14.refs_0_, ...), custom_call_target="tpu_custom_call" | custom-call | flops 8053063680 | bytes 12582912 | tf_op jit(solution)/shard_map/attention/pallas_call | solution.py:163
  58.8 4.7 %collective-permute-start.14 = (bf16[128,640]{1,0:T(8,128)(2,1)S(1)}, bf16[128,640]{1,0:T(8,128)(2,1)S(1)}, u32[]{:S(2)}, u32[]{:S(2)}) collective-permute-start(bf16[128,640]{1,0:T(8,128)(2,1)S(1)} %get-tuple-element.31.refs_1_), channel_id=1, source_target_pairs={{0,1},{1,2},{2,3},{3,0},{4,5},{5,6},{6,7},{7,4},{8,9},{9,10},{10,1... | collective-permute-start | bytes 491528 | tf_op jit(solution)/shard_map/exchange/ppermute | solution.py:327
  63.7 2.3 %collective-permute-start.12 = (bf16[128,640]{1,0:T(8,128)(2,1)S(1)}, bf16[128,640]{1,0:T(8,128)(2,1)S(1)}, u32[]{:S(2)}, u32[]{:S(2)}) collective-permute-start(bf16[128,640]{1,0:T(8,128)(2,1)S(1)} %get-tuple-element.33.refs_3_), channel_id=1, source_target_pairs={{0,3},{1,0},{2,1},{3,2},{4,7},{5,4},{6,5},{7,6},{8,11},{9,8},{10,9... | collective-permute-start | bytes 491528 | tf_op jit(solution)/shard_map/exchange/ppermute | solution.py:327
  66.0 0.8 collective-permute-done.14.refs_6_
  66.8 4.6 %collective-permute-done.13.refs_5_ = bf16[128,640]{1,0:T(8,128)(2,1)S(1)} collective-permute-done((bf16[128,640]{1,0:T(8,128)(2,1)S(1)}, bf16[128,640]{1,0:T(8,128)(2,1)S(1)}, u32[]{:S(2)}, u32[]{:S(2)}) %collective-permute-start.13) | collective-permute-done | bytes 163872 | tf_op jit(solution)/shard_map/exchange/ppermute | solution.py:327
  71.6 0.6 exchange.1.c0
  72.3 2.0 %collective-permute-start.16 = (bf16[4,128,640]{2,1,0:T(8,128)(2,1)S(1)}, bf16[4,128,640]{2,1,0:T(8,128)(2,1)S(1)}, u32[]{:S(2)}, u32[]{:S(2)}) collective-permute-start(bf16[4,128,640]{2,1,0:T(8,128)(2,1)S(1)} %exchange.1.c0), channel_id=1, source_target_pairs={{0,2},{1,3},{2,0},{3,1},{4,132},{5,133},{6,134},{7,135},{8,10},{9,... | collective-permute-start | bytes 1966088 | tf_op jit(solution)/shard_map/exchange/ppermute | solution.py:327
  74.3 1.6 %collective-permute-start.15 = (bf16[4,128,640]{2,1,0:T(8,128)(2,1)S(1)}, bf16[4,128,640]{2,1,0:T(8,128)(2,1)}, u32[]{:S(2)}, u32[]{:S(2)}) collective-permute-start(bf16[4,128,640]{2,1,0:T(8,128)(2,1)S(1)} %exchange.1.c0), channel_id=1, source_target_pairs={{0,3},{1,0},{2,1},{3,2},{4,196},{5,197},{6,198},{7,199},{8,11},{9,... | collective-permute-start | bytes 1966088 | tf_op jit(solution)/shard_map/exchange/ppermute | solution.py:327
  75.9 14.4 %collective-permute-done.17.c3 = bf16[4,128,640]{2,1,0:T(8,128)(2,1)S(1)} collective-permute-done((bf16[4,128,640]{2,1,0:T(8,128)(2,1)S(1)}, bf16[4,128,640]{2,1,0:T(8,128)(2,1)S(1)}, u32[]{:S(2)}, u32[]{:S(2)}) %collective-permute-start.17) | collective-permute-done | bytes 655392 | tf_op jit(solution)/shard_map/exchange/ppermute | solution.py:327
  90.3 0.7 collective-permute-done.15.c1
  91.3 7.7 %project.1 = (bf16[128,1280]{1,0:T(8,128)(2,1)S(1)}, bf16[128,1280]{1,0:T(8,128)(2,1)S(1)}, bf16[128,1280]{1,0:T(8,128)(2,1)S(1)}, bf16[128,1280]{1,0:T(8,128)(2,1)S(1)}) custom-call(s32[4]{0:T(128)S(1)} %pad_add_fusion.place, bf16[4,128,640]{2,1,0:T(8,128)(2,1)} %copy-done.1, bf16[4,128,640]{2,1,0:T(8,128)(2,1)} %collective-permute-done.15.c1, ...), custom_call_target="tpu_custom_call" | custom-call | flops 3355443200 | bytes 10485760 | tf_op jit(solution)/shard_map/project/pallas_call | solution.py:257
  99.1 2.0 %collective-permute-start.19 = (bf16[128,1280]{1,0:T(8,128)(2,1)S(1)}, bf16[128,1280]{1,0:T(8,128)(2,1)S(1)}, u32[]{:S(2)}, u32[]{:S(2)}) collective-permute-start(bf16[128,1280]{1,0:T(8,128)(2,1)S(1)} %get-tuple-element.35), channel_id=1, source_target_pairs={{0,3},{1,0},{2,1},{3,2},{4,196},{5,197},{6,198},{7,199},{8,11},{9,... | collective-permute-start | bytes 983048 | tf_op jit(solution)/shard_map/project/ppermute | solution.py:327
  101.8 6.9 %collective-permute-done.19.p1 = bf16[128,1280]{1,0:T(8,128)(2,1)S(1)} collective-permute-done((bf16[128,1280]{1,0:T(8,128)(2,1)S(1)}, bf16[128,1280]{1,0:T(8,128)(2,1)S(1)}, u32[]{:S(2)}, u32[]{:S(2)}) %collective-permute-start.19) | collective-permute-done | bytes 327712 | tf_op jit(solution)/shard_map/project/ppermute | solution.py:327
  108.9 3.5 %collective-permute-done.21.p3 = bf16[128,1280]{1,0:T(8,128)(2,1)S(1)} collective-permute-done((bf16[128,1280]{1,0:T(8,128)(2,1)S(1)}, bf16[128,1280]{1,0:T(8,128)(2,1)S(1)}, u32[]{:S(2)}, u32[]{:S(2)}) %collective-permute-start.21) | collective-permute-done | bytes 327712 | tf_op jit(solution)/shard_map/project/ppermute | solution.py:327
  112.3 2.4 %finish.1 = (bf16[128,5120]{1,0:T(8,128)(2,1)}, bf16[128,5120]{1,0:T(8,128)(2,1)}) custom-call(s32[4]{0:T(128)S(1)} %pad_add_fusion.place, bf16[128,1280]{1,0:T(8,128)(2,1)S(1)} %get-tuple-element.34.p0, bf16[128,1280]{1,0:T(8,128)(2,1)S(1)} %collective-permute-done.19.p1, bf16[128,1280]{1,0:T(8,128)(2,1)S(1)} %collective-permute-done.20.p2, ...), custom_call_target="tpu_custom_call" | custom-call | tf_op jit(solution)/shard_map/finish/pallas_call | solution.py:288
  (47 shorter events, 2.9 us)
Async XLA Ops:
  7.2 14.1 %copy-start.4 = (bf16[1,1,512,640]{3,2,1,0:T(8,128)(2,1)S(1)}, bf16[1,1,512,640]{3,2,1,0:T(8,128)(2,1)}, u32[]{:S(2)}) copy-start(bf16[1,1,512,640]{3,2,1,0:T(8,128)(2,1)} %param.7) | copy-start | bytes 1966084
  7.2 83.8 %all-gather.2.cloned.1.call-start = ((), (), s32[]{:S(2)}) async-start(), calls=%async_computation | async-start | bytes 6963200 | tf_op jit(solution)/shard_map/weights/all_gather | solution.py:368
  8.2 7.4 %collective-permute-start = (bf16[1,2,256,128]{3,2,1,0:T(8,128)(2,1)S(1)}, bf16[1,2,256,128]{3,2,1,0:T(8,128)(2,1)S(1)}, u32[]{:S(2)}, u32[]{:S(2)}) collective-permute-start(bf16[1,2,256,128]{3,2,1,0:T(8,128)(2,1)S(1)} %bitcast.34), channel_id=1, source_target_pairs={{0,4},{4,0},{8,12},{12,8},{16,20},{20,16},{24,28},{28,24},{32,36},... | collective-permute-start | bytes 393224 | tf_op jit(solution)/shard_map/prompt/ppermute | solution.py:348
  11.5 13.7 %collective-permute-start.4 = (bf16[80,640]{1,0:T(8,128)(2,1)}, bf16[80,640]{1,0:T(8,128)(2,1)S(1)}, u32[]{:S(2)}, u32[]{:S(2)}) collective-permute-start(bf16[80,640]{1,0:T(8,128)(2,1)} %bitcast.25), channel_id=1, source_target_pairs={{0,1},{1,2},{2,3},{3,0},{4,5},{5,6},{6,7},{7,4},{8,9},{9,10},{10,1... | collective-permute-start | bytes 307208 | tf_op jit(solution)/shard_map/weights/ppermute | solution.py:327
  11.5 13.7 %collective-permute-start.3 = (bf16[80,640]{1,0:T(8,128)(2,1)}, bf16[80,640]{1,0:T(8,128)(2,1)S(1)}, u32[]{:S(2)}, u32[]{:S(2)}) collective-permute-start(bf16[80,640]{1,0:T(8,128)(2,1)} %bitcast.26), channel_id=1, source_target_pairs={{0,2},{1,3},{2,0},{3,1},{4,6},{5,7},{6,4},{7,5},{8,10},{9,11},{10,... | collective-permute-start | bytes 307208 | tf_op jit(solution)/shard_map/weights/ppermute | solution.py:327
  13.5 11.8 %collective-permute-start.2 = (bf16[80,640]{1,0:T(8,128)(2,1)}, bf16[80,640]{1,0:T(8,128)(2,1)S(1)}, u32[]{:S(2)}, u32[]{:S(2)}) collective-permute-start(bf16[80,640]{1,0:T(8,128)(2,1)} %bitcast.27), channel_id=1, source_target_pairs={{0,3},{1,0},{2,1},{3,2},{4,7},{5,4},{6,5},{7,6},{8,11},{9,8},{10,9... | collective-permute-start | bytes 307208 | tf_op jit(solution)/shard_map/weights/ppermute | solution.py:327
  15.7 9.6 %collective-permute-start.1 = (bf16[2,2,256,128]{3,2,1,0:T(8,128)(2,1)S(1)}, bf16[2,2,256,128]{3,2,1,0:T(8,128)(2,1)S(1)}, u32[]{:S(2)}, u32[]{:S(2)}) collective-permute-start(bf16[2,2,256,128]{3,2,1,0:T(8,128)(2,1)S(1)} %pad_maximum_fusion.refs_0_), channel_id=1, source_target_pairs={{0,8},{4,60},{8,16},{12,4},{16,24},{20,12},{24,32},{28,20},{32,40}... | collective-permute-start | bytes 786440 | tf_op jit(solution)/shard_map/attention/ppermute | solution.py:355
  21.3 3.9 %copy-start.2 = (bf16[640,80]{0,1:T(8,128)(2,1)S(1)}, bf16[640,80]{0,1:T(8,128)(2,1)}, u32[]{:S(2)}) copy-start(bf16[640,80]{0,1:T(8,128)(2,1)} %param.11) | copy-start | bytes 307204
  25.3 7.0 %collective-permute-start.6 = (bf16[2,2,256,128]{3,2,1,0:T(8,128)(2,1)S(1)}, bf16[2,2,256,128]{3,2,1,0:T(8,128)(2,1)S(1)}, u32[]{:S(2)}, u32[]{:S(2)}) collective-permute-start(bf16[2,2,256,128]{3,2,1,0:T(8,128)(2,1)S(1)} %attention.9.refs_0_), channel_id=1, source_target_pairs={{0,4},{4,0},{8,12},{12,8},{16,20},{20,16},{24,28},{28,24},{32,36},... | collective-permute-start | bytes 786440 | tf_op jit(solution)/shard_map/attention/ppermute | solution.py:364
  27.0 11.2 %collective-permute-start.18 = (bf16[80,2560]{1,0:T(8,128)(2,1)S(1)}, bf16[80,2560]{1,0:T(8,128)(2,1)S(1)}, u32[]{:S(2)}, u32[]{:S(2)}) collective-permute-start(bf16[80,2560]{1,0:T(8,128)(2,1)S(1)} %weights.2.refs_0_), channel_id=1, source_target_pairs={{0,0},{1,193},{2,130},{3,67},{64,64},{65,1},{66,194},{67,131},{128... | collective-permute-start | bytes 1228808 | tf_op jit(solution)/shard_map/weights/ppermute | solution.py:359
  27.7 10.4 %collective-permute-start.5 = (bf16[2,2,256,128]{3,2,1,0:T(8,128)(2,1)S(1)}, bf16[2,2,256,128]{3,2,1,0:T(8,128)(2,1)S(1)}, u32[]{:S(2)}, u32[]{:S(2)}) collective-permute-start(bf16[2,2,256,128]{3,2,1,0:T(8,128)(2,1)S(1)} %attention.9.refs_0_), channel_id=1, source_target_pairs={{0,8},{4,60},{8,16},{12,4},{16,24},{20,12},{24,32},{28,20},{32,40}... | collective-permute-start | bytes 786440 | tf_op jit(solution)/shard_map/attention/ppermute | solution.py:362
  29.5 8.6 %collective-permute-start.8 = (bf16[1,2,256,128]{3,2,1,0:T(8,128)(2,1)S(1)}, bf16[1,2,256,128]{3,2,1,0:T(8,128)(2,1)S(1)}, u32[]{:S(2)}, u32[]{:S(2)}) collective-permute-start(bf16[1,2,256,128]{3,2,1,0:T(8,128)(2,1)S(1)} %slice.4), channel_id=1, source_target_pairs={{0,24},{4,44},{8,32},{12,52},{16,40},{20,60},{24,48},{28,4},{32,56... | collective-permute-start | bytes 393224 | tf_op jit(solution)/shard_map/attention/ppermute | solution.py:363
  39.0 2.0 %collective-permute-start.9 = (bf16[2,2,256,128]{3,2,1,0:T(8,128)(2,1)S(1)}, bf16[2,2,256,128]{3,2,1,0:T(8,128)(2,1)S(1)}, u32[]{:S(2)}, u32[]{:S(2)}) collective-permute-start(bf16[2,2,256,128]{3,2,1,0:T(8,128)(2,1)S(1)} %attention.11.refs_0_), channel_id=1, source_target_pairs={{0,4},{4,0},{8,12},{12,8},{16,20},{20,16},{24,28},{28,24},{32,36},... | collective-permute-start | bytes 786440 | tf_op jit(solution)/shard_map/attention/ppermute | solution.py:372
  39.7 1.3 %collective-permute-start.10 = (bf16[1,2,256,128]{3,2,1,0:T(8,128)(2,1)S(1)}, bf16[1,2,256,128]{3,2,1,0:T(8,128)(2,1)S(1)}, u32[]{:S(2)}, u32[]{:S(2)}) collective-permute-start(bf16[1,2,256,128]{3,2,1,0:T(8,128)(2,1)S(1)} %attention.12.refs_1_.refs_0_), channel_id=1, source_target_pairs={{0,4},{4,0},{8,12},{12,8},{16,20},{20,16},{24,28},{28,24},{32,36},... | collective-permute-start | bytes 393224 | tf_op jit(solution)/shard_map/attention/ppermute | solution.py:372
  39.8 9.9 %collective-permute-start.7 = (bf16[2,2,256,128]{3,2,1,0:T(8,128)(2,1)S(1)}, bf16[2,2,256,128]{3,2,1,0:T(8,128)(2,1)S(1)}, u32[]{:S(2)}, u32[]{:S(2)}) collective-permute-start(bf16[2,2,256,128]{3,2,1,0:T(8,128)(2,1)S(1)} %attention.11.refs_0_), channel_id=1, source_target_pairs={{0,8},{4,60},{8,16},{12,4},{16,24},{20,12},{24,32},{28,20},{32,40}... | collective-permute-start | bytes 786440 | tf_op jit(solution)/shard_map/attention/ppermute | solution.py:370
  49.6 3.2 %collective-permute-start.11 = (bf16[2,2,256,128]{3,2,1,0:T(8,128)(2,1)S(1)}, bf16[2,2,256,128]{3,2,1,0:T(8,128)(2,1)S(1)}, u32[]{:S(2)}, u32[]{:S(2)}) collective-permute-start(bf16[2,2,256,128]{3,2,1,0:T(8,128)(2,1)S(1)} %attention.14.refs_0_), channel_id=1, source_target_pairs={{0,4},{4,0},{8,12},{12,8},{16,20},{20,16},{24,28},{28,24},{32,36},... | collective-permute-start | bytes 786440 | tf_op jit(solution)/shard_map/attention/ppermute | solution.py:375
  58.8 7.9 %collective-permute-start.14 = (bf16[128,640]{1,0:T(8,128)(2,1)S(1)}, bf16[128,640]{1,0:T(8,128)(2,1)S(1)}, u32[]{:S(2)}, u32[]{:S(2)}) collective-permute-start(bf16[128,640]{1,0:T(8,128)(2,1)S(1)} %get-tuple-element.31.refs_1_), channel_id=1, source_target_pairs={{0,1},{1,2},{2,3},{3,0},{4,5},{5,6},{6,7},{7,4},{8,9},{9,10},{10,1... | collective-permute-start | bytes 491528 | tf_op jit(solution)/shard_map/exchange/ppermute | solution.py:327
  63.5 7.9 %collective-permute-start.13 = (bf16[128,640]{1,0:T(8,128)(2,1)S(1)}, bf16[128,640]{1,0:T(8,128)(2,1)S(1)}, u32[]{:S(2)}, u32[]{:S(2)}) collective-permute-start(bf16[128,640]{1,0:T(8,128)(2,1)S(1)} %get-tuple-element.32.refs_2_), channel_id=1, source_target_pairs={{0,2},{1,3},{2,0},{3,1},{4,6},{5,7},{6,4},{7,5},{8,10},{9,11},{10,... | collective-permute-start | bytes 491528 | tf_op jit(solution)/shard_map/exchange/ppermute | solution.py:327
  63.7 7.9 %collective-permute-start.12 = (bf16[128,640]{1,0:T(8,128)(2,1)S(1)}, bf16[128,640]{1,0:T(8,128)(2,1)S(1)}, u32[]{:S(2)}, u32[]{:S(2)}) collective-permute-start(bf16[128,640]{1,0:T(8,128)(2,1)S(1)} %get-tuple-element.33.refs_3_), channel_id=1, source_target_pairs={{0,3},{1,0},{2,1},{3,2},{4,7},{5,4},{6,5},{7,6},{8,11},{9,8},{10,9... | collective-permute-start | bytes 491528 | tf_op jit(solution)/shard_map/exchange/ppermute | solution.py:327
  72.2 18.8 %copy-start.1 = (bf16[4,128,640]{2,1,0:T(8,128)(2,1)}, bf16[4,128,640]{2,1,0:T(8,128)(2,1)S(1)}, u32[]{:S(2)}) copy-start(bf16[4,128,640]{2,1,0:T(8,128)(2,1)S(1)} %exchange.1.c0) | copy-start | bytes 1966084
  72.2 40.1 %copy-start = (bf16[1,1,128,5120]{3,2,1,0:T(8,128)(2,1)S(1)}, bf16[1,1,128,5120]{3,2,1,0:T(8,128)(2,1)}, u32[]{:S(2)}) copy-start(bf16[1,1,128,5120]{3,2,1,0:T(8,128)(2,1)} %param.10) | copy-start | bytes 3932164
  72.2 40.1 %copy-start.3 = (f32[5120]{0:T(1024)S(1)}, f32[5120]{0:T(1024)}, u32[]{:S(2)}) copy-start(f32[5120]{0:T(1024)} %param.12) | copy-start | bytes 61444
  72.2 18.0 %collective-permute-start.17 = (bf16[4,128,640]{2,1,0:T(8,128)(2,1)S(1)}, bf16[4,128,640]{2,1,0:T(8,128)(2,1)S(1)}, u32[]{:S(2)}, u32[]{:S(2)}) collective-permute-start(bf16[4,128,640]{2,1,0:T(8,128)(2,1)S(1)} %exchange.1.c0), channel_id=1, source_target_pairs={{0,1},{1,2},{2,3},{3,0},{4,68},{5,69},{6,70},{7,71},{8,9},{9,10},{... | collective-permute-start | bytes 1966088 | tf_op jit(solution)/shard_map/exchange/ppermute | solution.py:327
  72.3 17.9 %collective-permute-start.16 = (bf16[4,128,640]{2,1,0:T(8,128)(2,1)S(1)}, bf16[4,128,640]{2,1,0:T(8,128)(2,1)S(1)}, u32[]{:S(2)}, u32[]{:S(2)}) collective-permute-start(bf16[4,128,640]{2,1,0:T(8,128)(2,1)S(1)} %exchange.1.c0), channel_id=1, source_target_pairs={{0,2},{1,3},{2,0},{3,1},{4,132},{5,133},{6,134},{7,135},{8,10},{9,... | collective-permute-start | bytes 1966088 | tf_op jit(solution)/shard_map/exchange/ppermute | solution.py:327
  74.3 16.7 %collective-permute-start.15 = (bf16[4,128,640]{2,1,0:T(8,128)(2,1)S(1)}, bf16[4,128,640]{2,1,0:T(8,128)(2,1)}, u32[]{:S(2)}, u32[]{:S(2)}) collective-permute-start(bf16[4,128,640]{2,1,0:T(8,128)(2,1)S(1)} %exchange.1.c0), channel_id=1, source_target_pairs={{0,3},{1,0},{2,1},{3,2},{4,196},{5,197},{6,198},{7,199},{8,11},{9,... | collective-permute-start | bytes 1966088 | tf_op jit(solution)/shard_map/exchange/ppermute | solution.py:327
  90.3 0.9 copy-start.5
  90.3 1.0 copy-start.6
  99.1 9.5 %collective-permute-start.19 = (bf16[128,1280]{1,0:T(8,128)(2,1)S(1)}, bf16[128,1280]{1,0:T(8,128)(2,1)S(1)}, u32[]{:S(2)}, u32[]{:S(2)}) collective-permute-start(bf16[128,1280]{1,0:T(8,128)(2,1)S(1)} %get-tuple-element.35), channel_id=1, source_target_pairs={{0,3},{1,0},{2,1},{3,2},{4,196},{5,197},{6,198},{7,199},{8,11},{9,... | collective-permute-start | bytes 983048 | tf_op jit(solution)/shard_map/project/ppermute | solution.py:327
  101.1 7.8 %collective-permute-start.20 = (bf16[128,1280]{1,0:T(8,128)(2,1)S(1)}, bf16[128,1280]{1,0:T(8,128)(2,1)S(1)}, u32[]{:S(2)}, u32[]{:S(2)}) collective-permute-start(bf16[128,1280]{1,0:T(8,128)(2,1)S(1)} %get-tuple-element.36), channel_id=1, source_target_pairs={{0,2},{1,3},{2,0},{3,1},{4,132},{5,133},{6,134},{7,135},{8,10},{9,... | collective-permute-start | bytes 983048 | tf_op jit(solution)/shard_map/project/ppermute | solution.py:327
  101.5 10.8 %collective-permute-start.21 = (bf16[128,1280]{1,0:T(8,128)(2,1)S(1)}, bf16[128,1280]{1,0:T(8,128)(2,1)S(1)}, u32[]{:S(2)}, u32[]{:S(2)}) collective-permute-start(bf16[128,1280]{1,0:T(8,128)(2,1)S(1)} %get-tuple-element.37), channel_id=1, source_target_pairs={{0,1},{1,2},{2,3},{3,0},{4,68},{5,69},{6,70},{7,71},{8,9},{9,10},{... | collective-permute-start | bytes 983048 | tf_op jit(solution)/shard_map/project/ppermute | solution.py:327
Sparse Core Ops, SparseCore 0:
  39.1 48.9 all-gather.1

commit v5 on v4

--- a/solution.py
+++ b/solution.py
@@ -369,7 +369,7 @@
     with jax.named_scope("attention"):
         z3 = lax.ppermute(z2, "group", along(1))
         *state, token = more_part(
-            query, [z2, z4, swap(z2), swap(z4)], kept(state), 1536, True
+            query, [z2, z4, swap(z2), swap(z4)], kept(state), 768, True
         )
         z3 = gated(z3, token)
         c0, c1, c2, c3 = last_part(place, query, [z3, swap(z3)], kept(state))

time: 123 us -> 123 us (level)
  no operation moved by 1% of the time
where the time goes in v5:
time: 123 us; the launch traced here: 122 us
  Pallas kernels  36.3 us (30%)
  starting transfers between devices  35.6 us (29%)
  waiting for transfers between devices  32.5 us (26%)
  between operations  14.9 us (12%)
  local copies, waits for them, and re-layouts  2.33 us (2%)
    ppermute x12, waiting for transfers between devices, around(): lax.ppermute(a, axes, way)  31.5 us
    ppermute x12, starting transfers between devices, around(): lax.ppermute(a, axes, way)  16.1 us
    pallas_call x2, Pallas kernels, more_part(): pl.pallas_call(functools.partial(attend_more, len(blocks), width), in_spe...  14.8 us
    pallas_call x1, Pallas kernels, projected(): pl.pallas_call(project, grid=(5,), in_specs=[SMEM] + [whole(c) for c in c...  7.74 us
    pallas_call x1, Pallas kernels, last_part(): pl.pallas_call(functools.partial(attend_last, len(blocks)), in_specs=[SME...  5.97 us
    ppermute x1, starting transfers between devices, shards(): z1 = lax.ppermute(pair, 'group', along(1))  5.65 us
    pallas_call x1, Pallas kernels, first_part(): pl.pallas_call(functools.partial(attend_first, len(blocks)), in_specs=[VM...  3.89 us
    ppermute x1, starting transfers between devices, shards(): pair = jnp.concatenate([piece, swap(piece)], axis=0)  3.33 us
  transfers between devices with their start and end apart: 23, of which 10 were waited for; matrix products, arithmetic and copies ran while one was open for 1% of the time, Pallas kernels for 21%

profile of v5, /device:TPU:1, one launch (start us, length us, event | category | flops | bytes accessed | tf_op | source)
XLA Modules:
  0.0 121.8 jit_solution(16718496710271946210)
XLA Ops:
  7.2 1.0 copy.14
  8.2 3.3 %collective-permute-start = (bf16[1,2,256,128]{3,2,1,0:T(8,128)(2,1)S(1)}, bf16[1,2,256,128]{3,2,1,0:T(8,128)(2,1)S(1)}, u32[]{:S(2)}, u32[]{:S(2)}) collective-permute-start(bf16[1,2,256,128]{3,2,1,0:T(8,128)(2,1)S(1)} %bitcast.34), channel_id=1, source_target_pairs={{0,4},{4,0},{8,12},{12,8},{16,20},{20,16},{24,28},{28,24},{32,36},... | collective-permute-start | bytes 393224 | tf_op jit(solution)/shard_map/prompt/ppermute | solution.py:348
  11.5 1.9 %collective-permute-start.3 = (bf16[80,640]{1,0:T(8,128)(2,1)}, bf16[80,640]{1,0:T(8,128)(2,1)S(1)}, u32[]{:S(2)}, u32[]{:S(2)}) collective-permute-start(bf16[80,640]{1,0:T(8,128)(2,1)} %bitcast.26), channel_id=1, source_target_pairs={{0,2},{1,3},{2,0},{3,1},{4,6},{5,7},{6,4},{7,5},{8,10},{9,11},{10,... | collective-permute-start | bytes 307208 | tf_op jit(solution)/shard_map/weights/ppermute | solution.py:327
  13.5 1.2 collective-permute-start.2
  14.6 1.0 copy.13
  15.7 5.7 %collective-permute-start.1 = (bf16[2,2,256,128]{3,2,1,0:T(8,128)(2,1)S(1)}, bf16[2,2,256,128]{3,2,1,0:T(8,128)(2,1)S(1)}, u32[]{:S(2)}, u32[]{:S(2)}) collective-permute-start(bf16[2,2,256,128]{3,2,1,0:T(8,128)(2,1)S(1)} %pad_maximum_fusion.refs_0_), channel_id=1, source_target_pairs={{0,8},{4,60},{8,16},{12,4},{16,24},{20,12},{24,32},{28,20},{32,40}... | collective-permute-start | bytes 786440 | tf_op jit(solution)/shard_map/attention/ppermute | solution.py:355
  21.3 3.9 %attention.8 = (f32[5,512,128]{2,1,0:T(8,128)S(1)}, f32[5,512,128]{2,1,0:T(8,128)S(1)}, f32[8,128]{1,0:T(8,128)S(1)}) custom-call(bf16[512,640]{1,0:T(8,128)(2,1)S(1)} %bitcast.30, bf16[2,512,128]{2,1,0:T(8,128)(2,1)S(1)} %bitcast.24, bf16[2,2,256,128]{3,2,1,0:T(8,128)(2,1)S(1)} %pad_maximum_fusion.refs_0_), custom_call_target="tpu_custom_call" | custom-call | flops 16106127360 | bytes 12582912 | tf_op jit(solution)/shard_map/attention/pallas_call | solution.py:139
  25.3 1.6 %collective-permute-start.6 = (bf16[2,2,256,128]{3,2,1,0:T(8,128)(2,1)S(1)}, bf16[2,2,256,128]{3,2,1,0:T(8,128)(2,1)S(1)}, u32[]{:S(2)}, u32[]{:S(2)}) collective-permute-start(bf16[2,2,256,128]{3,2,1,0:T(8,128)(2,1)S(1)} %attention.9.refs_0_), channel_id=1, source_target_pairs={{0,4},{4,0},{8,12},{12,8},{16,20},{20,16},{24,28},{28,24},{32,36},... | collective-permute-start | bytes 786440 | tf_op jit(solution)/shard_map/attention/ppermute | solution.py:364
  27.0 0.7 collective-permute-start.18
  27.7 1.8 %collective-permute-start.5 = (bf16[2,2,256,128]{3,2,1,0:T(8,128)(2,1)S(1)}, bf16[2,2,256,128]{3,2,1,0:T(8,128)(2,1)S(1)}, u32[]{:S(2)}, u32[]{:S(2)}) collective-permute-start(bf16[2,2,256,128]{3,2,1,0:T(8,128)(2,1)S(1)} %attention.9.refs_0_), channel_id=1, source_target_pairs={{0,8},{4,60},{8,16},{12,4},{16,24},{20,12},{24,32},{28,20},{32,40}... | collective-permute-start | bytes 786440 | tf_op jit(solution)/shard_map/attention/ppermute | solution.py:362
  29.5 2.8 %collective-permute-start.8 = (bf16[1,2,256,128]{3,2,1,0:T(8,128)(2,1)S(1)}, bf16[1,2,256,128]{3,2,1,0:T(8,128)(2,1)S(1)}, u32[]{:S(2)}, u32[]{:S(2)}) collective-permute-start(bf16[1,2,256,128]{3,2,1,0:T(8,128)(2,1)S(1)} %slice.4), channel_id=1, source_target_pairs={{0,24},{4,44},{8,32},{12,52},{16,40},{20,60},{24,48},{28,4},{32,56... | collective-permute-start | bytes 393224 | tf_op jit(solution)/shard_map/attention/ppermute | solution.py:363
  32.3 5.8 %attention.10 = (f32[5,512,128]{2,1,0:T(8,128)}, f32[5,512,128]{2,1,0:T(8,128)}, f32[8,128]{1,0:T(8,128)S(1)}) custom-call(bf16[512,640]{1,0:T(8,128)(2,1)S(1)} %bitcast.31, bf16[2,2,256,128]{3,2,1,0:T(8,128)(2,1)S(1)} %attention.9.refs_0_, bf16[2,2,256,128]{3,2,1,0:T(8,128)(2,1)S(1)} %collective-permute-done.6.refs_1_, ...), custom_call_target="tpu_custom_call" | custom-call | flops 8053063680 | bytes 12582912 | tf_op jit(solution)/shard_map/attention/pallas_call | solution.py:151
  38.2 0.8 weights.3
  39.0 0.7 collective-permute-start.9
  39.8 0.9 collective-permute-start.7
  41.0 9.1 %attention.13 = (f32[5,512,128]{2,1,0:T(8,128)}, f32[5,512,128]{2,1,0:T(8,128)}, f32[8,128]{1,0:T(8,128)S(1)}) custom-call(bf16[512,640]{1,0:T(8,128)(2,1)S(1)} %bitcast.32, bf16[2,2,256,128]{3,2,1,0:T(8,128)(2,1)S(1)} %attention.11.refs_0_, bf16[1,2,256,128]{3,2,1,0:T(8,128)(2,1)S(1)} %attention.12.refs_1_.refs_0_, ...), custom_call_target="tpu_custom_call" | custom-call | flops 8053063680 | bytes 12582912 | tf_op jit(solution)/shard_map/attention/pallas_call | solution.py:151
  50.1 1.9 %collective-permute-start.11 = (bf16[2,2,256,128]{3,2,1,0:T(8,128)(2,1)S(1)}, bf16[2,2,256,128]{3,2,1,0:T(8,128)(2,1)S(1)}, u32[]{:S(2)}, u32[]{:S(2)}) collective-permute-start(bf16[2,2,256,128]{3,2,1,0:T(8,128)(2,1)S(1)} %attention.14.refs_0_), channel_id=1, source_target_pairs={{0,4},{4,0},{8,12},{12,8},{16,20},{20,16},{24,28},{28,24},{32,36},... | collective-permute-start | bytes 786440 | tf_op jit(solution)/shard_map/attention/ppermute | solution.py:375
  52.7 0.7 collective-permute-done.11.refs_1_
  53.3 6.0 %attention.15 = (bf16[128,640]{1,0:T(8,128)(2,1)S(1)}, bf16[128,640]{1,0:T(8,128)(2,1)S(1)}, bf16[128,640]{1,0:T(8,128)(2,1)S(1)}, bf16[128,640]{1,0:T(8,128)(2,1)S(1)}) custom-call(s32[4]{0:T(128)S(1)} %pad_add_fusion.place, bf16[512,640]{1,0:T(8,128)(2,1)S(1)} %bitcast.33, bf16[2,2,256,128]{3,2,1,0:T(8,128)(2,1)S(1)} %attention.14.refs_0_, ...), custom_call_target="tpu_custom_call" | custom-call | flops 8053063680 | bytes 12582912 | tf_op jit(solution)/shard_map/attention/pallas_call | solution.py:163
  59.3 4.5 %collective-permute-start.14 = (bf16[128,640]{1,0:T(8,128)(2,1)S(1)}, bf16[128,640]{1,0:T(8,128)(2,1)S(1)}, u32[]{:S(2)}, u32[]{:S(2)}) collective-permute-start(bf16[128,640]{1,0:T(8,128)(2,1)S(1)} %get-tuple-element.31.refs_1_), channel_id=1, source_target_pairs={{0,1},{1,2},{2,3},{3,0},{4,5},{5,6},{6,7},{7,4},{8,9},{9,10},{10,1... | collective-permute-start | bytes 491528 | tf_op jit(solution)/shard_map/exchange/ppermute | solution.py:327
  64.2 2.4 %collective-permute-start.12 = (bf16[128,640]{1,0:T(8,128)(2,1)S(1)}, bf16[128,640]{1,0:T(8,128)(2,1)S(1)}, u32[]{:S(2)}, u32[]{:S(2)}) collective-permute-start(bf16[128,640]{1,0:T(8,128)(2,1)S(1)} %get-tuple-element.33.refs_3_), channel_id=1, source_target_pairs={{0,3},{1,0},{2,1},{3,2},{4,7},{5,4},{6,5},{7,6},{8,11},{9,8},{10,9... | collective-permute-start | bytes 491528 | tf_op jit(solution)/shard_map/exchange/ppermute | solution.py:327
  67.0 4.5 %collective-permute-done.13.refs_5_ = bf16[128,640]{1,0:T(8,128)(2,1)S(1)} collective-permute-done((bf16[128,640]{1,0:T(8,128)(2,1)S(1)}, bf16[128,640]{1,0:T(8,128)(2,1)S(1)}, u32[]{:S(2)}, u32[]{:S(2)}) %collective-permute-start.13) | collective-permute-done | bytes 163872 | tf_op jit(solution)/shard_map/exchange/ppermute | solution.py:327
  72.9 1.7 %collective-permute-start.16 = (bf16[4,128,640]{2,1,0:T(8,128)(2,1)S(1)}, bf16[4,128,640]{2,1,0:T(8,128)(2,1)S(1)}, u32[]{:S(2)}, u32[]{:S(2)}) collective-permute-start(bf16[4,128,640]{2,1,0:T(8,128)(2,1)S(1)} %exchange.1.c0), channel_id=1, source_target_pairs={{0,2},{1,3},{2,0},{3,1},{4,132},{5,133},{6,134},{7,135},{8,10},{9,... | collective-permute-start | bytes 1966088 | tf_op jit(solution)/shard_map/exchange/ppermute | solution.py:327
  74.6 1.3 %collective-permute-start.15 = (bf16[4,128,640]{2,1,0:T(8,128)(2,1)S(1)}, bf16[4,128,640]{2,1,0:T(8,128)(2,1)}, u32[]{:S(2)}, u32[]{:S(2)}) collective-permute-start(bf16[4,128,640]{2,1,0:T(8,128)(2,1)S(1)} %exchange.1.c0), channel_id=1, source_target_pairs={{0,3},{1,0},{2,1},{3,2},{4,196},{5,197},{6,198},{7,199},{8,11},{9,... | collective-permute-start | bytes 1966088 | tf_op jit(solution)/shard_map/exchange/ppermute | solution.py:327
  75.9 14.9 %collective-permute-done.17.c3 = bf16[4,128,640]{2,1,0:T(8,128)(2,1)S(1)} collective-permute-done((bf16[4,128,640]{2,1,0:T(8,128)(2,1)S(1)}, bf16[4,128,640]{2,1,0:T(8,128)(2,1)S(1)}, u32[]{:S(2)}, u32[]{:S(2)}) %collective-permute-start.17) | collective-permute-done | bytes 655392 | tf_op jit(solution)/shard_map/exchange/ppermute | solution.py:327
  90.8 0.7 collective-permute-done.15.c1
  91.9 7.7 %project.1 = (bf16[128,1280]{1,0:T(8,128)(2,1)S(1)}, bf16[128,1280]{1,0:T(8,128)(2,1)S(1)}, bf16[128,1280]{1,0:T(8,128)(2,1)S(1)}, bf16[128,1280]{1,0:T(8,128)(2,1)S(1)}) custom-call(s32[4]{0:T(128)S(1)} %pad_add_fusion.place, bf16[4,128,640]{2,1,0:T(8,128)(2,1)} %copy-done.1, bf16[4,128,640]{2,1,0:T(8,128)(2,1)} %collective-permute-done.15.c1, ...), custom_call_target="tpu_custom_call" | custom-call | flops 3355443200 | bytes 10485760 | tf_op jit(solution)/shard_map/project/pallas_call | solution.py:257
  99.6 2.0 %collective-permute-start.19 = (bf16[128,1280]{1,0:T(8,128)(2,1)S(1)}, bf16[128,1280]{1,0:T(8,128)(2,1)S(1)}, u32[]{:S(2)}, u32[]{:S(2)}) collective-permute-start(bf16[128,1280]{1,0:T(8,128)(2,1)S(1)} %get-tuple-element.35), channel_id=1, source_target_pairs={{0,3},{1,0},{2,1},{3,2},{4,196},{5,197},{6,198},{7,199},{8,11},{9,... | collective-permute-start | bytes 983048 | tf_op jit(solution)/shard_map/project/ppermute | solution.py:327
  101.6 0.7 collective-permute-start.21
  102.3 6.9 %collective-permute-done.19.p1 = bf16[128,1280]{1,0:T(8,128)(2,1)S(1)} collective-permute-done((bf16[128,1280]{1,0:T(8,128)(2,1)S(1)}, bf16[128,1280]{1,0:T(8,128)(2,1)S(1)}, u32[]{:S(2)}, u32[]{:S(2)}) %collective-permute-start.19) | collective-permute-done | bytes 327712 | tf_op jit(solution)/shard_map/project/ppermute | solution.py:327
  109.4 3.2 %collective-permute-done.21.p3 = bf16[128,1280]{1,0:T(8,128)(2,1)S(1)} collective-permute-done((bf16[128,1280]{1,0:T(8,128)(2,1)S(1)}, bf16[128,1280]{1,0:T(8,128)(2,1)S(1)}, u32[]{:S(2)}, u32[]{:S(2)}) %collective-permute-start.21) | collective-permute-done | bytes 327712 | tf_op jit(solution)/shard_map/project/ppermute | solution.py:327
  112.6 2.4 %finish.1 = (bf16[128,5120]{1,0:T(8,128)(2,1)}, bf16[128,5120]{1,0:T(8,128)(2,1)}) custom-call(s32[4]{0:T(128)S(1)} %pad_add_fusion.place, bf16[128,1280]{1,0:T(8,128)(2,1)S(1)} %get-tuple-element.34.p0, bf16[128,1280]{1,0:T(8,128)(2,1)S(1)} %collective-permute-done.19.p1, bf16[128,1280]{1,0:T(8,128)(2,1)S(1)} %collective-permute-done.20.p2, ...), custom_call_target="tpu_custom_call" | custom-call | tf_op jit(solution)/shard_map/finish/pallas_call | solution.py:288
  (47 shorter events, 3.5 us)
Async XLA Ops:
  7.2 14.1 %copy-start.4 = (bf16[1,1,512,640]{3,2,1,0:T(8,128)(2,1)S(1)}, bf16[1,1,512,640]{3,2,1,0:T(8,128)(2,1)}, u32[]{:S(2)}) copy-start(bf16[1,1,512,640]{3,2,1,0:T(8,128)(2,1)} %param.7) | copy-start | bytes 1966084
  7.2 84.4 %all-gather.2.cloned.1.call-start = ((), (), s32[]{:S(2)}) async-start(), calls=%async_computation | async-start | bytes 6963200 | tf_op jit(solution)/shard_map/weights/all_gather | solution.py:368
  8.2 7.4 %collective-permute-start = (bf16[1,2,256,128]{3,2,1,0:T(8,128)(2,1)S(1)}, bf16[1,2,256,128]{3,2,1,0:T(8,128)(2,1)S(1)}, u32[]{:S(2)}, u32[]{:S(2)}) collective-permute-start(bf16[1,2,256,128]{3,2,1,0:T(8,128)(2,1)S(1)} %bitcast.34), channel_id=1, source_target_pairs={{0,4},{4,0},{8,12},{12,8},{16,20},{20,16},{24,28},{28,24},{32,36},... | collective-permute-start | bytes 393224 | tf_op jit(solution)/shard_map/prompt/ppermute | solution.py:348
  11.5 13.7 %collective-permute-start.4 = (bf16[80,640]{1,0:T(8,128)(2,1)}, bf16[80,640]{1,0:T(8,128)(2,1)S(1)}, u32[]{:S(2)}, u32[]{:S(2)}) collective-permute-start(bf16[80,640]{1,0:T(8,128)(2,1)} %bitcast.25), channel_id=1, source_target_pairs={{0,1},{1,2},{2,3},{3,0},{4,5},{5,6},{6,7},{7,4},{8,9},{9,10},{10,1... | collective-permute-start | bytes 307208 | tf_op jit(solution)/shard_map/weights/ppermute | solution.py:327
  11.5 13.7 %collective-permute-start.3 = (bf16[80,640]{1,0:T(8,128)(2,1)}, bf16[80,640]{1,0:T(8,128)(2,1)S(1)}, u32[]{:S(2)}, u32[]{:S(2)}) collective-permute-start(bf16[80,640]{1,0:T(8,128)(2,1)} %bitcast.26), channel_id=1, source_target_pairs={{0,2},{1,3},{2,0},{3,1},{4,6},{5,7},{6,4},{7,5},{8,10},{9,11},{10,... | collective-permute-start | bytes 307208 | tf_op jit(solution)/shard_map/weights/ppermute | solution.py:327
  13.5 11.8 %collective-permute-start.2 = (bf16[80,640]{1,0:T(8,128)(2,1)}, bf16[80,640]{1,0:T(8,128)(2,1)S(1)}, u32[]{:S(2)}, u32[]{:S(2)}) collective-permute-start(bf16[80,640]{1,0:T(8,128)(2,1)} %bitcast.27), channel_id=1, source_target_pairs={{0,3},{1,0},{2,1},{3,2},{4,7},{5,4},{6,5},{7,6},{8,11},{9,8},{10,9... | collective-permute-start | bytes 307208 | tf_op jit(solution)/shard_map/weights/ppermute | solution.py:327
  15.7 9.6 %collective-permute-start.1 = (bf16[2,2,256,128]{3,2,1,0:T(8,128)(2,1)S(1)}, bf16[2,2,256,128]{3,2,1,0:T(8,128)(2,1)S(1)}, u32[]{:S(2)}, u32[]{:S(2)}) collective-permute-start(bf16[2,2,256,128]{3,2,1,0:T(8,128)(2,1)S(1)} %pad_maximum_fusion.refs_0_), channel_id=1, source_target_pairs={{0,8},{4,60},{8,16},{12,4},{16,24},{20,12},{24,32},{28,20},{32,40}... | collective-permute-start | bytes 786440 | tf_op jit(solution)/shard_map/attention/ppermute | solution.py:355
  21.3 3.9 %copy-start.2 = (bf16[640,80]{0,1:T(8,128)(2,1)S(1)}, bf16[640,80]{0,1:T(8,128)(2,1)}, u32[]{:S(2)}) copy-start(bf16[640,80]{0,1:T(8,128)(2,1)} %param.11) | copy-start | bytes 307204
  25.3 7.0 %collective-permute-start.6 = (bf16[2,2,256,128]{3,2,1,0:T(8,128)(2,1)S(1)}, bf16[2,2,256,128]{3,2,1,0:T(8,128)(2,1)S(1)}, u32[]{:S(2)}, u32[]{:S(2)}) collective-permute-start(bf16[2,2,256,128]{3,2,1,0:T(8,128)(2,1)S(1)} %attention.9.refs_0_), channel_id=1, source_target_pairs={{0,4},{4,0},{8,12},{12,8},{16,20},{20,16},{24,28},{28,24},{32,36},... | collective-permute-start | bytes 786440 | tf_op jit(solution)/shard_map/attention/ppermute | solution.py:364
  27.0 11.2 %collective-permute-start.18 = (bf16[80,2560]{1,0:T(8,128)(2,1)S(1)}, bf16[80,2560]{1,0:T(8,128)(2,1)S(1)}, u32[]{:S(2)}, u32[]{:S(2)}) collective-permute-start(bf16[80,2560]{1,0:T(8,128)(2,1)S(1)} %weights.2.refs_0_), channel_id=1, source_target_pairs={{0,0},{1,193},{2,130},{3,67},{64,64},{65,1},{66,194},{67,131},{128... | collective-permute-start | bytes 1228808 | tf_op jit(solution)/shard_map/weights/ppermute | solution.py:359
  27.7 10.4 %collective-permute-start.5 = (bf16[2,2,256,128]{3,2,1,0:T(8,128)(2,1)S(1)}, bf16[2,2,256,128]{3,2,1,0:T(8,128)(2,1)S(1)}, u32[]{:S(2)}, u32[]{:S(2)}) collective-permute-start(bf16[2,2,256,128]{3,2,1,0:T(8,128)(2,1)S(1)} %attention.9.refs_0_), channel_id=1, source_target_pairs={{0,8},{4,60},{8,16},{12,4},{16,24},{20,12},{24,32},{28,20},{32,40}... | collective-permute-start | bytes 786440 | tf_op jit(solution)/shard_map/attention/ppermute | solution.py:362
  29.5 8.6 %collective-permute-start.8 = (bf16[1,2,256,128]{3,2,1,0:T(8,128)(2,1)S(1)}, bf16[1,2,256,128]{3,2,1,0:T(8,128)(2,1)S(1)}, u32[]{:S(2)}, u32[]{:S(2)}) collective-permute-start(bf16[1,2,256,128]{3,2,1,0:T(8,128)(2,1)S(1)} %slice.4), channel_id=1, source_target_pairs={{0,24},{4,44},{8,32},{12,52},{16,40},{20,60},{24,48},{28,4},{32,56... | collective-permute-start | bytes 393224 | tf_op jit(solution)/shard_map/attention/ppermute | solution.py:363
  39.0 2.0 %collective-permute-start.9 = (bf16[2,2,256,128]{3,2,1,0:T(8,128)(2,1)S(1)}, bf16[2,2,256,128]{3,2,1,0:T(8,128)(2,1)S(1)}, u32[]{:S(2)}, u32[]{:S(2)}) collective-permute-start(bf16[2,2,256,128]{3,2,1,0:T(8,128)(2,1)S(1)} %attention.11.refs_0_), channel_id=1, source_target_pairs={{0,4},{4,0},{8,12},{12,8},{16,20},{20,16},{24,28},{28,24},{32,36},... | collective-permute-start | bytes 786440 | tf_op jit(solution)/shard_map/attention/ppermute | solution.py:372
  39.7 1.3 %collective-permute-start.10 = (bf16[1,2,256,128]{3,2,1,0:T(8,128)(2,1)S(1)}, bf16[1,2,256,128]{3,2,1,0:T(8,128)(2,1)S(1)}, u32[]{:S(2)}, u32[]{:S(2)}) collective-permute-start(bf16[1,2,256,128]{3,2,1,0:T(8,128)(2,1)S(1)} %attention.12.refs_1_.refs_0_), channel_id=1, source_target_pairs={{0,4},{4,0},{8,12},{12,8},{16,20},{20,16},{24,28},{28,24},{32,36},... | collective-permute-start | bytes 393224 | tf_op jit(solution)/shard_map/attention/ppermute | solution.py:372
  39.8 10.3 %collective-permute-start.7 = (bf16[2,2,256,128]{3,2,1,0:T(8,128)(2,1)S(1)}, bf16[2,2,256,128]{3,2,1,0:T(8,128)(2,1)S(1)}, u32[]{:S(2)}, u32[]{:S(2)}) collective-permute-start(bf16[2,2,256,128]{3,2,1,0:T(8,128)(2,1)S(1)} %attention.11.refs_0_), channel_id=1, source_target_pairs={{0,8},{4,60},{8,16},{12,4},{16,24},{20,12},{24,32},{28,20},{32,40}... | collective-permute-start | bytes 786440 | tf_op jit(solution)/shard_map/attention/ppermute | solution.py:370
  50.1 3.2 %collective-permute-start.11 = (bf16[2,2,256,128]{3,2,1,0:T(8,128)(2,1)S(1)}, bf16[2,2,256,128]{3,2,1,0:T(8,128)(2,1)S(1)}, u32[]{:S(2)}, u32[]{:S(2)}) collective-permute-start(bf16[2,2,256,128]{3,2,1,0:T(8,128)(2,1)S(1)} %attention.14.refs_0_), channel_id=1, source_target_pairs={{0,4},{4,0},{8,12},{12,8},{16,20},{20,16},{24,28},{28,24},{32,36},... | collective-permute-start | bytes 786440 | tf_op jit(solution)/shard_map/attention/ppermute | solution.py:375
  59.3 7.8 %collective-permute-start.14 = (bf16[128,640]{1,0:T(8,128)(2,1)S(1)}, bf16[128,640]{1,0:T(8,128)(2,1)S(1)}, u32[]{:S(2)}, u32[]{:S(2)}) collective-permute-start(bf16[128,640]{1,0:T(8,128)(2,1)S(1)} %get-tuple-element.31.refs_1_), channel_id=1, source_target_pairs={{0,1},{1,2},{2,3},{3,0},{4,5},{5,6},{6,7},{7,4},{8,9},{9,10},{10,1... | collective-permute-start | bytes 491528 | tf_op jit(solution)/shard_map/exchange/ppermute | solution.py:327
  63.8 7.8 %collective-permute-start.13 = (bf16[128,640]{1,0:T(8,128)(2,1)S(1)}, bf16[128,640]{1,0:T(8,128)(2,1)S(1)}, u32[]{:S(2)}, u32[]{:S(2)}) collective-permute-start(bf16[128,640]{1,0:T(8,128)(2,1)S(1)} %get-tuple-element.32.refs_2_), channel_id=1, source_target_pairs={{0,2},{1,3},{2,0},{3,1},{4,6},{5,7},{6,4},{7,5},{8,10},{9,11},{10,... | collective-permute-start | bytes 491528 | tf_op jit(solution)/shard_map/exchange/ppermute | solution.py:327
  64.2 7.9 %collective-permute-start.12 = (bf16[128,640]{1,0:T(8,128)(2,1)S(1)}, bf16[128,640]{1,0:T(8,128)(2,1)S(1)}, u32[]{:S(2)}, u32[]{:S(2)}) collective-permute-start(bf16[128,640]{1,0:T(8,128)(2,1)S(1)} %get-tuple-element.33.refs_3_), channel_id=1, source_target_pairs={{0,3},{1,0},{2,1},{3,2},{4,7},{5,4},{6,5},{7,6},{8,11},{9,8},{10,9... | collective-permute-start | bytes 491528 | tf_op jit(solution)/shard_map/exchange/ppermute | solution.py:327
  72.7 18.8 %copy-start.1 = (bf16[4,128,640]{2,1,0:T(8,128)(2,1)}, bf16[4,128,640]{2,1,0:T(8,128)(2,1)S(1)}, u32[]{:S(2)}) copy-start(bf16[4,128,640]{2,1,0:T(8,128)(2,1)S(1)} %exchange.1.c0) | copy-start | bytes 1966084
  72.7 39.8 %copy-start = (bf16[1,1,128,5120]{3,2,1,0:T(8,128)(2,1)S(1)}, bf16[1,1,128,5120]{3,2,1,0:T(8,128)(2,1)}, u32[]{:S(2)}) copy-start(bf16[1,1,128,5120]{3,2,1,0:T(8,128)(2,1)} %param.10) | copy-start | bytes 3932164
  72.8 39.8 %copy-start.3 = (f32[5120]{0:T(1024)S(1)}, f32[5120]{0:T(1024)}, u32[]{:S(2)}) copy-start(f32[5120]{0:T(1024)} %param.12) | copy-start | bytes 61444
  72.8 18.0 %collective-permute-start.17 = (bf16[4,128,640]{2,1,0:T(8,128)(2,1)S(1)}, bf16[4,128,640]{2,1,0:T(8,128)(2,1)S(1)}, u32[]{:S(2)}, u32[]{:S(2)}) collective-permute-start(bf16[4,128,640]{2,1,0:T(8,128)(2,1)S(1)} %exchange.1.c0), channel_id=1, source_target_pairs={{0,1},{1,2},{2,3},{3,0},{4,68},{5,69},{6,70},{7,71},{8,9},{9,10},{... | collective-permute-start | bytes 1966088 | tf_op jit(solution)/shard_map/exchange/ppermute | solution.py:327
  72.9 18.0 %collective-permute-start.16 = (bf16[4,128,640]{2,1,0:T(8,128)(2,1)S(1)}, bf16[4,128,640]{2,1,0:T(8,128)(2,1)S(1)}, u32[]{:S(2)}, u32[]{:S(2)}) collective-permute-start(bf16[4,128,640]{2,1,0:T(8,128)(2,1)S(1)} %exchange.1.c0), channel_id=1, source_target_pairs={{0,2},{1,3},{2,0},{3,1},{4,132},{5,133},{6,134},{7,135},{8,10},{9,... | collective-permute-start | bytes 1966088 | tf_op jit(solution)/shard_map/exchange/ppermute | solution.py:327
  74.6 17.0 %collective-permute-start.15 = (bf16[4,128,640]{2,1,0:T(8,128)(2,1)S(1)}, bf16[4,128,640]{2,1,0:T(8,128)(2,1)}, u32[]{:S(2)}, u32[]{:S(2)}) collective-permute-start(bf16[4,128,640]{2,1,0:T(8,128)(2,1)S(1)} %exchange.1.c0), channel_id=1, source_target_pairs={{0,3},{1,0},{2,1},{3,2},{4,196},{5,197},{6,198},{7,199},{8,11},{9,... | collective-permute-start | bytes 1966088 | tf_op jit(solution)/shard_map/exchange/ppermute | solution.py:327
  90.8 0.9 copy-start.5
  90.8 1.0 copy-start.6
  99.6 9.6 %collective-permute-start.19 = (bf16[128,1280]{1,0:T(8,128)(2,1)S(1)}, bf16[128,1280]{1,0:T(8,128)(2,1)S(1)}, u32[]{:S(2)}, u32[]{:S(2)}) collective-permute-start(bf16[128,1280]{1,0:T(8,128)(2,1)S(1)} %get-tuple-element.35), channel_id=1, source_target_pairs={{0,3},{1,0},{2,1},{3,2},{4,196},{5,197},{6,198},{7,199},{8,11},{9,... | collective-permute-start | bytes 983048 | tf_op jit(solution)/shard_map/project/ppermute | solution.py:327
  101.6 7.8 %collective-permute-start.20 = (bf16[128,1280]{1,0:T(8,128)(2,1)S(1)}, bf16[128,1280]{1,0:T(8,128)(2,1)S(1)}, u32[]{:S(2)}, u32[]{:S(2)}) collective-permute-start(bf16[128,1280]{1,0:T(8,128)(2,1)S(1)} %get-tuple-element.36), channel_id=1, source_target_pairs={{0,2},{1,3},{2,0},{3,1},{4,132},{5,133},{6,134},{7,135},{8,10},{9,... | collective-permute-start | bytes 983048 | tf_op jit(solution)/shard_map/project/ppermute | solution.py:327
  101.6 10.9 %collective-permute-start.21 = (bf16[128,1280]{1,0:T(8,128)(2,1)S(1)}, bf16[128,1280]{1,0:T(8,128)(2,1)S(1)}, u32[]{:S(2)}, u32[]{:S(2)}) collective-permute-start(bf16[128,1280]{1,0:T(8,128)(2,1)S(1)} %get-tuple-element.37), channel_id=1, source_target_pairs={{0,1},{1,2},{2,3},{3,0},{4,68},{5,69},{6,70},{7,71},{8,9},{9,10},{... | collective-permute-start | bytes 983048 | tf_op jit(solution)/shard_map/project/ppermute | solution.py:327
Sparse Core Ops, SparseCore 0:
  39.1 48.9 all-gather.1
